TPU v7x, 32 devices: a whole 2x2x4 slice. The times are simulated.
32 devices in a mesh: ctx: 8 (over z, y), head: 4 (over x, core).
Axes of the slice: x: 2, y: 2, z: 4, core: 2. Of those that a mesh axis runs over, the one named last changes fastest.
Arguments:
- query_self: bfloat16 [512, 8192], P('ctx', 'head'), may hold values from -60 to 60
- key_self: bfloat16 [512, 1024], P('ctx', 'head'), may hold values from -6 to 6
- value_self: bfloat16 [512, 1024], P('ctx', 'head'), may hold values from -6 to 6
- positions: int32 [512], P('ctx'), may hold values from 0 to 1533, as said below
- query_cross: bfloat16 [512, 8192], P('ctx', 'head'), may hold values from -60 to 60
- key_vision: bfloat16 [7168, 1024], P('ctx', 'head'), may hold values from -6 to 6
- value_vision: bfloat16 [7168, 1024], P('ctx', 'head'), may hold values from -6 to 6
- media_range: int32 [32, 2], P('ctx'), may hold values from 0 to 8, as said below
- gate_scale: float32 [1], replicated, may hold values from 0.3 to 1.5
Outputs:
- self_context: bfloat16 [512, 8192], P(('ctx', 'head'))
- cross_context: bfloat16 [512, 8192], P(('ctx', 'head'))
Inputs may be any that keep to these rules, and one draw needn't show every extreme that they name: `positions`: strictly increasing along the transcript, starting at 0; gaps of 1 to 3 up to the next-to-last token, and the last token's position is exactly 1533. `media_range`: column 0 never exceeds column 1; column 1 never falls from block to block, is 0 for the leading blocks (which see no frame) and 8 for the last block.
All inputs are finite; a program needn't handle non-finite values.
Results may differ from a plain program's by a relative error of at most 0.0091.
Values may be sent and summed in bfloat16 or wider, within the bound.
No kernel may reach another device: no remote copies, remote signals or barrier semaphores. Data moves between devices by JAX's collectives and lax.ppermute only.
A program may use at most 64 MiB of HBM per device.

v0:
```python
import jax
import jax.numpy as jnp
from jax import lax
from jax.sharding import PartitionSpec as P

HD = 128
TBLOCK = 16
FRAME_LEN = 896


rope_base = 500000.0
lowest = -1e30


def rotate(values, positions):
    half_width = values.shape[-1] // 2
    exponents = jnp.arange(half_width, dtype=jnp.float32) * (2.0 / values.shape[-1])
    frequency = jnp.power(rope_base, -exponents)
    angles = positions.astype(jnp.float32)[:, None] * frequency[None, :]
    cosine = jnp.cos(angles)[:, None, :]
    sine_part = jnp.sin(angles)[:, None, :]
    first_half = values[..., :half_width]
    second_half = values[..., half_width:]
    return jnp.concatenate(
        [
            first_half * cosine - second_half * sine_part,
            second_half * cosine + first_half * sine_part,
        ],
        axis=-1,
    )


def key_block(key_count):
    block_size = min(key_count, 1024)
    while key_count % block_size != 0:
        block_size = block_size - 1
    return block_size


def attend_block(state_in, queries, key_rows, value_rows, allowed):
    maxima, totals, accumulated = state_in
    scale_factor = queries.shape[-1] ** (-0.5)
    scores = (
        jnp.einsum("rkgd,nkd->kgrn", queries, key_rows, preferred_element_type=jnp.float32)
        * scale_factor
    )
    visible = allowed[None, None, :, :]
    scores = jnp.where(visible, scores, lowest)
    new_maxima = jnp.maximum(maxima, jnp.max(scores, axis=-1))
    weights = jnp.where(visible, jnp.exp(scores - new_maxima[..., None]), 0.0)
    factor = jnp.exp(maxima - new_maxima)
    totals = totals * factor + jnp.sum(weights, axis=-1)
    accumulated = accumulated * factor[..., None] + jnp.einsum(
        "kgrn,nkd->kgrd",
        weights.astype(jnp.bfloat16),
        value_rows,
        preferred_element_type=jnp.float32,
    )
    return (new_maxima, totals, accumulated)


def attend(state_in, queries, key_rows, value_rows, allowed):
    key_count = key_rows.shape[0]
    block_size = key_block(key_count)
    if block_size == key_count:
        return attend_block(state_in, queries, key_rows, value_rows, allowed)

    def step_block(block_index, state_now):
        row_begin = block_index * block_size
        key_part = lax.dynamic_slice_in_dim(key_rows, row_begin, block_size, 0)
        value_part = lax.dynamic_slice_in_dim(value_rows, row_begin, block_size, 0)
        allowed_part = lax.dynamic_slice_in_dim(allowed, row_begin, block_size, 1)
        return attend_block(state_now, queries, key_part, value_part, allowed_part)

    return lax.fori_loop(0, key_count // block_size, step_block, state_in)


def keep_state(current):
    return current


def empty_state(row_count, kv_heads, group_size, head_size):
    maxima = jnp.full((kv_heads, group_size, row_count), lowest, jnp.float32)
    totals = jnp.zeros((kv_heads, group_size, row_count), jnp.float32)
    accumulated = jnp.zeros((kv_heads, group_size, row_count, head_size), jnp.float32)
    return (maxima, totals, accumulated)


def finish(state_in):
    maxima, totals, accumulated = state_in
    safe_totals = jnp.where(totals > 0.0, totals, 1.0)
    result = accumulated / safe_totals[..., None]
    kv_heads, group_size, row_count, head_size = result.shape
    return jnp.transpose(result, (2, 0, 1, 3)).reshape(row_count, kv_heads * group_size * head_size)


def causal_group(current, group, key_rows, value_rows, key_index, offset):
    queries, row_index = group
    allowed = key_index[None, :] <= row_index[:, None]

    def causal_compute(state_in):
        return attend(state_in, queries, key_rows, value_rows, allowed)

    return lax.cond(offset <= jnp.max(row_index), causal_compute, keep_state, current)


def frame_mask(frame_index, lower_frame, upper_frame):
    return jnp.logical_and(
        frame_index[None, :] >= lower_frame[:, None], frame_index[None, :] < upper_frame[:, None]
    )


def on_device(
    query_self,
    key_self,
    value_self,
    positions,
    query_cross,
    key_vision,
    value_vision,
    media_range,
    gate_scale,
):
    head_size = HD
    kv_heads = key_self.shape[1] // head_size
    group_size = query_self.shape[1] // key_self.shape[1]
    row_count = query_self.shape[0]
    vision_count = key_vision.shape[0]
    device = lax.axis_index("ctx")
    own_rows = device * row_count + jnp.arange(row_count, dtype=jnp.int32)
    rotated_query = rotate(
        query_self.astype(jnp.float32).reshape(row_count, kv_heads * group_size, head_size),
        positions,
    )
    rotated_query = rotated_query.astype(jnp.bfloat16).reshape(
        row_count, kv_heads, group_size, head_size
    )
    rotated_key = rotate(
        key_self.astype(jnp.float32).reshape(row_count, kv_heads, head_size), positions
    ).astype(jnp.bfloat16)
    self_values = value_self.reshape(row_count, kv_heads, head_size)
    vision_keys = key_vision.reshape(vision_count, kv_heads, head_size)
    vision_values = value_vision.reshape(vision_count, kv_heads, head_size)
    cross_queries = query_cross.reshape(row_count, kv_heads, group_size, head_size)
    lower_frame = jnp.repeat(media_range[:, 0], TBLOCK)
    upper_frame = jnp.repeat(media_range[:, 1], TBLOCK)
    has_frames = upper_frame > lower_frame
    query_groups = ((rotated_query, own_rows),)
    self_start = tuple(
        (empty_state(group[1].shape[0], kv_heads, group_size, head_size) for group in query_groups)
    )
    cross_start = empty_state(row_count, kv_heads, group_size, head_size)
    offset = jnp.int32(0)
    key_rows = lax.all_gather(rotated_key, "ctx", axis=0, tiled=True)
    value_rows = lax.all_gather(self_values, "ctx", axis=0, tiled=True)
    key_index = jnp.arange(key_rows.shape[0], dtype=jnp.int32)
    updated = []
    for current, group in zip(self_start, query_groups):
        updated.append(causal_group(current, group, key_rows, value_rows, key_index, offset))
    self_states = tuple(updated)
    key_rows = lax.all_gather(vision_keys, "ctx", axis=0, tiled=True)
    value_rows = lax.all_gather(vision_values, "ctx", axis=0, tiled=True)
    frame_index = jnp.arange(key_rows.shape[0], dtype=jnp.int32) // FRAME_LEN
    allowed = frame_mask(frame_index, lower_frame, upper_frame)
    touching = jnp.logical_and(lower_frame <= frame_index[-1], upper_frame > frame_index[0])
    needed = jnp.any(jnp.logical_and(has_frames, touching))

    def fold_compute(state_in):
        return attend(state_in, cross_queries, key_rows, value_rows, allowed)

    cross_state = lax.cond(needed, fold_compute, keep_state, cross_start)
    self_rows = finish(self_states[0]).astype(jnp.bfloat16)
    cross_rows = jnp.where(
        has_frames[:, None], jnp.tanh(gate_scale[0]) * finish(cross_state), 0.0
    ).astype(jnp.bfloat16)
    self_context, cross_context = (
        lax.all_to_all(self_rows, "head", split_axis=0, concat_axis=1, tiled=True),
        lax.all_to_all(cross_rows, "head", split_axis=0, concat_axis=1, tiled=True),
    )
    return (self_context, cross_context)


def solution(mesh):
    placed = (
        P("ctx", "head"),
        P("ctx", "head"),
        P("ctx", "head"),
        P("ctx"),
        P("ctx", "head"),
        P("ctx", "head"),
        P("ctx", "head"),
        P("ctx", None),
        P(),
    )
    return jax.shard_map(
        on_device,
        mesh=mesh,
        in_specs=placed,
        out_specs=(P(("ctx", "head"), None), P(("ctx", "head"), None)),
        check_vma=False,
    )
```

profile of v0, /device:TPU:8, one launch (start us, length us, event | category | flops | bytes accessed | tf_op | source)
XLA Modules:
  0.0 256.2 jit_solution(7957452608823905118)
XLA Ops:
  7.2 2.0 copy.58
  9.3 2.0 copy.59
  11.3 0.7 convert_element_type.40
  12.0 1.0 convert_bitcast_fusion
  13.2 0.6 add_reduce_fusion
  14.5 0.2 multiply_cosine_fusion
  14.7 0.2 subtract_convert_fusion.1
  14.8 0.1 pad_maximum_fusion.1
  15.0 29.0 %all_gather.12 = bf16[512,2,128]{2,1,0:T(2,128)(2,1)S(1)} all-gather(bf16[64,2,128]{2,1,0:T(2,128)(2,1)S(1)} %pad_maximum_fusion.1), channel_id=1, replica_groups=mesh['ctx'=8,'head'=4] {'ctx'}, dimensions={0}, use_global_device_ids=true | all-gather | bytes 294912 | tf_op jit(solution)/shard_map/all_gather | solution.py:154
  43.9 31.7 %all_gather.13 = bf16[512,2,128]{2,1,0:T(2,128)(2,1)S(1)} all-gather(bf16[64,2,128]{2,1,0:T(2,128)(2,1)S(1)} %reshape.147), channel_id=1, replica_groups=mesh['ctx'=8,'head'=4] {'ctx'}, dimensions={0}, use_global_device_ids=true | all-gather | bytes 294912 | tf_op jit(solution)/shard_map/all_gather | solution.py:155
  75.6 0.2 fusion.41
  75.8 0.3 subtract_convert_fusion
  76.2 0.2 pad_maximum_fusion
  76.4 2.2 conditional.2
  76.5 0.5 fusion
  77.1 0.7 fusion.2
  77.8 0.8 convolution_add_fusion
  78.6 0.2 fusion.35
  78.8 0.2 copy.56
  79.0 0.8 convert_element_type.43
  79.8 3.4 %all-to-all-start = ((bf16[4,16,2048]{2,1,0:T(8,128)(2,1)}), bf16[4,16,2048]{2,1,0:T(8,128)(2,1)S(1)}, u32[]{:S(2)}, u32[]{:S(2)}) async-start(bf16[4,16,2048]{2,1,0:T(8,128)(2,1)} %convert_element_type.43), calls=%async_computation | async-start | bytes 524288 | tf_op jit(solution)/shard_map/all_to_all | solution.py:177
  83.3 0.6 fusion.42
  83.8 1.3 and_and_fusion
  85.1 0.7 broadcast_reduce_fusion
  87.2 64.5 %all-gather.5.cloned.1.call-done = bf16[7168,2,128]{0,2,1:T(8,128)(2,1)} async-done(((bf16[896,2,128]{0,2,1:T(8,128)(2,1)}), bf16[7168,2,128]{0,2,1:T(8,128)(2,1)}) %all-gather.5.cloned.1.call-update) | async-done | bytes 3670032 | tf_op jit(solution)/shard_map/all_gather | solution.py:162
  151.7 84.4 %conditional.3 = (f32[2,8,64]{2,1,0:T(8,128)}, f32[2,8,64,128]{3,2,1,0:T(8,128)}) conditional(s32[]{:T(128)} %convert_element_type.44, () %tuple.44, (s32[7168]{0:T(1024)S(1)}, s32[7168]{0:T(1024)S(1)}, s32[4]{0:T(128)S(1)}, s32[4]{0:T(128)S(1)}, bf16[64,2048]{1,0:T(8,128)(2,1)S(1)}, /*index=5*/bf16[7168,2,128]{0,2,1:T(8,128)(2,1)}, ...), branch_computations={%region_6.7_spmd, %region_7.12_spmd} | conditional | flops 552276992 | bytes 33679724 | solution.py:171
  152.2 0.4 compare_and_fusion
  152.6 83.5 %while.20 = (s32[]{:T(128)}, f32[2,8,64]{2,1,0:T(8,128)S(1)}, f32[2,8,64]{2,1,0:T(8,128)}, f32[2,8,64,128]{3,2,1,0:T(8,128)}, pred[64,7168]{1,0:T(8,128)(4,1)S(1...) while((s32[]{:T(128)}, f32[2,8,64]{2,1,0:T(8,128)S(1)}, ...), condition=%wide.region_11.11_spmd.clone, body=%wide.region_8.10_spmd.clone.sunk | while | flops 550900736 | bytes 32112852 | solution.py:75
  152.6 3.8 %fusion.55 = (f32[2,8,64]{2,1,0:T(8,128)S(1)}, f32[2,1024,64,8]{1,2,3,0:T(8,128)}) fusion(pred[64,1024]{1,0:T(8,128)(4,1)S(1)} %constant_dynamic-slice_fusion.2, bf16[64,2,8,128]{3,0,2,1:T(8,128)(2,1)S(1)} %get-tuple-element.455, bf16[7168,2,128]{0,2,1:T(8,128)(2,1)} %get-tuple-element.454, s32[]{:T(128)S(6)} %select_n.114), kind=kOutput, calls=%fused_computation.23.clone.1 | convolution fusion | flops 271580160 | bytes 5050372 | tf_op jit(solution)/shard_map/cond/branch_1_fun/while/body/eval_jaxpr/rkgd,nkd->kgrn/dot_general | solution.py:44
  156.4 3.6 %fusion.56 = f32[2,8,64]{2,1,0:T(8,128)S(1)} fusion(f32[2,1024,64,8]{1,2,3,0:T(8,128)} %get-tuple-element.422, f32[2,8,64]{2,1,0:T(8,128)S(1)} %select_maximum_fusion.2, pred[64,1024]{1,0:T(8,128)(4,1)S(1)} %constant_dynamic-slice_fusion.2), kind=kLoop, calls=%fused_computation.25.clone.1 | loop fusion | flops 5241856 | bytes 4268032 | tf_op jit(solution)/shard_map/cond/branch_1_fun/while/body/eval_jaxpr/reduce_sum | solution.py:52
  160.1 0.6 fusion.57
  160.7 3.2 %fusion.58 = f32[2,8,64,128]{3,2,1,0:T(8,128)} fusion(f32[2,1024,64,8]{1,2,3,0:T(8,128)S(1)} %copy-done, f32[2,8,64]{2,1,0:T(8,128)S(1)} %select_maximum_fusion.2, pred[64,1024]{1,0:T(8,128)(4,1)S(1)} %constant_dynamic-slice_fusion.2, f32[2,8,64,128]{3,2,1,0:T(8,128)} %get-tuple-element.440, bf16[7168,2,128]{0,2,1:T(8,128)(2,1)} %get-tuple-element.456, ...), kind=kOutput, calls=%fused_computation.28.clone.1 | convolution fusion | flops 274071552 | bytes 5840901 | tf_op jit(solution)/shard_map/cond/branch_1_fun/while/body/eval_jaxpr/kgrn,nkd->kgrd/dot_general | solution.py:53
  163.8 3.8 %fusion.55 = (f32[2,8,64]{2,1,0:T(8,128)S(1)}, f32[2,1024,64,8]{1,2,3,0:T(8,128)}) fusion(pred[64,1024]{1,0:T(8,128)(4,1)S(1)} %constant_dynamic-slice_fusion.2, bf16[64,2,8,128]{3,0,2,1:T(8,128)(2,1)S(1)} %get-tuple-element.455, bf16[7168,2,128]{0,2,1:T(8,128)(2,1)} %get-tuple-element.454, s32[]{:T(128)S(6)} %select_n.114), kind=kOutput, calls=%fused_computation.23.clone.1 | convolution fusion | flops 271580160 | bytes 5050372 | tf_op jit(solution)/shard_map/cond/branch_1_fun/while/body/eval_jaxpr/rkgd,nkd->kgrn/dot_general | solution.py:44
  167.6 3.6 %fusion.56 = f32[2,8,64]{2,1,0:T(8,128)S(1)} fusion(f32[2,1024,64,8]{1,2,3,0:T(8,128)} %get-tuple-element.422, f32[2,8,64]{2,1,0:T(8,128)S(1)} %select_maximum_fusion.2, pred[64,1024]{1,0:T(8,128)(4,1)S(1)} %constant_dynamic-slice_fusion.2), kind=kLoop, calls=%fused_computation.25.clone.1 | loop fusion | flops 5241856 | bytes 4268032 | tf_op jit(solution)/shard_map/cond/branch_1_fun/while/body/eval_jaxpr/reduce_sum | solution.py:52
  171.3 1.3 fusion.57
  172.6 3.3 %fusion.58 = f32[2,8,64,128]{3,2,1,0:T(8,128)} fusion(f32[2,1024,64,8]{1,2,3,0:T(8,128)S(1)} %copy-done, f32[2,8,64]{2,1,0:T(8,128)S(1)} %select_maximum_fusion.2, pred[64,1024]{1,0:T(8,128)(4,1)S(1)} %constant_dynamic-slice_fusion.2, f32[2,8,64,128]{3,2,1,0:T(8,128)} %get-tuple-element.440, bf16[7168,2,128]{0,2,1:T(8,128)(2,1)} %get-tuple-element.456, ...), kind=kOutput, calls=%fused_computation.28.clone.1 | convolution fusion | flops 274071552 | bytes 5840901 | tf_op jit(solution)/shard_map/cond/branch_1_fun/while/body/eval_jaxpr/kgrn,nkd->kgrd/dot_general | solution.py:53
  175.9 3.8 %fusion.55 = (f32[2,8,64]{2,1,0:T(8,128)S(1)}, f32[2,1024,64,8]{1,2,3,0:T(8,128)}) fusion(pred[64,1024]{1,0:T(8,128)(4,1)S(1)} %constant_dynamic-slice_fusion.2, bf16[64,2,8,128]{3,0,2,1:T(8,128)(2,1)S(1)} %get-tuple-element.455, bf16[7168,2,128]{0,2,1:T(8,128)(2,1)} %get-tuple-element.454, s32[]{:T(128)S(6)} %select_n.114), kind=kOutput, calls=%fused_computation.23.clone.1 | convolution fusion | flops 271580160 | bytes 5050372 | tf_op jit(solution)/shard_map/cond/branch_1_fun/while/body/eval_jaxpr/rkgd,nkd->kgrn/dot_general | solution.py:44
  179.7 3.6 %fusion.56 = f32[2,8,64]{2,1,0:T(8,128)S(1)} fusion(f32[2,1024,64,8]{1,2,3,0:T(8,128)} %get-tuple-element.422, f32[2,8,64]{2,1,0:T(8,128)S(1)} %select_maximum_fusion.2, pred[64,1024]{1,0:T(8,128)(4,1)S(1)} %constant_dynamic-slice_fusion.2), kind=kLoop, calls=%fused_computation.25.clone.1 | loop fusion | flops 5241856 | bytes 4268032 | tf_op jit(solution)/shard_map/cond/branch_1_fun/while/body/eval_jaxpr/reduce_sum | solution.py:52
  183.3 1.3 fusion.57
  184.6 3.3 %fusion.58 = f32[2,8,64,128]{3,2,1,0:T(8,128)} fusion(f32[2,1024,64,8]{1,2,3,0:T(8,128)S(1)} %copy-done, f32[2,8,64]{2,1,0:T(8,128)S(1)} %select_maximum_fusion.2, pred[64,1024]{1,0:T(8,128)(4,1)S(1)} %constant_dynamic-slice_fusion.2, f32[2,8,64,128]{3,2,1,0:T(8,128)} %get-tuple-element.440, bf16[7168,2,128]{0,2,1:T(8,128)(2,1)} %get-tuple-element.456, ...), kind=kOutput, calls=%fused_computation.28.clone.1 | convolution fusion | flops 274071552 | bytes 5840901 | tf_op jit(solution)/shard_map/cond/branch_1_fun/while/body/eval_jaxpr/kgrn,nkd->kgrd/dot_general | solution.py:53
  187.9 3.8 %fusion.55 = (f32[2,8,64]{2,1,0:T(8,128)S(1)}, f32[2,1024,64,8]{1,2,3,0:T(8,128)}) fusion(pred[64,1024]{1,0:T(8,128)(4,1)S(1)} %constant_dynamic-slice_fusion.2, bf16[64,2,8,128]{3,0,2,1:T(8,128)(2,1)S(1)} %get-tuple-element.455, bf16[7168,2,128]{0,2,1:T(8,128)(2,1)} %get-tuple-element.454, s32[]{:T(128)S(6)} %select_n.114), kind=kOutput, calls=%fused_computation.23.clone.1 | convolution fusion | flops 271580160 | bytes 5050372 | tf_op jit(solution)/shard_map/cond/branch_1_fun/while/body/eval_jaxpr/rkgd,nkd->kgrn/dot_general | solution.py:44
  191.7 3.6 %fusion.56 = f32[2,8,64]{2,1,0:T(8,128)S(1)} fusion(f32[2,1024,64,8]{1,2,3,0:T(8,128)} %get-tuple-element.422, f32[2,8,64]{2,1,0:T(8,128)S(1)} %select_maximum_fusion.2, pred[64,1024]{1,0:T(8,128)(4,1)S(1)} %constant_dynamic-slice_fusion.2), kind=kLoop, calls=%fused_computation.25.clone.1 | loop fusion | flops 5241856 | bytes 4268032 | tf_op jit(solution)/shard_map/cond/branch_1_fun/while/body/eval_jaxpr/reduce_sum | solution.py:52
  195.4 1.3 fusion.57
  196.7 3.3 %fusion.58 = f32[2,8,64,128]{3,2,1,0:T(8,128)} fusion(f32[2,1024,64,8]{1,2,3,0:T(8,128)S(1)} %copy-done, f32[2,8,64]{2,1,0:T(8,128)S(1)} %select_maximum_fusion.2, pred[64,1024]{1,0:T(8,128)(4,1)S(1)} %constant_dynamic-slice_fusion.2, f32[2,8,64,128]{3,2,1,0:T(8,128)} %get-tuple-element.440, bf16[7168,2,128]{0,2,1:T(8,128)(2,1)} %get-tuple-element.456, ...), kind=kOutput, calls=%fused_computation.28.clone.1 | convolution fusion | flops 274071552 | bytes 5840901 | tf_op jit(solution)/shard_map/cond/branch_1_fun/while/body/eval_jaxpr/kgrn,nkd->kgrd/dot_general | solution.py:53
  200.0 3.8 %fusion.55 = (f32[2,8,64]{2,1,0:T(8,128)S(1)}, f32[2,1024,64,8]{1,2,3,0:T(8,128)}) fusion(pred[64,1024]{1,0:T(8,128)(4,1)S(1)} %constant_dynamic-slice_fusion.2, bf16[64,2,8,128]{3,0,2,1:T(8,128)(2,1)S(1)} %get-tuple-element.455, bf16[7168,2,128]{0,2,1:T(8,128)(2,1)} %get-tuple-element.454, s32[]{:T(128)S(6)} %select_n.114), kind=kOutput, calls=%fused_computation.23.clone.1 | convolution fusion | flops 271580160 | bytes 5050372 | tf_op jit(solution)/shard_map/cond/branch_1_fun/while/body/eval_jaxpr/rkgd,nkd->kgrn/dot_general | solution.py:44
  203.8 3.6 %fusion.56 = f32[2,8,64]{2,1,0:T(8,128)S(1)} fusion(f32[2,1024,64,8]{1,2,3,0:T(8,128)} %get-tuple-element.422, f32[2,8,64]{2,1,0:T(8,128)S(1)} %select_maximum_fusion.2, pred[64,1024]{1,0:T(8,128)(4,1)S(1)} %constant_dynamic-slice_fusion.2), kind=kLoop, calls=%fused_computation.25.clone.1 | loop fusion | flops 5241856 | bytes 4268032 | tf_op jit(solution)/shard_map/cond/branch_1_fun/while/body/eval_jaxpr/reduce_sum | solution.py:52
  207.4 1.3 fusion.57
  208.7 3.3 %fusion.58 = f32[2,8,64,128]{3,2,1,0:T(8,128)} fusion(f32[2,1024,64,8]{1,2,3,0:T(8,128)S(1)} %copy-done, f32[2,8,64]{2,1,0:T(8,128)S(1)} %select_maximum_fusion.2, pred[64,1024]{1,0:T(8,128)(4,1)S(1)} %constant_dynamic-slice_fusion.2, f32[2,8,64,128]{3,2,1,0:T(8,128)} %get-tuple-element.440, bf16[7168,2,128]{0,2,1:T(8,128)(2,1)} %get-tuple-element.456, ...), kind=kOutput, calls=%fused_computation.28.clone.1 | convolution fusion | flops 274071552 | bytes 5840901 | tf_op jit(solution)/shard_map/cond/branch_1_fun/while/body/eval_jaxpr/kgrn,nkd->kgrd/dot_general | solution.py:53
  212.0 3.8 %fusion.55 = (f32[2,8,64]{2,1,0:T(8,128)S(1)}, f32[2,1024,64,8]{1,2,3,0:T(8,128)}) fusion(pred[64,1024]{1,0:T(8,128)(4,1)S(1)} %constant_dynamic-slice_fusion.2, bf16[64,2,8,128]{3,0,2,1:T(8,128)(2,1)S(1)} %get-tuple-element.455, bf16[7168,2,128]{0,2,1:T(8,128)(2,1)} %get-tuple-element.454, s32[]{:T(128)S(6)} %select_n.114), kind=kOutput, calls=%fused_computation.23.clone.1 | convolution fusion | flops 271580160 | bytes 5050372 | tf_op jit(solution)/shard_map/cond/branch_1_fun/while/body/eval_jaxpr/rkgd,nkd->kgrn/dot_general | solution.py:44
  215.8 3.6 %fusion.56 = f32[2,8,64]{2,1,0:T(8,128)S(1)} fusion(f32[2,1024,64,8]{1,2,3,0:T(8,128)} %get-tuple-element.422, f32[2,8,64]{2,1,0:T(8,128)S(1)} %select_maximum_fusion.2, pred[64,1024]{1,0:T(8,128)(4,1)S(1)} %constant_dynamic-slice_fusion.2), kind=kLoop, calls=%fused_computation.25.clone.1 | loop fusion | flops 5241856 | bytes 4268032 | tf_op jit(solution)/shard_map/cond/branch_1_fun/while/body/eval_jaxpr/reduce_sum | solution.py:52
  219.5 1.3 fusion.57
  220.8 3.3 %fusion.58 = f32[2,8,64,128]{3,2,1,0:T(8,128)} fusion(f32[2,1024,64,8]{1,2,3,0:T(8,128)S(1)} %copy-done, f32[2,8,64]{2,1,0:T(8,128)S(1)} %select_maximum_fusion.2, pred[64,1024]{1,0:T(8,128)(4,1)S(1)} %constant_dynamic-slice_fusion.2, f32[2,8,64,128]{3,2,1,0:T(8,128)} %get-tuple-element.440, bf16[7168,2,128]{0,2,1:T(8,128)(2,1)} %get-tuple-element.456, ...), kind=kOutput, calls=%fused_computation.28.clone.1 | convolution fusion | flops 274071552 | bytes 5840901 | tf_op jit(solution)/shard_map/cond/branch_1_fun/while/body/eval_jaxpr/kgrn,nkd->kgrd/dot_general | solution.py:53
  224.1 3.8 %fusion.55 = (f32[2,8,64]{2,1,0:T(8,128)S(1)}, f32[2,1024,64,8]{1,2,3,0:T(8,128)}) fusion(pred[64,1024]{1,0:T(8,128)(4,1)S(1)} %constant_dynamic-slice_fusion.2, bf16[64,2,8,128]{3,0,2,1:T(8,128)(2,1)S(1)} %get-tuple-element.455, bf16[7168,2,128]{0,2,1:T(8,128)(2,1)} %get-tuple-element.454, s32[]{:T(128)S(6)} %select_n.114), kind=kOutput, calls=%fused_computation.23.clone.1 | convolution fusion | flops 271580160 | bytes 5050372 | tf_op jit(solution)/shard_map/cond/branch_1_fun/while/body/eval_jaxpr/rkgd,nkd->kgrn/dot_general | solution.py:44
  227.9 3.6 %fusion.56 = f32[2,8,64]{2,1,0:T(8,128)S(1)} fusion(f32[2,1024,64,8]{1,2,3,0:T(8,128)} %get-tuple-element.422, f32[2,8,64]{2,1,0:T(8,128)S(1)} %select_maximum_fusion.2, pred[64,1024]{1,0:T(8,128)(4,1)S(1)} %constant_dynamic-slice_fusion.2), kind=kLoop, calls=%fused_computation.25.clone.1 | loop fusion | flops 5241856 | bytes 4268032 | tf_op jit(solution)/shard_map/cond/branch_1_fun/while/body/eval_jaxpr/reduce_sum | solution.py:52
  231.5 1.3 fusion.57
  232.8 3.3 %fusion.58 = f32[2,8,64,128]{3,2,1,0:T(8,128)} fusion(f32[2,1024,64,8]{1,2,3,0:T(8,128)S(1)} %copy-done, f32[2,8,64]{2,1,0:T(8,128)S(1)} %select_maximum_fusion.2, pred[64,1024]{1,0:T(8,128)(4,1)S(1)} %constant_dynamic-slice_fusion.2, f32[2,8,64,128]{3,2,1,0:T(8,128)} %get-tuple-element.440, bf16[7168,2,128]{0,2,1:T(8,128)(2,1)} %get-tuple-element.456, ...), kind=kOutput, calls=%fused_computation.28.clone.1 | convolution fusion | flops 274071552 | bytes 5840901 | tf_op jit(solution)/shard_map/cond/branch_1_fun/while/body/eval_jaxpr/kgrn,nkd->kgrd/dot_general | solution.py:53
  236.1 0.7 compare_select_fusion
  236.8 1.3 multiply_bitcast_fusion
  238.1 0.2 copy.62
  238.4 0.8 select_convert_fusion
  239.2 3.4 %all-to-all-start.1 = ((bf16[4,16,2048]{2,1,0:T(8,128)(2,1)}), bf16[4,16,2048]{2,1,0:T(8,128)(2,1)S(1)}, u32[]{:S(2)}, u32[]{:S(2)}) async-start(bf16[4,16,2048]{2,1,0:T(8,128)(2,1)} %select_convert_fusion), calls=%async_computation.1 | async-start | bytes 524288 | tf_op jit(solution)/shard_map/all_to_all | solution.py:178
  242.6 0.7 copy.77
  243.3 5.3 %all-to-all-done.1 = bf16[4,16,2048]{2,1,0:T(8,128)(2,1)S(1)} async-done(((bf16[4,16,2048]{2,1,0:T(8,128)(2,1)}), bf16[4,16,2048]{2,1,0:T(8,128)(2,1)S(1)}, u32[]{:S(2)}, u32[]{:S(2)}) %all-to-all-start.1) | async-done | bytes 262176 | tf_op jit(solution)/shard_map/all_to_all | solution.py:178
  248.6 0.7 copy.78
  (72 shorter events, 1.1 us)
Async XLA Ops:
  7.2 5.9 %copy-start.2 = (bf16[64,256]{1,0:T(8,128)(2,1)S(1)}, bf16[64,256]{1,0:T(8,128)(2,1)}, u32[]{:S(2)}) copy-start(bf16[64,256]{1,0:T(8,128)(2,1)} %param.16) | copy-start | bytes 98308
  7.2 6.0 %copy-start.3 = (bf16[64,256]{1,0:T(8,128)(2,1)S(1)}, bf16[64,256]{1,0:T(8,128)(2,1)}, u32[]{:S(2)}) copy-start(bf16[64,256]{1,0:T(8,128)(2,1)} %param.17) | copy-start | bytes 98308
  7.2 80.0 %all-gather.3.cloned.1.call-start = ((), (), s32[]{:S(2)}) async-start(), calls=%async_computation.2 | async-start | bytes 4128768 | tf_op jit(solution)/shard_map/all_gather | solution.py:161
  9.3 142.5 %all-gather.5.cloned.1.call-start = ((), (), s32[]{:S(2)}) async-start(), calls=%async_computation.3 | async-start | bytes 4128768 | tf_op jit(solution)/shard_map/all_gather | solution.py:162
  76.4 7.5 %copy-start.4 = (s32[4,2]{0,1:T(2,128)S(1)}, s32[4,2]{0,1:T(2,128)}, u32[]{:S(2)}) copy-start(s32[4,2]{0,1:T(2,128)} %param.22) | copy-start | bytes 100
  76.4 75.3 %copy-start.1 = (bf16[64,2048]{1,0:T(8,128)(2,1)S(1)}, bf16[64,2048]{1,0:T(8,128)(2,1)}, u32[]{:S(2)}) copy-start(bf16[64,2048]{1,0:T(8,128)(2,1)} %param.19) | copy-start | bytes 786436
  79.8 159.4 %all-to-all-start = ((bf16[4,16,2048]{2,1,0:T(8,128)(2,1)}), bf16[4,16,2048]{2,1,0:T(8,128)(2,1)S(1)}, u32[]{:S(2)}, u32[]{:S(2)}) async-start(bf16[4,16,2048]{2,1,0:T(8,128)(2,1)} %convert_element_type.43), calls=%async_computation | async-start | bytes 524288 | tf_op jit(solution)/shard_map/all_to_all | solution.py:177
  156.4 4.2 %copy-start = (f32[2,1024,64,8]{1,2,3,0:T(8,128)S(1)}, f32[2,1024,64,8]{1,2,3,0:T(8,128)}, u32[]{:S(2)}) copy-start(f32[2,1024,64,8]{1,2,3,0:T(8,128)} %get-tuple-element.422) | copy-start | bytes 12582916 | tf_op jit(solution)/shard_map/cond/branch_1_fun/while
  167.6 4.9 %copy-start = (f32[2,1024,64,8]{1,2,3,0:T(8,128)S(1)}, f32[2,1024,64,8]{1,2,3,0:T(8,128)}, u32[]{:S(2)}) copy-start(f32[2,1024,64,8]{1,2,3,0:T(8,128)} %get-tuple-element.422) | copy-start | bytes 12582916 | tf_op jit(solution)/shard_map/cond/branch_1_fun/while
  179.7 4.9 %copy-start = (f32[2,1024,64,8]{1,2,3,0:T(8,128)S(1)}, f32[2,1024,64,8]{1,2,3,0:T(8,128)}, u32[]{:S(2)}) copy-start(f32[2,1024,64,8]{1,2,3,0:T(8,128)} %get-tuple-element.422) | copy-start | bytes 12582916 | tf_op jit(solution)/shard_map/cond/branch_1_fun/while
  191.7 4.9 %copy-start = (f32[2,1024,64,8]{1,2,3,0:T(8,128)S(1)}, f32[2,1024,64,8]{1,2,3,0:T(8,128)}, u32[]{:S(2)}) copy-start(f32[2,1024,64,8]{1,2,3,0:T(8,128)} %get-tuple-element.422) | copy-start | bytes 12582916 | tf_op jit(solution)/shard_map/cond/branch_1_fun/while
  203.8 4.9 %copy-start = (f32[2,1024,64,8]{1,2,3,0:T(8,128)S(1)}, f32[2,1024,64,8]{1,2,3,0:T(8,128)}, u32[]{:S(2)}) copy-start(f32[2,1024,64,8]{1,2,3,0:T(8,128)} %get-tuple-element.422) | copy-start | bytes 12582916 | tf_op jit(solution)/shard_map/cond/branch_1_fun/while
  215.8 4.9 %copy-start = (f32[2,1024,64,8]{1,2,3,0:T(8,128)S(1)}, f32[2,1024,64,8]{1,2,3,0:T(8,128)}, u32[]{:S(2)}) copy-start(f32[2,1024,64,8]{1,2,3,0:T(8,128)} %get-tuple-element.422) | copy-start | bytes 12582916 | tf_op jit(solution)/shard_map/cond/branch_1_fun/while
  227.9 4.9 %copy-start = (f32[2,1024,64,8]{1,2,3,0:T(8,128)S(1)}, f32[2,1024,64,8]{1,2,3,0:T(8,128)}, u32[]{:S(2)}) copy-start(f32[2,1024,64,8]{1,2,3,0:T(8,128)} %get-tuple-element.422) | copy-start | bytes 12582916 | tf_op jit(solution)/shard_map/cond/branch_1_fun/while
  239.2 9.4 %all-to-all-start.1 = ((bf16[4,16,2048]{2,1,0:T(8,128)(2,1)}), bf16[4,16,2048]{2,1,0:T(8,128)(2,1)S(1)}, u32[]{:S(2)}, u32[]{:S(2)}) async-start(bf16[4,16,2048]{2,1,0:T(8,128)(2,1)} %select_convert_fusion), calls=%async_computation.1 | async-start | bytes 524288 | tf_op jit(solution)/shard_map/all_to_all | solution.py:178
Sparse Core Ops, SparseCore 0:
  10.2 73.8 all-gather.2
  86.3 65.3 all-gather.4
where the time goes:
time: 257 us; the launch traced here: 256 us
  waiting for transfers between devices  69.8 us (27%)
  blocking collectives  60.7 us (24%)
  matrix products  50.8 us (20%)
  other arithmetic  43.3 us (17%)
  between operations  16.3 us (6%)
  local copies, waits for them, and re-layouts  8.18 us (3%)
  starting transfers between devices  6.89 us (3%)
    all_gather x1, waiting for transfers between devices, on_device(): value_rows = lax.all_gather(vision_values, 'ctx', axis=0, tiled=True)  64.5 us
    all_gather x1, blocking collectives, on_device(): value_rows = lax.all_gather(self_values, 'ctx', axis=0, tiled=True)  31.7 us
    all_gather x1, blocking collectives, on_device(): key_rows = lax.all_gather(rotated_key, 'ctx', axis=0, tiled=True)  29 us
    dot_general x8, matrix products, attend_block(): jnp.einsum('rkgd,nkd->kgrn', queries, key_rows, preferred_element_type=jn...  27 us
    reduce_sum x8, other arithmetic, attend_block(): totals = totals * factor + jnp.sum(weights, axis=-1)  26 us
    dot_general x8, matrix products, attend_block(): jnp.einsum('kgrn,nkd->kgrd', weights.astype(jnp.bfloat16), value_rows, pr...  23.8 us
    add x7, other arithmetic, attend_block(): totals = totals * factor + jnp.sum(weights, axis=-1)  8.5 us
    all_to_all x1, waiting for transfers between devices, on_device(): lax.all_to_all(cross_rows, 'head', split_axis=0, concat_axis=1, tiled=True)  5.28 us
  transfers between devices with their start and end apart: 4, of which 2 were waited for; matrix products, arithmetic and copies ran while one was open for 39% of the time, Pallas kernels for 0%

commit v1 on v0

--- a/solution.py
+++ b/solution.py
@@ -1,6 +1,10 @@
+import functools
+
 import jax
 import jax.numpy as jnp
 from jax import lax
+from jax.experimental import pallas as pl
+from jax.experimental.pallas import tpu as pltpu
 from jax.sharding import PartitionSpec as P
 
 HD = 128
@@ -110,7 +114,7 @@
     )
 
 
-def on_device(
+def on_device_gathered(
     query_self,
     key_self,
     value_self,
@@ -180,6 +184,479 @@
     return (self_context, cross_context)
 
 
+log2e = 1.4426950408889634
+stat_rows = 16
+unseen = -1e30
+contract_last = (((1,), (1,)), ((), ()))
+
+
+def whole(count):
+    return [pl.BlockSpec(memory_space=pltpu.VMEM)] * count
+
+
+def split_heads_kernel(inner, key_ref, value_ref, keep_ref, other_ref):
+    place = lax.rem(lax.axis_index("ctx"), inner)
+    for slot, source in enumerate((key_ref, value_ref)):
+        for side, target in enumerate((keep_ref, other_ref)):
+            head = place if side == 0 else 1 - place
+            target[slot] = source[:, pl.ds(pl.multiple_of(head * HD, HD), HD)]
+
+
+def split_heads(keys, values, inner):
+    rows, columns = keys.shape
+    shape = jax.ShapeDtypeStruct((2, rows, columns // inner), keys.dtype)
+    return pl.pallas_call(
+        functools.partial(split_heads_kernel, inner),
+        out_shape=(shape, shape),
+        in_specs=whole(2),
+        out_specs=whole(2),
+        compiler_params=pltpu.CompilerParams(vmem_limit_bytes=24 * 2**20),
+        name="split_vision_heads",
+    )(keys, values)
+
+
+def pack_queries_kernel(
+    inner,
+    query_ref,
+    key_ref,
+    value_ref,
+    cross_ref,
+    cosine_ref,
+    sine_ref,
+    range_ref,
+    keep_ref,
+    other_ref,
+):
+    group = query_ref.shape[1] // inner
+    place = lax.rem(lax.axis_index("ctx"), inner)
+    cosine = cosine_ref[...]
+    sine = sine_ref[...]
+
+    def turned(block):
+        block = block.astype(jnp.float32)
+        return (block * cosine + pltpu.roll(block, HD // 2, 1) * sine).astype(jnp.bfloat16)
+
+    def head_columns(head):
+        return pl.ds(pl.multiple_of(head * HD, HD), HD)
+
+    for side, target in enumerate((keep_ref, other_ref)):
+        head = place if side == 0 else 1 - place
+        target[:, :group] = cross_ref[:, pl.ds(pl.multiple_of(head * group, group), group)]
+        target[:, group : group + HD] = range_ref[...]
+        target[:, group + HD : group + 2 * HD] = turned(key_ref[:, head_columns(head)])
+        target[:, group + 2 * HD : group + 3 * HD] = value_ref[:, head_columns(head)]
+        begin = group + 3 * HD
+        for item in range(group // HD):
+            target[:, begin + item * HD : begin + (item + 1) * HD] = turned(
+                query_ref[:, head_columns(head * (group // HD) + item)]
+            )
+
+
+def pack_queries(query_self, key_self, value_self, query_cross, cosine, sine, ranges, inner):
+    rows, columns = query_self.shape
+    shape = jax.ShapeDtypeStruct((rows, 2 * (columns // inner) + 3 * HD), jnp.bfloat16)
+    return pl.pallas_call(
+        functools.partial(pack_queries_kernel, inner),
+        out_shape=(shape, shape),
+        in_specs=whole(7),
+        out_specs=whole(2),
+        name="rotate_and_pack",
+    )(query_self, key_self, value_self, query_cross, cosine, sine, ranges)
+
+
+def stack_heads(source_ref, row, column, heads, target_ref):
+    for block in range(target_ref.shape[0] // (heads * TBLOCK)):
+        for head in range(heads):
+            begin = (block * heads + head) * TBLOCK
+            target_ref[begin : begin + TBLOCK, :] = source_ref[
+                row + block * TBLOCK : row + (block + 1) * TBLOCK,
+                column + head * HD : column + (head + 1) * HD,
+            ]
+
+
+def fold_keys(keys, values_turned, stacked_ref, peak_ref, total_ref, visible):
+    scale = HD**-0.5 * log2e
+    width = min(256, stacked_ref.shape[0])
+    spans = [slice(begin, begin + width) for begin in range(0, stacked_ref.shape[0], width)]
+    scores = [
+        lax.dot_general(
+            keys, stacked_ref[span, :], contract_last, preferred_element_type=jnp.float32
+        )
+        for span in spans
+    ]
+    for span, score in zip(spans, scores):
+        peak = peak_ref[0:1, span]
+        seen = visible[:, span]
+        if seen.shape[0] == 1:
+            highest = jnp.max(score, axis=0, keepdims=True) * scale
+            new_peak = jnp.where(seen, jnp.maximum(peak, highest), peak)
+            weights = jnp.exp2(score * scale - jnp.where(seen, new_peak, -unseen))
+        else:
+            score = jnp.where(seen, score * scale, unseen)
+            new_peak = jnp.maximum(peak, jnp.max(score, axis=0, keepdims=True))
+            weights = jnp.where(seen, jnp.exp2(score - new_peak), 0.0)
+        total_ref[:, span] = total_ref[:, span] * jnp.exp2(peak - new_peak) + jnp.dot(
+            values_turned, weights.astype(jnp.bfloat16), preferred_element_type=jnp.float32
+        )
+        peak_ref[0:1, span] = new_peak
+
+
+def clear(peak_ref, total_ref):
+    peak_ref[...] = jnp.full(peak_ref.shape, unseen, jnp.float32)
+    total_ref[...] = jnp.zeros(total_ref.shape, jnp.float32)
+
+
+def finish_columns(peak_ref, total_ref):
+    sums = total_ref[HD : HD + 1, :]
+    some = sums > 0.0
+    safe = jnp.where(some, sums, 1.0)
+    log_sum = jnp.where(some, peak_ref[0:1, :] + jnp.log2(safe), unseen)
+    return total_ref[:HD, :] / safe, log_sum
+
+
+def turn_values(value, target_ref):
+    target_ref[:HD, :] = value.T
+    target_ref[HD:, :] = jnp.ones((stat_rows, target_ref.shape[1]), jnp.bfloat16)
+
+
+def frame_numbers(inner):
+    device = lax.axis_index("ctx")
+    plane, place = device // inner, lax.rem(device, inner)
+    near = plane + 1 - 2 * lax.rem(plane, 2)
+    return (
+        plane * inner + place,
+        plane * inner + 1 - place,
+        near * inner + place,
+        near * inner + 1 - place,
+    )
+
+
+def cross_kernel(inner, heads, groups, packed, table_ref, *refs):
+    query_count = 1 + max(argument for _, argument, _ in groups)
+    query_refs, frame_refs = refs[:query_count], refs[query_count : query_count + 4]
+    out_refs, scratch = refs[query_count + 4 : -4], refs[-4:]
+    turned_ref, stacked_ref, peak_ref, total_ref = scratch
+    lanes = heads * TBLOCK
+    blocks = stacked_ref.shape[0] // lanes
+    frames = frame_numbers(inner)
+    for index in range(4):
+        turn_values(frame_refs[index][1], turned_ref.at[index])
+    for slot, (number, argument, row) in enumerate(groups):
+        stack_heads(query_refs[argument], row, 0, heads, stacked_ref)
+        clear(peak_ref, total_ref)
+        for index in range(4):
+            flags = []
+            for block in range(blocks):
+                at = 2 * (number * blocks + block)
+                inside = jnp.logical_and(
+                    table_ref[at] <= frames[index], frames[index] < table_ref[at + 1]
+                )
+                flags.append(inside.astype(jnp.int32))
+
+            @pl.when(functools.reduce(jnp.maximum, flags) > 0)
+            def _():
+                visible = jnp.concatenate(
+                    [jnp.full((1, lanes), flag, jnp.int32) for flag in flags], axis=1
+                )
+                fold_keys(
+                    frame_refs[index][0],
+                    turned_ref[index],
+                    stacked_ref,
+                    peak_ref,
+                    total_ref,
+                    visible > 0,
+                )
+
+        mixed, log_sum = finish_columns(peak_ref, total_ref)
+        for block in range(blocks):
+            span = slice(block * lanes, (block + 1) * lanes)
+            part, stat = mixed[:, span], log_sum[:, span]
+            if packed:
+                high = stat.astype(jnp.bfloat16)
+                rest = stat - high.astype(jnp.float32)
+                middle = rest.astype(jnp.bfloat16)
+                low = (rest - middle.astype(jnp.float32)).astype(jnp.bfloat16)
+                rows = [high, middle, low, jnp.zeros((stat_rows - 3, lanes), jnp.bfloat16)]
+                out_refs[0][slot * blocks + block, :HD, :] = part.astype(jnp.bfloat16)
+                out_refs[0][slot * blocks + block, HD:, :] = jnp.concatenate(rows, axis=0)
+            else:
+                out_refs[0][slot * blocks + block] = part
+                out_refs[1][slot * blocks + block] = jnp.broadcast_to(stat, (8, lanes))
+
+
+def cross_part(table, queries, frames, groups, rows, inner, heads, packed):
+    lanes = heads * TBLOCK
+    count = len(groups) * (rows // TBLOCK)
+    if packed:
+        out_shape = (jax.ShapeDtypeStruct((count, HD + stat_rows, lanes), jnp.bfloat16),)
+    else:
+        out_shape = (
+            jax.ShapeDtypeStruct((count, HD, lanes), jnp.float32),
+            jax.ShapeDtypeStruct((count, 8, lanes), jnp.float32),
+        )
+    return pl.pallas_call(
+        functools.partial(cross_kernel, inner, heads, groups, packed),
+        out_shape=out_shape,
+        in_specs=[pl.BlockSpec(memory_space=pltpu.SMEM)] + whole(len(queries) + 4),
+        out_specs=whole(len(out_shape)),
+        scratch_shapes=[
+            pltpu.VMEM((4, HD + stat_rows, frames[0].shape[1]), jnp.bfloat16),
+            pltpu.VMEM((rows * heads, HD), jnp.bfloat16),
+            pltpu.VMEM((8, rows * heads), jnp.float32),
+            pltpu.VMEM((HD + stat_rows, rows * heads), jnp.float32),
+        ],
+        compiler_params=pltpu.CompilerParams(vmem_limit_bytes=40 * 2**20),
+        name="cross_return" if packed else "cross_own",
+    )(table, *queries, *frames)
+
+
+def self_kernel(
+    inner, heads, own_ref, partner_ref, far_ref, across_ref, near_ref, last_ref, out_ref, *scratch
+):
+    key_ref, turned_ref, stacked_ref, peak_ref, total_ref = scratch
+    device = lax.axis_index("ctx")
+    plane, place = device // inner, lax.rem(device, inner)
+    rows = own_ref.shape[0]
+    lanes = heads * TBLOCK
+    group = heads * HD
+    first = group + HD
+    key_ref[:rows, :] = own_ref[:, first : first + HD]
+    key_ref[rows : 2 * rows, :] = partner_ref[:, first : first + HD]
+    key_ref[2 * rows : 4 * rows, :] = near_ref[:, :HD]
+    key_ref[4 * rows : 5 * rows, :] = far_ref[:, first : first + HD]
+    key_ref[5 * rows : 6 * rows, :] = across_ref[:, first : first + HD]
+    key_ref[6 * rows :, :] = last_ref[:, :HD]
+    values = jnp.concatenate(
+        [
+            own_ref[:, first + HD : first + 2 * HD],
+            partner_ref[:, first + HD : first + 2 * HD],
+            near_ref[:, HD:],
+            far_ref[:, first + HD : first + 2 * HD],
+            across_ref[:, first + HD : first + 2 * HD],
+            last_ref[:, HD:],
+        ],
+        axis=0,
+    )
+    turn_values(values, turned_ref)
+    keys = key_ref[...]
+    planes = (
+        plane,
+        plane + 1 - 2 * lax.rem(plane, 2),
+        lax.rem(plane + 2, 4),
+        3 - plane,
+    )
+    starts = []
+    for source in planes:
+        starts.append((source * inner + place) * rows)
+        starts.append((source * inner + 1 - place) * rows)
+    down = lax.broadcasted_iota(jnp.int32, (rows, rows * heads), 0)
+    key_index = jnp.concatenate([down + start for start in starts], axis=0)
+    across = lax.broadcasted_iota(jnp.int32, key_index.shape, 1)
+    token = (across // lanes) * TBLOCK + lax.rem(across, TBLOCK)
+    for slot, query_ref in enumerate((own_ref, partner_ref)):
+        side = place if slot == 0 else 1 - place
+        stack_heads(query_ref, 0, group + 3 * HD, heads, stacked_ref)
+        clear(peak_ref, total_ref)
+        visible = key_index <= token + (plane * inner + side) * rows
+        fold_keys(keys, turned_ref[...], stacked_ref, peak_ref, total_ref, visible)
+        mixed, _ = finish_columns(peak_ref, total_ref)
+        blocks = rows // TBLOCK
+        for block in range(blocks):
+            part = mixed[:, block * lanes : (block + 1) * lanes].T.astype(jnp.bfloat16)
+            for head in range(heads):
+                out_ref[block * inner + side, :, head * HD : (head + 1) * HD] = part[
+                    head * TBLOCK : (head + 1) * TBLOCK
+                ]
+
+
+def self_part(own, partner, far, far_across, near, last, inner, heads):
+    rows = own.shape[0]
+    return pl.pallas_call(
+        functools.partial(self_kernel, inner, heads),
+        out_shape=jax.ShapeDtypeStruct((inner * rows // TBLOCK, TBLOCK, heads * HD), jnp.bfloat16),
+        in_specs=whole(6),
+        out_specs=whole(1)[0],
+        scratch_shapes=[
+            pltpu.VMEM((8 * rows, HD), jnp.bfloat16),
+            pltpu.VMEM((HD + stat_rows, 8 * rows), jnp.bfloat16),
+            pltpu.VMEM((rows * heads, HD), jnp.bfloat16),
+            pltpu.VMEM((8, rows * heads), jnp.float32),
+            pltpu.VMEM((HD + stat_rows, rows * heads), jnp.float32),
+        ],
+        compiler_params=pltpu.CompilerParams(vmem_limit_bytes=40 * 2**20),
+        name="self_attention",
+    )(own, partner, far, far_across, near, last)
+
+
+def combine_kernel(inner, heads, gate_ref, mixed_ref, stat_ref, returned_ref, self_ref, out_ref):
+    count = mixed_ref.shape[0]
+    group = heads * HD
+    side = count // inner
+    place = lax.rem(lax.axis_index("ctx"), inner)
+    gate = jnp.tanh(jnp.full((1, heads * TBLOCK), gate_ref[0], jnp.float32))
+    for block in range(count):
+        target = (block % side) * inner + (place if block < side else 1 - place)
+        stats = returned_ref[block, HD:, :].astype(jnp.float32)
+        far_stat = stats[0:1] + stats[1:2] + stats[2:3]
+        own_stat = stat_ref[block, 0:1, :]
+        peak = jnp.maximum(own_stat, far_stat)
+        own_weight = jnp.exp2(own_stat - peak)
+        far_weight = jnp.exp2(far_stat - peak)
+        ratio = gate / (own_weight + far_weight)
+        mixed = mixed_ref[block] * (own_weight * ratio) + returned_ref[block, :HD, :].astype(
+            jnp.float32
+        ) * (far_weight * ratio)
+        part = mixed.T.astype(jnp.bfloat16)
+        for head in range(heads):
+            out_ref[target, :, head * HD : (head + 1) * HD] = part[
+                head * TBLOCK : (head + 1) * TBLOCK
+            ]
+    out_ref[:, :, group:] = self_ref[...]
+
+
+def combine(gate_scale, mixed, stat, returned, self_rows, inner, heads):
+    count = mixed.shape[0]
+    return pl.pallas_call(
+        functools.partial(combine_kernel, inner, heads),
+        out_shape=jax.ShapeDtypeStruct((count, TBLOCK, 2 * heads * HD), jnp.bfloat16),
+        in_specs=[pl.BlockSpec(memory_space=pltpu.SMEM)] + whole(4),
+        out_specs=whole(1)[0],
+        name="combine_planes",
+    )(gate_scale, mixed, stat, returned, self_rows)
+
+
+def spread_kernel(in_ref, self_ref, cross_ref):
+    group = in_ref.shape[2] // 2
+    for head in range(in_ref.shape[0]):
+        span = slice(head * group, (head + 1) * group)
+        cross_ref[:, span] = in_ref[head, :, :group]
+        self_ref[:, span] = in_ref[head, :, group:]
+
+
+def spread(inward):
+    count, rows, columns = inward.shape
+    shape = jax.ShapeDtypeStruct((rows, count * columns // 2), inward.dtype)
+    return pl.pallas_call(
+        spread_kernel,
+        out_shape=(shape, shape),
+        in_specs=whole(1),
+        out_specs=whole(2),
+        name="spread_heads",
+    )(inward)
+
+
+def on_device_split(
+    axes,
+    query_self,
+    key_self,
+    value_self,
+    positions,
+    query_cross,
+    key_vision,
+    value_vision,
+    media_range,
+    gate_scale,
+):
+    inner = key_self.shape[1] // HD
+    heads = query_self.shape[1] // key_self.shape[1]
+    rows = query_self.shape[0]
+    group = heads * HD
+    columns = axes["head"]
+    devices = axes["ctx"]
+    plane_count = devices // inner
+
+    def place_of(device):
+        return device // inner, device % inner
+
+    def send(values, turn, flip, upward=False):
+        pairs = []
+        for device in range(devices):
+            plane, place = place_of(device)
+            target = plane ^ turn
+            if not upward or target > plane:
+                pairs.append((device, target * inner + (place ^ flip)))
+        return lax.ppermute(values, "ctx", pairs)
+
+    kept_vision, other_vision = split_heads(key_vision, value_vision, inner)
+    vision_across = send(other_vision, 1, 1)
+    vision_near = send(kept_vision, 1, 0)
+    vision_beside = send(other_vision, 0, 1)
+
+    exponents = jnp.arange(HD // 2, dtype=jnp.float32) * (2.0 / HD)
+    frequency = jnp.power(rope_base, -exponents)
+    angles = positions.astype(jnp.float32)[:, None] * frequency[None, :]
+    cosine, sine = jnp.cos(angles), jnp.sin(angles)
+    ranges = jnp.repeat(media_range.astype(jnp.bfloat16), TBLOCK, axis=0)
+    ranges = jnp.pad(ranges, ((0, 0), (0, HD - media_range.shape[1])))
+    kept, other = pack_queries(
+        query_self,
+        key_self,
+        value_self,
+        query_cross,
+        jnp.concatenate([cosine, cosine], axis=1),
+        jnp.concatenate([-sine, sine], axis=1),
+        ranges,
+        inner,
+    )
+    partner = send(other, 0, 1)
+    first = group + HD
+    last = first + 2 * HD
+    far = send(kept[:, :last], 2, 0)
+    far_across = send(other[:, :last], 2, 1)
+    sides = (kept, partner)
+    packet = jnp.concatenate([side[:, first:last] for side in sides], axis=0)
+    near_self = send(packet, 1, 0, upward=True)
+    last_self = send(packet, 3, 0, upward=True)
+
+    table = [side[::TBLOCK, group : group + 2] for side in (kept, partner, far, far_across)]
+    table = jnp.concatenate(table).astype(jnp.int32).reshape(-1)
+    frames = (kept_vision, vision_beside, vision_near, vision_across)
+    (outgoing,) = cross_part(
+        table, (far, far_across), frames, ((2, 0, 0), (3, 1, 0)), rows, inner, heads, True
+    )
+    returned = send(outgoing, 2, 0)
+    mixed, stat = cross_part(
+        table, (kept, partner), frames, ((0, 0, 0), (1, 1, 0)), rows, inner, heads, False
+    )
+    self_rows = self_part(kept, partner, far, far_across, near_self, last_self, inner, heads)
+    outward = combine(gate_scale, mixed, stat, returned, self_rows, inner, heads)
+    planes = [
+        [
+            (plane * inner + place) * columns + column
+            for column in range(columns)
+            for place in range(inner)
+        ]
+        for plane in range(plane_count)
+    ]
+    inward = lax.all_to_all(
+        outward.reshape(-1, 2 * group),
+        ("ctx", "head"),
+        0,
+        0,
+        axis_index_groups=planes,
+        tiled=True,
+    )
+    return spread(inward.reshape(outward.shape))
+
+
+def on_device(axes, *arguments):
+    query_self, key_self, _, _, _, key_vision, _, media_range, _ = arguments
+    inner = key_self.shape[1] // HD
+    heads = query_self.shape[1] // key_self.shape[1]
+    rows = query_self.shape[0]
+    suited = (
+        inner == 2
+        and axes["ctx"] == 4 * inner
+        and heads * TBLOCK == HD
+        and key_vision.shape[0] == FRAME_LEN
+        and rows == axes["head"] * TBLOCK
+        and media_range.shape[0] * TBLOCK == rows
+    )
+    if suited:
+        return on_device_split(axes, *arguments)
+    return on_device_gathered(*arguments)
+
+
 def solution(mesh):
     placed = (
         P("ctx", "head"),
@@ -193,7 +670,7 @@
         P(),
     )
     return jax.shard_map(
-        on_device,
+        functools.partial(on_device, dict(mesh.shape)),
         mesh=mesh,
         in_specs=placed,
         out_specs=(P(("ctx", "head"), None), P(("ctx", "head"), None)),

time: 257 us -> 95 us (0.37)
  the two profiles are of different devices: /device:TPU:8 before, /device:TPU:9 now
where the time goes in v1:
time: 95 us; the launch traced here: 94.6 us
  waiting for transfers between devices  29.6 us (31%)
  Pallas kernels  24.4 us (26%)
  starting transfers between devices  16.9 us (18%)
  blocking collectives  14.4 us (15%)
  local copies, waits for them, and re-layouts  6.83 us (7%)
  between operations  1.46 us (2%)
  other arithmetic  1.01 us (1%)
    ppermute x9, waiting for transfers between devices, send(): return lax.ppermute(values, 'ctx', pairs)  29.6 us
    ppermute x9, starting transfers between devices, send(): return lax.ppermute(values, 'ctx', pairs)  16.9 us
    pallas_call x2, Pallas kernels, cross_part(): pl.pallas_call(functools.partial(cross_kernel, inner, heads, groups, pack...  16.7 us
    all_to_all x1, blocking collectives, on_device_split(): lax.all_to_all(outward.reshape(-1, 2 * group), ('ctx', 'head'), 0, 0, axi...  14.4 us
    unnamed x19, local copies, waits for them, and re-layouts  3.56 us
    pallas_call x1, Pallas kernels, combine(): pl.pallas_call(functools.partial(combine_kernel, inner, heads), out_shape...  2.22 us
    pallas_call x1, Pallas kernels, pack_queries(): pl.pallas_call(functools.partial(pack_queries_kernel, inner), out_shape=(...  2.14 us
  transfers between devices with their start and end apart: 9, of which 5 were waited for; matrix products, arithmetic and copies ran while one was open for 2% of the time, Pallas kernels for 9%

profile of v1, /device:TPU:9, one launch (start us, length us, event | category | flops | bytes accessed | tf_op | source)
XLA Modules:
  0.0 94.6 jit_solution(18260314092667174916)
XLA Ops:
  0.6 0.0 copy-start.8
  0.7 0.6 copy-done.8
  1.3 0.0 copy-start.7
  1.3 0.7 copy-done.7
  2.0 0.1 copy.20
  2.1 0.2 fusion
  2.3 0.6 pad.4.range_ref
  2.9 0.7 pad_maximum_fusion.1
  3.6 0.0 copy-start.3
  3.6 0.0 copy-start.4
  3.6 2.1 %rotate_and_pack.1 = (bf16[64,2432]{1,0:T(8,128)(2,1)}, bf16[64,2432]{1,0:T(8,128)(2,1)}) custom-call(bf16[64,2048]{1,0:T(8,128)(2,1)} %query_ref.1, bf16[64,256]{1,0:T(8,128)(2,1)} %key_ref.2, bf16[64,256]{1,0:T(8,128)(2,1)} %value_ref.2, bf16[64,2048]{1,0:T(8,128)(2,1)} %cross_ref.1, f32[64,128]{1,0:T(8,128)} %get-tuple-element.17.cosine_ref, ...), custom_call_target="tpu_custom_call" | custom-call | tf_op jit(solution)/shard_map/rotate_and_pack/pallas_call | solution.py:258
  5.8 0.9 slice.26
  6.7 2.4 %collective-permute-start.1 = (bf16[64,1408]{1,0:T(8,128)(2,1)S(1)}, bf16[64,1408]{1,0:T(8,128)(2,1)S(1)}, u32[]{:S(2)}, u32[]{:S(2)}) collective-permute-start(bf16[64,1408]{1,0:T(8,128)(2,1)S(1)} %slice.26), channel_id=1, source_target_pairs={{0,16},{4,20},{8,24},{12,28},{16,0},{20,4},{24,8},{28,12},{1,17},{... | collective-permute-start | bytes 540680 | tf_op jit(solution)/shard_map/ppermute | solution.py:578
  9.1 0.0 copy-done.3
  9.1 0.0 copy-done.4
  9.1 0.2 split_vision_heads.1
  9.3 0.0 copy-start
  9.3 0.2 collective-permute-start.4
  9.5 1.2 %collective-permute-start.3 = (bf16[2,896,128]{2,1,0:T(8,128)(2,1)S(1)}, bf16[2,896,128]{2,1,0:T(8,128)(2,1)S(1)}, u32[]{:S(2)}, u32[]{:S(2)}) collective-permute-start(bf16[2,896,128]{2,1,0:T(8,128)(2,1)S(1)} %get-tuple-element.11), channel_id=1, source_target_pairs={{0,4},{4,0},{8,12},{12,8},{16,20},{20,16},{24,28},{28,24},{1,5},{5... | collective-permute-start | bytes 1376264 | tf_op jit(solution)/shard_map/ppermute | solution.py:578
  10.7 1.2 %collective-permute-start.5 = (bf16[2,896,128]{2,1,0:T(8,128)(2,1)S(1)}, bf16[2,896,128]{2,1,0:T(8,128)(2,1)S(1)}, u32[]{:S(2)}, u32[]{:S(2)}) collective-permute-start(bf16[2,896,128]{2,1,0:T(8,128)(2,1)S(1)} %get-tuple-element.11), channel_id=1, source_target_pairs={{0,12},{4,8},{8,4},{12,0},{16,28},{20,24},{24,20},{28,16},{1,13},{... | collective-permute-start | bytes 1376264 | tf_op jit(solution)/shard_map/ppermute | solution.py:578
  12.0 1.2 %collective-permute-start = (bf16[64,2432]{1,0:T(8,128)(2,1)}, bf16[64,2432]{1,0:T(8,128)(2,1)S(1)}, u32[]{:S(2)}, u32[]{:S(2)}) collective-permute-start(bf16[64,2432]{1,0:T(8,128)(2,1)} %get-tuple-element.9), channel_id=1, source_target_pairs={{0,4},{4,0},{8,12},{12,8},{16,20},{20,16},{24,28},{28,24},{1,5},{5... | collective-permute-start | bytes 933896 | tf_op jit(solution)/shard_map/ppermute | solution.py:578
  13.2 1.0 %slice.28 = bf16[64,1408]{1,0:T(8,128)(2,1)S(1)} slice(bf16[64,2432]{1,0:T(8,128)(2,1)} %get-tuple-element.9), slice={[0:64], [0:1408]} | slice | bytes 360448 | tf_op jit(solution)/shard_map/slice | solution.py:605
  14.2 3.0 %collective-permute-done.1.refs_0_.far_ref = bf16[64,1408]{1,0:T(8,128)(2,1)S(1)} collective-permute-done((bf16[64,1408]{1,0:T(8,128)(2,1)S(1)}, bf16[64,1408]{1,0:T(8,128)(2,1)S(1)}, u32[]{:S(2)}, u32[]{:S(2)}) %collective-permute-start.1) | collective-permute-done | bytes 180256 | tf_op jit(solution)/shard_map/ppermute | solution.py:578
  17.2 4.1 %collective-permute-start.2 = (bf16[64,1408]{1,0:T(8,128)(2,1)S(1)}, bf16[64,1408]{1,0:T(8,128)(2,1)S(1)}, u32[]{:S(2)}, u32[]{:S(2)}) collective-permute-start(bf16[64,1408]{1,0:T(8,128)(2,1)S(1)} %slice.28), channel_id=1, source_target_pairs={{0,20},{4,16},{8,28},{12,24},{16,4},{20,0},{24,12},{28,8},{1,21},{... | collective-permute-start | bytes 540680 | tf_op jit(solution)/shard_map/ppermute | solution.py:578
  21.2 0.0 copy-done
  21.2 0.1 copy.14
  21.4 0.1 copy.16
  21.5 16.2 %collective-permute-done.2.refs_1_.across_ref = bf16[64,1408]{1,0:T(8,128)(2,1)S(1)} collective-permute-done((bf16[64,1408]{1,0:T(8,128)(2,1)S(1)}, bf16[64,1408]{1,0:T(8,128)(2,1)S(1)}, u32[]{:S(2)}, u32[]{:S(2)}) %collective-permute-start.2) | collective-permute-done | bytes 180256 | tf_op jit(solution)/shard_map/ppermute | solution.py:578
  37.7 0.1 copy.17
  37.8 2.8 %collective-permute-done.refs_1_.partner_ref = bf16[64,2432]{1,0:T(8,128)(2,1)S(1)} collective-permute-done((bf16[64,2432]{1,0:T(8,128)(2,1)}, bf16[64,2432]{1,0:T(8,128)(2,1)S(1)}, u32[]{:S(2)}, u32[]{:S(2)}) %collective-permute-start) | collective-permute-done | bytes 311328 | tf_op jit(solution)/shard_map/ppermute | solution.py:578
  40.7 0.1 copy.15
  40.8 0.1 maximum_convert_fusion
  40.9 0.1 copy.18
  40.9 0.1 reshape.25.table_ref
  41.0 0.0 collective-permute-done.4.refs_4_
  41.0 0.0 collective-permute-done.3.refs_3_
  41.1 0.0 collective-permute-done.5.refs_5_
  41.1 9.3 %cross_return.1 = bf16[8,144,128]{2,1,0:T(8,128)(2,1)S(1)} custom-call(s32[32]{0:T(128)S(1)} %reshape.25.table_ref, bf16[64,1408]{1,0:T(8,128)(2,1)S(1)} %collective-permute-done.1.refs_0_.far_ref, bf16[64,1408]{1,0:T(8,128)(2,1)S(1)} %collective-permute-done.2.refs_1_.across_ref, bf16[2,896,128]{2,1,0:T(8,128)(2,1)S(1)} %get-tuple-element.10.refs_2_, ...), custom_call_target="tpu_custom_call" | custom-call | tf_op jit(solution)/shard_map/cross_return/pallas_call | solution.py:397
  50.4 0.1 collective-permute-start.6
  50.5 1.3 %collective-permute-start.7 = (bf16[128,256]{1,0:T(8,128)(2,1)S(1)}, bf16[128,256]{1,0:T(8,128)(2,1)S(1)}, u32[]{:S(2)}, u32[]{:S(2)}) collective-permute-start(bf16[128,256]{1,0:T(8,128)(2,1)S(1)} %pad_maximum_fusion), channel_id=1, source_target_pairs={{0,8},{4,12},{16,24},{20,28},{1,9},{5,13},{17,25},{21,29},{2,10},{... | collective-permute-start | bytes 196616 | tf_op jit(solution)/shard_map/ppermute | solution.py:578
  51.8 5.1 %collective-permute-start.8 = (bf16[128,256]{1,0:T(8,128)(2,1)S(1)}, bf16[128,256]{1,0:T(8,128)(2,1)S(1)}, u32[]{:S(2)}, u32[]{:S(2)}) collective-permute-start(bf16[128,256]{1,0:T(8,128)(2,1)S(1)} %pad_maximum_fusion), channel_id=1, source_target_pairs={{0,24},{4,28},{8,16},{12,20},{1,25},{5,29},{9,17},{13,21},{2,26},{... | collective-permute-start | bytes 196616 | tf_op jit(solution)/shard_map/ppermute | solution.py:578
  57.6 0.8 collective-permute-done.7.near_ref
  58.4 6.8 %collective-permute-done.8.last_ref = bf16[128,256]{1,0:T(8,128)(2,1)S(1)} collective-permute-done((bf16[128,256]{1,0:T(8,128)(2,1)S(1)}, bf16[128,256]{1,0:T(8,128)(2,1)S(1)}, u32[]{:S(2)}, u32[]{:S(2)}) %collective-permute-start.8) | collective-permute-done | bytes 65568 | tf_op jit(solution)/shard_map/ppermute | solution.py:578
  65.2 1.3 %self_attention.1.self_ref = bf16[8,16,1024]{2,1,0:T(8,128)(2,1)S(1)} custom-call(bf16[64,2432]{1,0:T(8,128)(2,1)S(1)} %copy-done, bf16[64,2432]{1,0:T(8,128)(2,1)S(1)} %collective-permute-done.refs_1_.partner_ref, bf16[64,1408]{1,0:T(8,128)(2,1)S(1)} %collective-permute-done.1.refs_0_.far_ref, ...), custom_call_target="tpu_custom_call" | custom-call | tf_op jit(solution)/shard_map/self_attention/pallas_call | solution.py:474
  66.5 0.0 copy-start.1
  66.5 7.4 %cross_own.1 = (f32[8,128,128]{2,1,0:T(8,128)S(1)}, f32[8,8,128]{2,1,0:T(8,128)S(1)}) custom-call(s32[32]{0:T(128)S(1)} %reshape.25.table_ref, bf16[64,2432]{1,0:T(8,128)(2,1)S(1)} %copy-done, bf16[64,2432]{1,0:T(8,128)(2,1)S(1)} %collective-permute-done.refs_1_.partner_ref, bf16[2,896,128]{2,1,0:T(8,128)(2,1)S(1)} %get-tuple-element.10.refs_2_, ...), custom_call_target="tpu_custom_call" | custom-call | tf_op jit(solution)/shard_map/cross_own/pallas_call | solution.py:397
  73.9 0.0 copy-done.1
  74.0 0.0 copy-start.2
  74.0 0.8 copy-done.2
  74.8 0.0 copy-start.5
  74.8 0.6 copy-done.5
  75.4 0.0 collective-permute-done.6.returned_ref
  75.4 0.0 copy-start.6
  75.4 0.7 copy-done.6
  76.1 2.2 %combine_planes.1 = bf16[8,16,2048]{2,1,0:T(8,128)(2,1)} custom-call(f32[1]{0:T(128)S(6)} %copy.21.gate_ref, f32[8,128,128]{2,1,0:T(8,128)} %copy-done.2, f32[8,8,128]{2,1,0:T(8,128)} %copy-done.5, bf16[8,144,128]{2,1,0:T(8,128)(2,1)} %copy-done.6, bf16[8,16,1024]{2,1,0:T(8,128)(2,1)} %copy-done.1), custom_call_target="tpu_custom_call" | custom-call | tf_op jit(solution)/shard_map/combine_planes/pallas_call | solution.py:519
  78.3 14.4 %all_to_all.6.in_ref = bf16[8,16,2048]{2,1,0:T(8,128)(2,1)} all-to-all(bf16[8,16,2048]{2,1,0:T(8,128)(2,1)} %combine_planes.1), channel_id=1, replica_groups={{0,4,1,5,2,6,3,7},{8,12,9,13,10,14,11,15},{16,20,17,21,18,22,19,23},{24..., dimensions={0} | all-to-all | bytes 1048576 | tf_op jit(solution)/shard_map/all_to_all | solution.py:631
  92.7 1.9 %spread_heads.1 = (bf16[16,8192]{1,0:T(8,128)(2,1)}, bf16[16,8192]{1,0:T(8,128)(2,1)}) custom-call(bf16[8,16,2048]{2,1,0:T(8,128)(2,1)} %all_to_all.6.in_ref), custom_call_target="tpu_custom_call" | custom-call | tf_op jit(solution)/shard_map/spread_heads/pallas_call | solution.py:539
  (11 shorter events, 0.2 us)
Async XLA Ops:
  0.6 0.7 copy-start.8
  1.3 0.7 copy-start.7
  3.6 5.5 %copy-start.3 = (bf16[896,256]{1,0:T(8,128)(2,1)S(1)}, bf16[896,256]{1,0:T(8,128)(2,1)}, u32[]{:S(2)}) copy-start(bf16[896,256]{1,0:T(8,128)(2,1)} %key_ref.3) | copy-start | bytes 1376260
  3.6 5.5 %copy-start.4 = (bf16[896,256]{1,0:T(8,128)(2,1)S(1)}, bf16[896,256]{1,0:T(8,128)(2,1)}, u32[]{:S(2)}) copy-start(bf16[896,256]{1,0:T(8,128)(2,1)} %value_ref.3) | copy-start | bytes 1376260
  6.7 10.4 %collective-permute-start.1 = (bf16[64,1408]{1,0:T(8,128)(2,1)S(1)}, bf16[64,1408]{1,0:T(8,128)(2,1)S(1)}, u32[]{:S(2)}, u32[]{:S(2)}) collective-permute-start(bf16[64,1408]{1,0:T(8,128)(2,1)S(1)} %slice.26), channel_id=1, source_target_pairs={{0,16},{4,20},{8,24},{12,28},{16,0},{20,4},{24,8},{28,12},{1,17},{... | collective-permute-start | bytes 540680 | tf_op jit(solution)/shard_map/ppermute | solution.py:578
  9.3 12.0 %copy-start = (bf16[64,2432]{1,0:T(8,128)(2,1)S(1)}, bf16[64,2432]{1,0:T(8,128)(2,1)}, u32[]{:S(2)}) copy-start(bf16[64,2432]{1,0:T(8,128)(2,1)} %get-tuple-element.8.refs_0_.own_ref) | copy-start | bytes 933892
  9.3 31.8 %collective-permute-start.4 = (bf16[2,896,128]{2,1,0:T(8,128)(2,1)S(1)}, bf16[2,896,128]{2,1,0:T(8,128)(2,1)S(1)}, u32[]{:S(2)}, u32[]{:S(2)}) collective-permute-start(bf16[2,896,128]{2,1,0:T(8,128)(2,1)S(1)} %get-tuple-element.10.refs_2_), channel_id=1, source_target_pairs={{0,8},{4,12},{8,0},{12,4},{16,24},{20,28},{24,16},{28,20},{1,9},{5... | collective-permute-start | bytes 1376264 | tf_op jit(solution)/shard_map/ppermute | solution.py:578
  9.5 31.6 %collective-permute-start.3 = (bf16[2,896,128]{2,1,0:T(8,128)(2,1)S(1)}, bf16[2,896,128]{2,1,0:T(8,128)(2,1)S(1)}, u32[]{:S(2)}, u32[]{:S(2)}) collective-permute-start(bf16[2,896,128]{2,1,0:T(8,128)(2,1)S(1)} %get-tuple-element.11), channel_id=1, source_target_pairs={{0,4},{4,0},{8,12},{12,8},{16,20},{20,16},{24,28},{28,24},{1,5},{5... | collective-permute-start | bytes 1376264 | tf_op jit(solution)/shard_map/ppermute | solution.py:578
  10.7 30.3 %collective-permute-start.5 = (bf16[2,896,128]{2,1,0:T(8,128)(2,1)S(1)}, bf16[2,896,128]{2,1,0:T(8,128)(2,1)S(1)}, u32[]{:S(2)}, u32[]{:S(2)}) collective-permute-start(bf16[2,896,128]{2,1,0:T(8,128)(2,1)S(1)} %get-tuple-element.11), channel_id=1, source_target_pairs={{0,12},{4,8},{8,4},{12,0},{16,28},{20,24},{24,20},{28,16},{1,13},{... | collective-permute-start | bytes 1376264 | tf_op jit(solution)/shard_map/ppermute | solution.py:578
  12.0 28.7 %collective-permute-start = (bf16[64,2432]{1,0:T(8,128)(2,1)}, bf16[64,2432]{1,0:T(8,128)(2,1)S(1)}, u32[]{:S(2)}, u32[]{:S(2)}) collective-permute-start(bf16[64,2432]{1,0:T(8,128)(2,1)} %get-tuple-element.9), channel_id=1, source_target_pairs={{0,4},{4,0},{8,12},{12,8},{16,20},{20,16},{24,28},{28,24},{1,5},{5... | collective-permute-start | bytes 933896 | tf_op jit(solution)/shard_map/ppermute | solution.py:578
  17.2 20.6 %collective-permute-start.2 = (bf16[64,1408]{1,0:T(8,128)(2,1)S(1)}, bf16[64,1408]{1,0:T(8,128)(2,1)S(1)}, u32[]{:S(2)}, u32[]{:S(2)}) collective-permute-start(bf16[64,1408]{1,0:T(8,128)(2,1)S(1)} %slice.28), channel_id=1, source_target_pairs={{0,20},{4,16},{8,28},{12,24},{16,4},{20,0},{24,12},{28,8},{1,21},{... | collective-permute-start | bytes 540680 | tf_op jit(solution)/shard_map/ppermute | solution.py:578
  50.4 25.0 %collective-permute-start.6 = (bf16[8,144,128]{2,1,0:T(8,128)(2,1)S(1)}, bf16[8,144,128]{2,1,0:T(8,128)(2,1)S(1)}, u32[]{:S(2)}, u32[]{:S(2)}) collective-permute-start(bf16[8,144,128]{2,1,0:T(8,128)(2,1)S(1)} %cross_return.1), channel_id=1, source_target_pairs={{0,16},{4,20},{8,24},{12,28},{16,0},{20,4},{24,8},{28,12},{1,17},{... | collective-permute-start | bytes 884744 | tf_op jit(solution)/shard_map/ppermute | solution.py:578
  50.5 7.9 %collective-permute-start.7 = (bf16[128,256]{1,0:T(8,128)(2,1)S(1)}, bf16[128,256]{1,0:T(8,128)(2,1)S(1)}, u32[]{:S(2)}, u32[]{:S(2)}) collective-permute-start(bf16[128,256]{1,0:T(8,128)(2,1)S(1)} %pad_maximum_fusion), channel_id=1, source_target_pairs={{0,8},{4,12},{16,24},{20,28},{1,9},{5,13},{17,25},{21,29},{2,10},{... | collective-permute-start | bytes 196616 | tf_op jit(solution)/shard_map/ppermute | solution.py:578
  51.8 13.4 %collective-permute-start.8 = (bf16[128,256]{1,0:T(8,128)(2,1)S(1)}, bf16[128,256]{1,0:T(8,128)(2,1)S(1)}, u32[]{:S(2)}, u32[]{:S(2)}) collective-permute-start(bf16[128,256]{1,0:T(8,128)(2,1)S(1)} %pad_maximum_fusion), channel_id=1, source_target_pairs={{0,24},{4,28},{8,16},{12,20},{1,25},{5,29},{9,17},{13,21},{2,26},{... | collective-permute-start | bytes 196616 | tf_op jit(solution)/shard_map/ppermute | solution.py:578
  66.5 7.4 %copy-start.1 = (bf16[8,16,1024]{2,1,0:T(8,128)(2,1)}, bf16[8,16,1024]{2,1,0:T(8,128)(2,1)S(1)}, u32[]{:S(2)}) copy-start(bf16[8,16,1024]{2,1,0:T(8,128)(2,1)S(1)} %self_attention.1.self_ref) | copy-start | bytes 786436
  74.0 0.8 copy-start.2
  74.8 0.6 copy-start.5
  75.4 0.7 copy-start.6

commit v2 on v1

--- a/solution.py
+++ b/solution.py
@@ -194,84 +194,121 @@
     return [pl.BlockSpec(memory_space=pltpu.VMEM)] * count
 
 
-def split_heads_kernel(inner, key_ref, value_ref, keep_ref, other_ref):
-    place = lax.rem(lax.axis_index("ctx"), inner)
-    for slot, source in enumerate((key_ref, value_ref)):
-        for side, target in enumerate((keep_ref, other_ref)):
-            head = place if side == 0 else 1 - place
-            target[slot] = source[:, pl.ds(pl.multiple_of(head * HD, HD), HD)]
-
-
-def split_heads(keys, values, inner):
-    rows, columns = keys.shape
-    shape = jax.ShapeDtypeStruct((2, rows, columns // inner), keys.dtype)
-    return pl.pallas_call(
-        functools.partial(split_heads_kernel, inner),
-        out_shape=(shape, shape),
-        in_specs=whole(2),
-        out_specs=whole(2),
-        compiler_params=pltpu.CompilerParams(vmem_limit_bytes=24 * 2**20),
-        name="split_vision_heads",
-    )(keys, values)
-
-
-def pack_queries_kernel(
+def prepare_kernel(
     inner,
+    range_ref,
+    cosine_ref,
+    sine_ref,
+    vision_key_ref,
+    vision_value_ref,
+    cross_ref,
     query_ref,
     key_ref,
     value_ref,
-    cross_ref,
-    cosine_ref,
-    sine_ref,
-    range_ref,
-    keep_ref,
+    near_ref,
+    across_ref,
+    beside_ref,
+    own_ref,
     other_ref,
+    own_self_ref,
+    cross_rows,
+    query_rows,
+    key_rows,
+    value_rows,
+    semaphores,
 ):
-    group = query_ref.shape[1] // inner
+    rows = query_rows.shape[0]
+    heads = query_rows.shape[1] // inner // HD
+    vision = vision_key_ref.shape[0]
     place = lax.rem(lax.axis_index("ctx"), inner)
-    cosine = cosine_ref[...]
-    sine = sine_ref[...]
+    sides = (place, 1 - place)
+
+    def head_columns(head):
+        return pl.ds(pl.multiple_of(head * HD, HD), HD)
+
+    copies = []
+    for source, target in (
+        (cross_ref, cross_rows),
+        (key_ref, key_rows),
+        (value_ref, value_rows),
+        (query_ref, query_rows),
+    ):
+        copies.append(pltpu.make_async_copy(source, target, semaphores.at[len(copies)]))
+    for target, head in ((near_ref, sides[0]), (across_ref, sides[1]), (beside_ref, sides[1])):
+        for slot, source in enumerate((vision_key_ref, vision_value_ref)):
+            copies.append(
+                pltpu.make_async_copy(
+                    source.at[:, head_columns(head)],
+                    target.at[pl.ds(slot * vision, vision), :],
+                    semaphores.at[len(copies)],
+                )
+            )
+    for copy in copies:
+        copy.start()
+    cosine = jnp.concatenate([cosine_ref[...]] * 2, axis=1)
+    sine = jnp.concatenate([-sine_ref[...], sine_ref[...]], axis=1)
 
     def turned(block):
         block = block.astype(jnp.float32)
         return (block * cosine + pltpu.roll(block, HD // 2, 1) * sine).astype(jnp.bfloat16)
 
-    def head_columns(head):
-        return pl.ds(pl.multiple_of(head * HD, HD), HD)
-
-    for side, target in enumerate((keep_ref, other_ref)):
-        head = place if side == 0 else 1 - place
-        target[:, :group] = cross_ref[:, pl.ds(pl.multiple_of(head * group, group), group)]
-        target[:, group : group + HD] = range_ref[...]
-        target[:, group + HD : group + 2 * HD] = turned(key_ref[:, head_columns(head)])
-        target[:, group + 2 * HD : group + 3 * HD] = value_ref[:, head_columns(head)]
-        begin = group + 3 * HD
-        for item in range(group // HD):
-            target[:, begin + item * HD : begin + (item + 1) * HD] = turned(
-                query_ref[:, head_columns(head * (group // HD) + item)]
+    lane = lax.broadcasted_iota(jnp.int32, (TBLOCK, HD), 1)
+    ranges = jnp.zeros((TBLOCK, HD), jnp.int32)
+    for item in range(2 * rows // TBLOCK):
+        ranges = jnp.where(lane == item, range_ref[item], ranges)
+    ranges = ranges.astype(jnp.float32).astype(jnp.bfloat16)
+    stacked = heads * rows
+
+    def stack(target, begin, head, block):
+        for step in range(rows // TBLOCK):
+            row = begin + (step * heads + head) * TBLOCK
+            target[row : row + TBLOCK, :] = block[step * TBLOCK : (step + 1) * TBLOCK]
+
+    for copy in copies[:4]:
+        copy.wait()
+    for side, target in enumerate((own_ref, other_ref)):
+        for head in range(heads):
+            stack(target, 0, head, cross_rows[:, head_columns(sides[side] * heads + head)])
+        target[stacked : stacked + rows, :] = turned(key_rows[:, head_columns(sides[side])])
+        target[stacked + rows : stacked + 2 * rows, :] = value_rows[:, head_columns(sides[side])]
+        target[stacked + 2 * rows :, :] = ranges
+    for side, (target, begin) in enumerate(((own_self_ref, 0), (beside_ref, 2 * vision))):
+        for head in range(heads):
+            stack(
+                target,
+                begin,
+                head,
+                turned(query_rows[:, head_columns(sides[side] * heads + head)]),
             )
-
-
-def pack_queries(query_self, key_self, value_self, query_cross, cosine, sine, ranges, inner):
-    rows, columns = query_self.shape
-    shape = jax.ShapeDtypeStruct((rows, 2 * (columns // inner) + 3 * HD), jnp.bfloat16)
+    near_ref[2 * vision :, :] = own_ref[stacked : stacked + 2 * rows, :]
+    across_ref[2 * vision :, :] = other_ref[stacked : stacked + 2 * rows, :]
+    for copy in copies[4:]:
+        copy.wait()
+
+
+def prepare(ranges, cosine, sine, vision_keys, vision_values, cross, query, key, value, inner):
+    rows, columns = query.shape
+    stacked = rows * (columns // inner // HD)
+    vision = vision_keys.shape[0]
+    counts = [2 * vision + 2 * rows] * 2 + [2 * vision + stacked]
+    counts += [stacked + 2 * rows + TBLOCK] * 2 + [stacked]
     return pl.pallas_call(
-        functools.partial(pack_queries_kernel, inner),
-        out_shape=(shape, shape),
-        in_specs=whole(7),
-        out_specs=whole(2),
-        name="rotate_and_pack",
-    )(query_self, key_self, value_self, query_cross, cosine, sine, ranges)
-
-
-def stack_heads(source_ref, row, column, heads, target_ref):
-    for block in range(target_ref.shape[0] // (heads * TBLOCK)):
-        for head in range(heads):
-            begin = (block * heads + head) * TBLOCK
-            target_ref[begin : begin + TBLOCK, :] = source_ref[
-                row + block * TBLOCK : row + (block + 1) * TBLOCK,
-                column + head * HD : column + (head + 1) * HD,
-            ]
+        functools.partial(prepare_kernel, inner),
+        out_shape=[jax.ShapeDtypeStruct((count, HD), jnp.bfloat16) for count in counts],
+        in_specs=[pl.BlockSpec(memory_space=pltpu.SMEM)]
+        + whole(2)
+        + [pl.BlockSpec(memory_space=pltpu.HBM)] * 6,
+        out_specs=whole(6),
+        scratch_shapes=[
+            pltpu.VMEM(cross.shape, jnp.bfloat16),
+            pltpu.VMEM(query.shape, jnp.bfloat16),
+            pltpu.VMEM(key.shape, jnp.bfloat16),
+            pltpu.VMEM(value.shape, jnp.bfloat16),
+            pltpu.SemaphoreType.DMA((10,)),
+        ],
+        compiler_params=pltpu.CompilerParams(vmem_limit_bytes=60 * 2**20),
+        name="prepare_packets",
+    )(ranges.reshape(-1), cosine, sine, vision_keys, vision_values, cross, query, key, value)
 
 
 def fold_keys(keys, values_turned, stacked_ref, peak_ref, total_ref, visible):
@@ -331,20 +368,29 @@
     )
 
 
-def cross_kernel(inner, heads, groups, packed, table_ref, *refs):
-    query_count = 1 + max(argument for _, argument, _ in groups)
-    query_refs, frame_refs = refs[:query_count], refs[query_count : query_count + 4]
-    out_refs, scratch = refs[query_count + 4 : -4], refs[-4:]
-    turned_ref, stacked_ref, peak_ref, total_ref = scratch
+def cross_kernel(inner, heads, columns, groups, chosen, resumed, finish, table_ref, *refs):
+    refs = list(refs)
+    query_refs = [refs.pop(0) for _ in groups]
+    frame_refs = [refs.pop(0) for _ in chosen]
+    state_refs = [refs.pop(0) for _ in range(2)] if resumed else None
+    out_refs, (turned_ref, peaks_ref, totals_ref) = refs[:-3], refs[-3:]
     lanes = heads * TBLOCK
-    blocks = stacked_ref.shape[0] // lanes
+    blocks = columns // lanes
     frames = frame_numbers(inner)
-    for index in range(4):
-        turn_values(frame_refs[index][1], turned_ref.at[index])
-    for slot, (number, argument, row) in enumerate(groups):
-        stack_heads(query_refs[argument], row, 0, heads, stacked_ref)
-        clear(peak_ref, total_ref)
-        for index in range(4):
+    vision = turned_ref.shape[2]
+    for slot in range(len(chosen)):
+        turn_values(frame_refs[slot][vision : 2 * vision, :], turned_ref.at[slot])
+    for turn, number in enumerate(groups):
+        if finish == "state":
+            peak_ref, total_ref = out_refs[0].at[turn], out_refs[1].at[turn]
+        else:
+            peak_ref, total_ref = peaks_ref, totals_ref
+        if resumed:
+            peak_ref[...] = state_refs[0][number]
+            total_ref[...] = state_refs[1][number]
+        else:
+            clear(peak_ref, total_ref)
+        for slot, index in enumerate(chosen):
             flags = []
             for block in range(blocks):
                 at = 2 * (number * blocks + block)
@@ -359,109 +405,102 @@
                     [jnp.full((1, lanes), flag, jnp.int32) for flag in flags], axis=1
                 )
                 fold_keys(
-                    frame_refs[index][0],
-                    turned_ref[index],
-                    stacked_ref,
+                    frame_refs[slot][:vision, :],
+                    turned_ref[slot],
+                    query_refs[turn].at[:columns, :],
                     peak_ref,
                     total_ref,
                     visible > 0,
                 )
 
+        if finish == "state":
+            continue
         mixed, log_sum = finish_columns(peak_ref, total_ref)
         for block in range(blocks):
             span = slice(block * lanes, (block + 1) * lanes)
             part, stat = mixed[:, span], log_sum[:, span]
-            if packed:
+            if finish == "packed":
                 high = stat.astype(jnp.bfloat16)
                 rest = stat - high.astype(jnp.float32)
                 middle = rest.astype(jnp.bfloat16)
                 low = (rest - middle.astype(jnp.float32)).astype(jnp.bfloat16)
                 rows = [high, middle, low, jnp.zeros((stat_rows - 3, lanes), jnp.bfloat16)]
-                out_refs[0][slot * blocks + block, :HD, :] = part.astype(jnp.bfloat16)
-                out_refs[0][slot * blocks + block, HD:, :] = jnp.concatenate(rows, axis=0)
+                out_refs[0][turn * blocks + block, :HD, :] = part.astype(jnp.bfloat16)
+                out_refs[0][turn * blocks + block, HD:, :] = jnp.concatenate(rows, axis=0)
             else:
-                out_refs[0][slot * blocks + block] = part
-                out_refs[1][slot * blocks + block] = jnp.broadcast_to(stat, (8, lanes))
-
-
-def cross_part(table, queries, frames, groups, rows, inner, heads, packed):
+                out_refs[0][turn * blocks + block] = part
+                out_refs[1][turn * blocks + block] = jnp.broadcast_to(stat, (8, lanes))
+
+
+def cross_part(table, queries, frames, chosen, groups, state, finish, rows, inner, heads):
     lanes = heads * TBLOCK
+    columns = rows * heads
+    vision = FRAME_LEN
     count = len(groups) * (rows // TBLOCK)
-    if packed:
+    if finish == "state":
+        out_shape = (
+            jax.ShapeDtypeStruct((len(groups), 8, columns), jnp.float32),
+            jax.ShapeDtypeStruct((len(groups), HD + stat_rows, columns), jnp.float32),
+        )
+    elif finish == "packed":
         out_shape = (jax.ShapeDtypeStruct((count, HD + stat_rows, lanes), jnp.bfloat16),)
     else:
         out_shape = (
             jax.ShapeDtypeStruct((count, HD, lanes), jnp.float32),
             jax.ShapeDtypeStruct((count, 8, lanes), jnp.float32),
         )
+    arguments = [*(queries[number] for number in groups), *(frames[index] for index in chosen), *state]
     return pl.pallas_call(
-        functools.partial(cross_kernel, inner, heads, groups, packed),
+        functools.partial(
+            cross_kernel, inner, heads, columns, groups, chosen, len(state) > 0, finish
+        ),
         out_shape=out_shape,
-        in_specs=[pl.BlockSpec(memory_space=pltpu.SMEM)] + whole(len(queries) + 4),
+        in_specs=[pl.BlockSpec(memory_space=pltpu.SMEM)] + whole(len(arguments)),
         out_specs=whole(len(out_shape)),
         scratch_shapes=[
-            pltpu.VMEM((4, HD + stat_rows, frames[0].shape[1]), jnp.bfloat16),
-            pltpu.VMEM((rows * heads, HD), jnp.bfloat16),
-            pltpu.VMEM((8, rows * heads), jnp.float32),
-            pltpu.VMEM((HD + stat_rows, rows * heads), jnp.float32),
+            pltpu.VMEM((len(chosen), HD + stat_rows, vision), jnp.bfloat16),
+            pltpu.VMEM((8, columns), jnp.float32),
+            pltpu.VMEM((HD + stat_rows, columns), jnp.float32),
         ],
-        compiler_params=pltpu.CompilerParams(vmem_limit_bytes=40 * 2**20),
-        name="cross_return" if packed else "cross_own",
-    )(table, *queries, *frames)
-
-
-def self_kernel(
-    inner, heads, own_ref, partner_ref, far_ref, across_ref, near_ref, last_ref, out_ref, *scratch
-):
-    key_ref, turned_ref, stacked_ref, peak_ref, total_ref = scratch
+        compiler_params=pltpu.CompilerParams(vmem_limit_bytes=24 * 2**20),
+        name="cross_" + finish,
+    )(table, *arguments)
+
+
+def self_kernel(inner, heads, rows, own_ref, beside_ref, *refs):
+    key_value_refs, out_ref = refs[:7], refs[7]
+    key_ref, value_ref, turned_ref, peak_ref, total_ref = refs[8:]
     device = lax.axis_index("ctx")
     plane, place = device // inner, lax.rem(device, inner)
-    rows = own_ref.shape[0]
     lanes = heads * TBLOCK
-    group = heads * HD
-    first = group + HD
-    key_ref[:rows, :] = own_ref[:, first : first + HD]
-    key_ref[rows : 2 * rows, :] = partner_ref[:, first : first + HD]
-    key_ref[2 * rows : 4 * rows, :] = near_ref[:, :HD]
-    key_ref[4 * rows : 5 * rows, :] = far_ref[:, first : first + HD]
-    key_ref[5 * rows : 6 * rows, :] = across_ref[:, first : first + HD]
-    key_ref[6 * rows :, :] = last_ref[:, :HD]
-    values = jnp.concatenate(
-        [
-            own_ref[:, first + HD : first + 2 * HD],
-            partner_ref[:, first + HD : first + 2 * HD],
-            near_ref[:, HD:],
-            far_ref[:, first + HD : first + 2 * HD],
-            across_ref[:, first + HD : first + 2 * HD],
-            last_ref[:, HD:],
-        ],
-        axis=0,
-    )
-    turn_values(values, turned_ref)
-    keys = key_ref[...]
-    planes = (
-        plane,
-        plane + 1 - 2 * lax.rem(plane, 2),
-        lax.rem(plane + 2, 4),
-        3 - plane,
-    )
+    columns = rows * heads
+    vision = beside_ref.shape[0] - columns
+    tails = [(ref, ref.shape[0] - TBLOCK - 2 * rows) for ref in key_value_refs[:2]]
+    tails += [(ref, ref.shape[0] - 2 * rows) for ref in key_value_refs[2:4]]
+    tails += [(ref, ref.shape[0] - TBLOCK - 2 * rows) for ref in key_value_refs[4:6]]
+    tails += [(key_value_refs[6], 0), (key_value_refs[6], 2 * rows)]
+    for slot, (ref, begin) in enumerate(tails):
+        span = slice(slot * rows, (slot + 1) * rows)
+        key_ref[span, :] = ref[begin : begin + rows, :]
+        value_ref[span, :] = ref[begin + rows : begin + 2 * rows, :]
+    turn_values(value_ref[...], turned_ref)
+    planes = (plane, plane + 1 - 2 * lax.rem(plane, 2), lax.rem(plane + 2, 4), 3 - plane)
     starts = []
     for source in planes:
         starts.append((source * inner + place) * rows)
         starts.append((source * inner + 1 - place) * rows)
-    down = lax.broadcasted_iota(jnp.int32, (rows, rows * heads), 0)
+    down = lax.broadcasted_iota(jnp.int32, (rows, columns), 0)
     key_index = jnp.concatenate([down + start for start in starts], axis=0)
     across = lax.broadcasted_iota(jnp.int32, key_index.shape, 1)
     token = (across // lanes) * TBLOCK + lax.rem(across, TBLOCK)
-    for slot, query_ref in enumerate((own_ref, partner_ref)):
+    queries = (own_ref, beside_ref.at[pl.ds(vision, columns), :])
+    for slot, query_ref in enumerate(queries):
         side = place if slot == 0 else 1 - place
-        stack_heads(query_ref, 0, group + 3 * HD, heads, stacked_ref)
         clear(peak_ref, total_ref)
         visible = key_index <= token + (plane * inner + side) * rows
-        fold_keys(keys, turned_ref[...], stacked_ref, peak_ref, total_ref, visible)
+        fold_keys(key_ref[...], turned_ref[...], query_ref, peak_ref, total_ref, visible)
         mixed, _ = finish_columns(peak_ref, total_ref)
-        blocks = rows // TBLOCK
-        for block in range(blocks):
+        for block in range(rows // TBLOCK):
             part = mixed[:, block * lanes : (block + 1) * lanes].T.astype(jnp.bfloat16)
             for head in range(heads):
                 out_ref[block * inner + side, :, head * HD : (head + 1) * HD] = part[
@@ -469,28 +508,26 @@
                 ]
 
 
-def self_part(own, partner, far, far_across, near, last, inner, heads):
-    rows = own.shape[0]
+def self_part(own, beside, key_values, rows, inner, heads):
     return pl.pallas_call(
-        functools.partial(self_kernel, inner, heads),
+        functools.partial(self_kernel, inner, heads, rows),
         out_shape=jax.ShapeDtypeStruct((inner * rows // TBLOCK, TBLOCK, heads * HD), jnp.bfloat16),
-        in_specs=whole(6),
+        in_specs=whole(2 + len(key_values)),
         out_specs=whole(1)[0],
         scratch_shapes=[
             pltpu.VMEM((8 * rows, HD), jnp.bfloat16),
+            pltpu.VMEM((8 * rows, HD), jnp.bfloat16),
             pltpu.VMEM((HD + stat_rows, 8 * rows), jnp.bfloat16),
-            pltpu.VMEM((rows * heads, HD), jnp.bfloat16),
             pltpu.VMEM((8, rows * heads), jnp.float32),
             pltpu.VMEM((HD + stat_rows, rows * heads), jnp.float32),
         ],
-        compiler_params=pltpu.CompilerParams(vmem_limit_bytes=40 * 2**20),
+        compiler_params=pltpu.CompilerParams(vmem_limit_bytes=24 * 2**20),
         name="self_attention",
-    )(own, partner, far, far_across, near, last)
-
-
-def combine_kernel(inner, heads, gate_ref, mixed_ref, stat_ref, returned_ref, self_ref, out_ref):
+    )(own, beside, *key_values)
+
+
+def combine_kernel(inner, heads, gate_ref, mixed_ref, stat_ref, returned_ref, out_ref):
     count = mixed_ref.shape[0]
-    group = heads * HD
     side = count // inner
     place = lax.rem(lax.axis_index("ctx"), inner)
     gate = jnp.tanh(jnp.full((1, heads * TBLOCK), gate_ref[0], jnp.float32))
@@ -511,36 +548,34 @@
             out_ref[target, :, head * HD : (head + 1) * HD] = part[
                 head * TBLOCK : (head + 1) * TBLOCK
             ]
-    out_ref[:, :, group:] = self_ref[...]
-
-
-def combine(gate_scale, mixed, stat, returned, self_rows, inner, heads):
+
+
+def combine(gate_scale, mixed, stat, returned, inner, heads):
     count = mixed.shape[0]
     return pl.pallas_call(
         functools.partial(combine_kernel, inner, heads),
-        out_shape=jax.ShapeDtypeStruct((count, TBLOCK, 2 * heads * HD), jnp.bfloat16),
-        in_specs=[pl.BlockSpec(memory_space=pltpu.SMEM)] + whole(4),
+        out_shape=jax.ShapeDtypeStruct((count, TBLOCK, heads * HD), jnp.bfloat16),
+        in_specs=[pl.BlockSpec(memory_space=pltpu.SMEM)] + whole(3),
         out_specs=whole(1)[0],
+        compiler_params=pltpu.CompilerParams(vmem_limit_bytes=16 * 2**20),
         name="combine_planes",
-    )(gate_scale, mixed, stat, returned, self_rows)
-
-
-def spread_kernel(in_ref, self_ref, cross_ref):
-    group = in_ref.shape[2] // 2
+    )(gate_scale, mixed, stat, returned)
+
+
+def spread_kernel(in_ref, out_ref):
+    group = in_ref.shape[2]
     for head in range(in_ref.shape[0]):
-        span = slice(head * group, (head + 1) * group)
-        cross_ref[:, span] = in_ref[head, :, :group]
-        self_ref[:, span] = in_ref[head, :, group:]
+        out_ref[:, head * group : (head + 1) * group] = in_ref[head]
 
 
 def spread(inward):
     count, rows, columns = inward.shape
-    shape = jax.ShapeDtypeStruct((rows, count * columns // 2), inward.dtype)
     return pl.pallas_call(
         spread_kernel,
-        out_shape=(shape, shape),
+        out_shape=jax.ShapeDtypeStruct((rows, count * columns), inward.dtype),
         in_specs=whole(1),
-        out_specs=whole(2),
+        out_specs=whole(1)[0],
+        compiler_params=pltpu.CompilerParams(vmem_limit_bytes=16 * 2**20),
         name="spread_heads",
     )(inward)
 
@@ -577,49 +612,47 @@
                 pairs.append((device, target * inner + (place ^ flip)))
         return lax.ppermute(values, "ctx", pairs)
 
-    kept_vision, other_vision = split_heads(key_vision, value_vision, inner)
-    vision_across = send(other_vision, 1, 1)
-    vision_near = send(kept_vision, 1, 0)
-    vision_beside = send(other_vision, 0, 1)
-
     exponents = jnp.arange(HD // 2, dtype=jnp.float32) * (2.0 / HD)
     frequency = jnp.power(rope_base, -exponents)
     angles = positions.astype(jnp.float32)[:, None] * frequency[None, :]
-    cosine, sine = jnp.cos(angles), jnp.sin(angles)
-    ranges = jnp.repeat(media_range.astype(jnp.bfloat16), TBLOCK, axis=0)
-    ranges = jnp.pad(ranges, ((0, 0), (0, HD - media_range.shape[1])))
-    kept, other = pack_queries(
+    near_out, across_out, beside_out, own, other, own_self = prepare(
+        media_range,
+        jnp.cos(angles),
+        jnp.sin(angles),
+        key_vision,
+        value_vision,
+        query_cross,
         query_self,
         key_self,
         value_self,
-        query_cross,
-        jnp.concatenate([cosine, cosine], axis=1),
-        jnp.concatenate([-sine, sine], axis=1),
-        ranges,
         inner,
     )
     partner = send(other, 0, 1)
-    first = group + HD
-    last = first + 2 * HD
-    far = send(kept[:, :last], 2, 0)
-    far_across = send(other[:, :last], 2, 1)
-    sides = (kept, partner)
-    packet = jnp.concatenate([side[:, first:last] for side in sides], axis=0)
-    near_self = send(packet, 1, 0, upward=True)
-    last_self = send(packet, 3, 0, upward=True)
-
-    table = [side[::TBLOCK, group : group + 2] for side in (kept, partner, far, far_across)]
-    table = jnp.concatenate(table).astype(jnp.int32).reshape(-1)
-    frames = (kept_vision, vision_beside, vision_near, vision_across)
-    (outgoing,) = cross_part(
-        table, (far, far_across), frames, ((2, 0, 0), (3, 1, 0)), rows, inner, heads, True
-    )
+    far = send(own, 2, 0)
+    near = send(near_out, 1, 0)
+    beside_out, across_out, partner = lax.optimization_barrier((beside_out, across_out, partner))
+    far_across = send(partner, 2, 0)
+    across = send(across_out, 1, 1)
+    beside = send(beside_out, 0, 1)
+    tail = slice(rows * heads, rows * heads + 2 * rows)
+    last = send(jnp.concatenate([far[tail], far_across[tail]], axis=0), 1, 0)
+
+    queries = (own, partner, far, far_across)
+    table = [values[-TBLOCK, : 2 * (rows // TBLOCK)] for values in queries]
+    table = jnp.concatenate(table).astype(jnp.int32)
+    frames = (near_out, beside, near, across)
+    sizes = (rows, inner, heads)
+    everyone = (0, 1, 2, 3)
+    state = cross_part(table, queries, frames, (0, 2), everyone, (), "state", *sizes)
+    state = cross_part(table, queries, frames, (3,), everyone, state, "state", *sizes)
+    state, last = lax.optimization_barrier((state, last))
+    (outgoing,) = cross_part(table, queries, frames, (1,), (2, 3), state, "packed", *sizes)
     returned = send(outgoing, 2, 0)
-    mixed, stat = cross_part(
-        table, (kept, partner), frames, ((0, 0, 0), (1, 1, 0)), rows, inner, heads, False
-    )
-    self_rows = self_part(kept, partner, far, far_across, near_self, last_self, inner, heads)
-    outward = combine(gate_scale, mixed, stat, returned, self_rows, inner, heads)
+    outgoing, table, own_self = lax.optimization_barrier((outgoing, table, own_self))
+    mixed, stat = cross_part(table, queries, frames, (1,), (0, 1), state, "own", *sizes)
+    self_rows = self_part(
+        own_self, beside, (own, partner, near, across, far, far_across, last), *sizes
+    )
     planes = [
         [
             (plane * inner + place) * columns + column
@@ -628,15 +661,21 @@
         ]
         for plane in range(plane_count)
     ]
-    inward = lax.all_to_all(
-        outward.reshape(-1, 2 * group),
-        ("ctx", "head"),
-        0,
-        0,
-        axis_index_groups=planes,
-        tiled=True,
-    )
-    return spread(inward.reshape(outward.shape))
+
+    def exchange(outward):
+        inward = lax.all_to_all(
+            outward.reshape(-1, outward.shape[2]),
+            ("ctx", "head"),
+            0,
+            0,
+            axis_index_groups=planes,
+            tiled=True,
+        )
+        return spread(inward.reshape(outward.shape))
+
+    self_context = exchange(self_rows)
+    cross_context = exchange(combine(gate_scale, mixed, stat, returned, inner, heads))
+    return self_context, cross_context
 
 
 def on_device(axes, *arguments):

time: 95 us -> 74.3 us (0.78)
  the two profiles are of different devices: /device:TPU:9 before, /device:TPU:0 now
where the time goes in v2:
time: 74.3 us; the launch traced here: 73.5 us
  waiting for transfers between devices  26 us (35%)
  starting transfers between devices  22 us (30%)
  Pallas kernels  18.5 us (25%)
  local copies, waits for them, and re-layouts  4.05 us (5%)
  other arithmetic  1.58 us (2%)
  between operations  1.4 us (2%)
    ppermute x8, waiting for transfers between devices, send(): return lax.ppermute(values, 'ctx', pairs)  20.8 us
    ppermute x8, starting transfers between devices, send(): return lax.ppermute(values, 'ctx', pairs)  15.2 us
    pallas_call x4, Pallas kernels, cross_part(): pl.pallas_call(functools.partial(cross_kernel, inner, heads, columns, gro...  10.5 us
    all_to_all x2, starting transfers between devices, exchange(): lax.all_to_all(outward.reshape(-1, outward.shape[2]), ('ctx', 'head'), 0,...  6.82 us
    all_to_all x2, waiting for transfers between devices, exchange(): lax.all_to_all(outward.reshape(-1, outward.shape[2]), ('ctx', 'head'), 0,...  5.23 us
    pallas_call x1, Pallas kernels, prepare(): pl.pallas_call(functools.partial(prepare_kernel, inner), out_shape=[jax.S...  3.65 us
    unnamed x9, local copies, waits for them, and re-layouts  2.73 us
    pallas_call x1, Pallas kernels, self_part(): pl.pallas_call(functools.partial(self_kernel, inner, heads, rows), out_sh...  2.02 us
  transfers between devices with their start and end apart: 10, of which 5 were waited for; matrix products, arithmetic and copies ran while one was open for 1% of the time, Pallas kernels for 15%

profile of v2, /device:TPU:0, one launch (start us, length us, event | category | flops | bytes accessed | tf_op | source)
XLA Modules:
  0.0 73.5 jit_solution(12900756015579746822)
XLA Ops:
  0.6 0.8 %copy.12 = s32[4,2]{1,0:T(4,128)S(1)} copy(s32[4,2]{0,1:T(2,128)} %param.16) | data formatting | bytes 64 | tf_op args[7]
  1.4 0.6 reshape.26.range_ref
  2.0 0.7 convert_element_type.6
  2.7 0.8 %multiply_sine_fusion = (f32[64,64]{1,0:T(8,128)}, f32[64,64]{1,0:T(8,128)}) fusion(f32[64]{0:T(128)S(1)} %negate_power_fusion, f32[64]{0:T(128)S(1)} %convert_element_type.6), kind=kLoop, calls=%fused_computation.1 | loop fusion | flops 4096 | bytes 33280 | tf_op jit(solution)/shard_map/sin | solution.py:621
  3.5 3.7 %prepare_packets.1 = (bf16[1920,128]{1,0:T(8,128)(2,1)}, bf16[1920,128]{1,0:T(8,128)(2,1)}, bf16[2304,128]{1,0:T(8,128)(2,1)}, bf16[656,128]{1,0:T(8,128)(2,1)},...) custom-call(s32[8]{0:T(128)} %reshape.26.range_ref, f32[64,64]{1,0:T(8,128)} %get-tuple-element.43.cosine_ref, ...), custom_call_target="tpu_custom_call" | custom-call | tf_op jit(solution)/shard_map/prepare_packets/pallas_call | solution.py:295
  7.2 0.0 copy-start.1
  7.2 3.0 %collective-permute-start = (bf16[656,128]{1,0:T(8,128)(2,1)}, bf16[656,128]{1,0:T(8,128)(2,1)S(1)}, u32[]{:S(2)}, u32[]{:S(2)}) collective-permute-start(bf16[656,128]{1,0:T(8,128)(2,1)} %get-tuple-element.25), channel_id=1, source_target_pairs={{0,4},{4,0},{8,12},{12,8},{16,20},{20,16},{24,28},{28,24},{1,5},{5... | collective-permute-start | bytes 503816 | tf_op jit(solution)/shard_map/ppermute | solution.py:613
  10.2 2.6 %collective-permute-start.1 = (bf16[656,128]{1,0:T(8,128)(2,1)}, bf16[656,128]{1,0:T(8,128)(2,1)S(1)}, u32[]{:S(2)}, u32[]{:S(2)}) collective-permute-start(bf16[656,128]{1,0:T(8,128)(2,1)} %get-tuple-element.22.refs_0_), channel_id=1, source_target_pairs={{0,16},{4,20},{8,24},{12,28},{16,0},{20,4},{24,8},{28,12},{1,17},{... | collective-permute-start | bytes 503816 | tf_op jit(solution)/shard_map/ppermute | solution.py:613
  12.8 1.6 %collective-permute-start.5 = (bf16[1920,128]{1,0:T(8,128)(2,1)}, bf16[1920,128]{1,0:T(8,128)(2,1)S(1)}, u32[]{:S(2)}, u32[]{:S(2)}) collective-permute-start(bf16[1920,128]{1,0:T(8,128)(2,1)} %get-tuple-element.29.refs_4_), channel_id=1, source_target_pairs={{0,8},{4,12},{8,0},{12,4},{16,24},{20,28},{24,16},{28,20},{1,9},{5... | collective-permute-start | bytes 1474568 | tf_op jit(solution)/shard_map/ppermute | solution.py:613
  14.4 0.7 slice_bitcast_fusion.3
  15.1 0.0 collective-permute-done.refs_1_
  15.1 2.5 %collective-permute-start.2 = (bf16[656,128]{1,0:T(8,128)(2,1)S(1)}, bf16[656,128]{1,0:T(8,128)(2,1)S(1)}, u32[]{:S(2)}, u32[]{:S(2)}) collective-permute-start(bf16[656,128]{1,0:T(8,128)(2,1)S(1)} %collective-permute-done.refs_1_), channel_id=1, source_target_pairs={{0,16},{4,20},{8,24},{12,28},{16,0},{20,4},{24,8},{28,12},{1,17},{... | collective-permute-start | bytes 503816 | tf_op jit(solution)/shard_map/ppermute | solution.py:613
  17.5 1.5 %collective-permute-start.3 = (bf16[2304,128]{1,0:T(8,128)(2,1)}, bf16[2304,128]{1,0:T(8,128)(2,1)S(1)}, u32[]{:S(2)}, u32[]{:S(2)}) collective-permute-start(bf16[2304,128]{1,0:T(8,128)(2,1)} %get-tuple-element.27), channel_id=1, source_target_pairs={{0,4},{4,0},{8,12},{12,8},{16,20},{20,16},{24,28},{28,24},{1,5},{5... | collective-permute-start | bytes 1769480 | tf_op jit(solution)/shard_map/ppermute | solution.py:613
  19.0 1.5 %collective-permute-start.4 = (bf16[1920,128]{1,0:T(8,128)(2,1)}, bf16[1920,128]{1,0:T(8,128)(2,1)S(1)}, u32[]{:S(2)}, u32[]{:S(2)}) collective-permute-start(bf16[1920,128]{1,0:T(8,128)(2,1)} %get-tuple-element.28), channel_id=1, source_target_pairs={{0,12},{4,8},{8,4},{12,0},{16,28},{20,24},{24,20},{28,16},{1,13},{... | collective-permute-start | bytes 1474568 | tf_op jit(solution)/shard_map/ppermute | solution.py:613
  20.6 1.4 %collective-permute-done.1.refs_2_.refs_0_.refs_4_ = bf16[656,128]{1,0:T(8,128)(2,1)S(1)} collective-permute-done((bf16[656,128]{1,0:T(8,128)(2,1)}, bf16[656,128]{1,0:T(8,128)(2,1)S(1)}, u32[]{:S(2)}, u32[]{:S(2)}) %collective-permute-start.1) | collective-permute-done | bytes 167968 | tf_op jit(solution)/shard_map/ppermute | solution.py:613
  21.9 10.0 %collective-permute-done.2.refs_3_.refs_1_.refs_5_ = bf16[656,128]{1,0:T(8,128)(2,1)S(1)} collective-permute-done((bf16[656,128]{1,0:T(8,128)(2,1)S(1)}, bf16[656,128]{1,0:T(8,128)(2,1)S(1)}, u32[]{:S(2)}, u32[]{:S(2)}) %collective-permute-start.2) | collective-permute-done | bytes 167968 | tf_op jit(solution)/shard_map/ppermute | solution.py:613
  31.9 2.4 %collective-permute-start.6 = (bf16[256,128]{1,0:T(8,128)(2,1)S(1)}, bf16[256,128]{1,0:T(8,128)(2,1)S(1)}, u32[]{:S(2)}, u32[]{:S(2)}) collective-permute-start(bf16[256,128]{1,0:T(8,128)(2,1)S(1)} %pad_maximum_fusion), channel_id=1, source_target_pairs={{0,8},{4,12},{8,0},{12,4},{16,24},{20,28},{24,16},{28,20},{1,9},{5... | collective-permute-start | bytes 196616 | tf_op jit(solution)/shard_map/ppermute | solution.py:613
  34.3 0.1 maximum_convert_fusion.table_ref
  34.4 0.0 collective-permute-done.5.refs_5_.refs_2_
  34.4 0.0 copy-start
  34.4 0.9 %copy-done = bf16[656,128]{1,0:T(8,128)(2,1)S(1)} copy-done((bf16[656,128]{1,0:T(8,128)(2,1)S(1)}, bf16[656,128]{1,0:T(8,128)(2,1)}, u32[]{:S(2)}) %copy-start) | copy-done | bytes 167960
  35.3 0.0 copy-start.2
  35.3 1.0 %copy-done.2 = bf16[1920,128]{1,0:T(8,128)(2,1)S(1)} copy-done((bf16[1920,128]{1,0:T(8,128)(2,1)S(1)}, bf16[1920,128]{1,0:T(8,128)(2,1)}, u32[]{:S(2)}) %copy-start.2) | copy-done | bytes 491544
  36.4 4.0 %cross_state.2 = (f32[4,8,512]{2,1,0:T(8,128)S(1)}, f32[4,144,512]{2,1,0:T(8,128)S(1)}) custom-call(s32[32]{0:T(128)S(1)} %maximum_convert_fusion.table_ref, bf16[656,128]{1,0:T(8,128)(2,1)S(1)} %copy-done, bf16[656,128]{1,0:T(8,128)(2,1)S(1)} %collective-permute-done.refs_1_, bf16[656,128]{1,0:T(8,128)(2,1)S(1)} %collective-permute-done.1.refs_2_.refs_0_.refs_4_, ...), custom_call_target="tpu_custom_call" | custom-call | tf_op jit(solution)/shard_map/cross_state/pallas_call | solution.py:453
  40.3 2.3 %collective-permute-done.4.refs_4_.refs_3_ = bf16[1920,128]{1,0:T(8,128)(2,1)S(1)} collective-permute-done((bf16[1920,128]{1,0:T(8,128)(2,1)}, bf16[1920,128]{1,0:T(8,128)(2,1)S(1)}, u32[]{:S(2)}, u32[]{:S(2)}) %collective-permute-start.4) | collective-permute-done | bytes 491552 | tf_op jit(solution)/shard_map/ppermute | solution.py:613
  42.7 0.0 copy-done.1
  42.7 2.8 %cross_state.3 = (f32[4,8,512]{2,1,0:T(8,128)S(1)}, f32[4,144,512]{2,1,0:T(8,128)S(1)}) custom-call(s32[32]{0:T(128)S(1)} %maximum_convert_fusion.table_ref, bf16[656,128]{1,0:T(8,128)(2,1)S(1)} %copy-done.1, bf16[656,128]{1,0:T(8,128)(2,1)S(1)} %collective-permute-done.refs_1_, bf16[656,128]{1,0:T(8,128)(2,1)S(1)} %collective-permute-done.1.refs_2_.refs_0_.refs_4_, ...), custom_call_target="tpu_custom_call" | custom-call | tf_op jit(solution)/shard_map/cross_state/pallas_call | solution.py:453
  45.5 0.0 collective-permute-done.6.refs_6_
  45.5 0.0 copy-start.3
  45.5 0.0 collective-permute-done.3.refs_2_.beside_ref
  45.5 3.0 %cross_packed.1 = bf16[8,144,128]{2,1,0:T(8,128)(2,1)S(1)} custom-call(s32[32]{0:T(128)S(1)} %maximum_convert_fusion.table_ref, bf16[656,128]{1,0:T(8,128)(2,1)S(1)} %collective-permute-done.1.refs_2_.refs_0_.refs_4_, bf16[656,128]{1,0:T(8,128)(2,1)S(1)} %collective-permute-done.2.refs_3_.refs_1_.refs_5_, ...), custom_call_target="tpu_custom_call" | custom-call | tf_op jit(solution)/shard_map/cross_packed/pallas_call | solution.py:453
  48.5 0.1 collective-permute-start.7
  48.6 0.0 copy-done.3
  48.6 2.0 %self_attention.1 = bf16[8,16,1024]{2,1,0:T(8,128)(2,1)} custom-call(bf16[512,128]{1,0:T(8,128)(2,1)S(1)} %copy-done.3, bf16[2304,128]{1,0:T(8,128)(2,1)S(1)} %collective-permute-done.3.refs_2_.beside_ref, bf16[656,128]{1,0:T(8,128)(2,1)S(1)} %copy-done.1, bf16[656,128]{1,0:T(8,128)(2,1)S(1)} %collective-permute-done.refs_1_, ...), custom_call_target="tpu_custom_call" | custom-call | tf_op jit(solution)/shard_map/self_attention/pallas_call | solution.py:512
  50.6 3.4 %all-to-all-start = ((bf16[8,16,1024]{2,1,0:T(8,128)(2,1)}), bf16[8,16,1024]{2,1,0:T(8,128)(2,1)S(1)}, u32[]{:S(2)}, u32[]{:S(2)}) async-start(bf16[8,16,1024]{2,1,0:T(8,128)(2,1)} %self_attention.1), calls=%async_computation | async-start | bytes 524288 | tf_op jit(solution)/shard_map/all_to_all | solution.py:666
  54.7 0.7 %cross_own.1 = (f32[8,128,128]{2,1,0:T(8,128)S(1)}, f32[8,8,128]{2,1,0:T(8,128)S(1)}) custom-call(s32[32]{0:T(128)S(1)} %maximum_convert_fusion.table_ref, bf16[656,128]{1,0:T(8,128)(2,1)S(1)} %copy-done.1, bf16[656,128]{1,0:T(8,128)(2,1)S(1)} %collective-permute-done.refs_1_, bf16[2304,128]{1,0:T(8,128)(2,1)S(1)} %collective-permute-done.3.refs_2_.beside_ref, ...), custom_call_target="tpu_custom_call" | custom-call | tf_op jit(solution)/shard_map/cross_own/pallas_call | solution.py:453
  55.5 7.1 %collective-permute-done.7.returned_ref = bf16[8,144,128]{2,1,0:T(8,128)(2,1)S(1)} collective-permute-done((bf16[8,144,128]{2,1,0:T(8,128)(2,1)S(1)}, bf16[8,144,128]{2,1,0:T(8,128)(2,1)S(1)}, u32[]{:S(2)}, u32[]{:S(2)}) %collective-permute-start.7) | collective-permute-done | bytes 294944 | tf_op jit(solution)/shard_map/ppermute | solution.py:613
  62.5 0.9 %combine_planes.1 = bf16[8,16,1024]{2,1,0:T(8,128)(2,1)} custom-call(f32[1]{0:T(128)S(6)} %copy.13.gate_ref, f32[8,128,128]{2,1,0:T(8,128)S(1)} %get-tuple-element.40.mixed_ref, f32[8,8,128]{2,1,0:T(8,128)S(1)} %get-tuple-element.41.stat_ref, bf16[8,144,128]{2,1,0:T(8,128)(2,1)S(1)} %collective-permute-done.7.returned_ref), custom_call_target="tpu_custom_call" | custom-call | tf_op jit(solution)/shard_map/combine_planes/pallas_call | solution.py:555
  63.4 0.0 all-to-all-done.in_ref
  63.4 3.4 %all-to-all-start.1 = ((bf16[8,16,1024]{2,1,0:T(8,128)(2,1)}), bf16[8,16,1024]{2,1,0:T(8,128)(2,1)S(1)}, u32[]{:S(2)}, u32[]{:S(2)}) async-start(bf16[8,16,1024]{2,1,0:T(8,128)(2,1)} %combine_planes.1), calls=%async_computation.1 | async-start | bytes 524288 | tf_op jit(solution)/shard_map/all_to_all | solution.py:666
  66.8 0.7 spread_heads.2
  67.6 5.2 %all-to-all-done.1.in_ref = bf16[8,16,1024]{2,1,0:T(8,128)(2,1)S(1)} async-done(((bf16[8,16,1024]{2,1,0:T(8,128)(2,1)}), bf16[8,16,1024]{2,1,0:T(8,128)(2,1)S(1)}, u32[]{:S(2)}, u32[]{:S(2)}) %all-to-all-start.1) | async-done | bytes 262176 | tf_op jit(solution)/shard_map/all_to_all | solution.py:666
  72.8 0.7 spread_heads.3
  (7 shorter events, 0.0 us)
Async XLA Ops:
  7.2 35.5 %copy-start.1 = (bf16[656,128]{1,0:T(8,128)(2,1)S(1)}, bf16[656,128]{1,0:T(8,128)(2,1)}, u32[]{:S(2)}) copy-start(bf16[656,128]{1,0:T(8,128)(2,1)} %get-tuple-element.22.refs_0_) | copy-start | bytes 503812
  7.2 7.9 %collective-permute-start = (bf16[656,128]{1,0:T(8,128)(2,1)}, bf16[656,128]{1,0:T(8,128)(2,1)S(1)}, u32[]{:S(2)}, u32[]{:S(2)}) collective-permute-start(bf16[656,128]{1,0:T(8,128)(2,1)} %get-tuple-element.25), channel_id=1, source_target_pairs={{0,4},{4,0},{8,12},{12,8},{16,20},{20,16},{24,28},{28,24},{1,5},{5... | collective-permute-start | bytes 503816 | tf_op jit(solution)/shard_map/ppermute | solution.py:613
  10.2 11.7 %collective-permute-start.1 = (bf16[656,128]{1,0:T(8,128)(2,1)}, bf16[656,128]{1,0:T(8,128)(2,1)S(1)}, u32[]{:S(2)}, u32[]{:S(2)}) collective-permute-start(bf16[656,128]{1,0:T(8,128)(2,1)} %get-tuple-element.22.refs_0_), channel_id=1, source_target_pairs={{0,16},{4,20},{8,24},{12,28},{16,0},{20,4},{24,8},{28,12},{1,17},{... | collective-permute-start | bytes 503816 | tf_op jit(solution)/shard_map/ppermute | solution.py:613
  12.8 21.6 %collective-permute-start.5 = (bf16[1920,128]{1,0:T(8,128)(2,1)}, bf16[1920,128]{1,0:T(8,128)(2,1)S(1)}, u32[]{:S(2)}, u32[]{:S(2)}) collective-permute-start(bf16[1920,128]{1,0:T(8,128)(2,1)} %get-tuple-element.29.refs_4_), channel_id=1, source_target_pairs={{0,8},{4,12},{8,0},{12,4},{16,24},{20,28},{24,16},{28,20},{1,9},{5... | collective-permute-start | bytes 1474568 | tf_op jit(solution)/shard_map/ppermute | solution.py:613
  15.1 16.9 %collective-permute-start.2 = (bf16[656,128]{1,0:T(8,128)(2,1)S(1)}, bf16[656,128]{1,0:T(8,128)(2,1)S(1)}, u32[]{:S(2)}, u32[]{:S(2)}) collective-permute-start(bf16[656,128]{1,0:T(8,128)(2,1)S(1)} %collective-permute-done.refs_1_), channel_id=1, source_target_pairs={{0,16},{4,20},{8,24},{12,28},{16,0},{20,4},{24,8},{28,12},{1,17},{... | collective-permute-start | bytes 503816 | tf_op jit(solution)/shard_map/ppermute | solution.py:613
  17.5 28.0 %collective-permute-start.3 = (bf16[2304,128]{1,0:T(8,128)(2,1)}, bf16[2304,128]{1,0:T(8,128)(2,1)S(1)}, u32[]{:S(2)}, u32[]{:S(2)}) collective-permute-start(bf16[2304,128]{1,0:T(8,128)(2,1)} %get-tuple-element.27), channel_id=1, source_target_pairs={{0,4},{4,0},{8,12},{12,8},{16,20},{20,16},{24,28},{28,24},{1,5},{5... | collective-permute-start | bytes 1769480 | tf_op jit(solution)/shard_map/ppermute | solution.py:613
  19.0 23.6 %collective-permute-start.4 = (bf16[1920,128]{1,0:T(8,128)(2,1)}, bf16[1920,128]{1,0:T(8,128)(2,1)S(1)}, u32[]{:S(2)}, u32[]{:S(2)}) collective-permute-start(bf16[1920,128]{1,0:T(8,128)(2,1)} %get-tuple-element.28), channel_id=1, source_target_pairs={{0,12},{4,8},{8,4},{12,0},{16,28},{20,24},{24,20},{28,16},{1,13},{... | collective-permute-start | bytes 1474568 | tf_op jit(solution)/shard_map/ppermute | solution.py:613
  31.9 13.6 %collective-permute-start.6 = (bf16[256,128]{1,0:T(8,128)(2,1)S(1)}, bf16[256,128]{1,0:T(8,128)(2,1)S(1)}, u32[]{:S(2)}, u32[]{:S(2)}) collective-permute-start(bf16[256,128]{1,0:T(8,128)(2,1)S(1)} %pad_maximum_fusion), channel_id=1, source_target_pairs={{0,8},{4,12},{8,0},{12,4},{16,24},{20,28},{24,16},{28,20},{1,9},{5... | collective-permute-start | bytes 196616 | tf_op jit(solution)/shard_map/ppermute | solution.py:613
  34.4 0.9 %copy-start = (bf16[656,128]{1,0:T(8,128)(2,1)S(1)}, bf16[656,128]{1,0:T(8,128)(2,1)}, u32[]{:S(2)}) copy-start(bf16[656,128]{1,0:T(8,128)(2,1)} %get-tuple-element.22.refs_0_) | copy-start | bytes 503812
  35.3 1.0 %copy-start.2 = (bf16[1920,128]{1,0:T(8,128)(2,1)S(1)}, bf16[1920,128]{1,0:T(8,128)(2,1)}, u32[]{:S(2)}) copy-start(bf16[1920,128]{1,0:T(8,128)(2,1)} %get-tuple-element.29.refs_4_) | copy-start | bytes 1474564
  45.5 3.1 %copy-start.3 = (bf16[512,128]{1,0:T(8,128)(2,1)S(1)}, bf16[512,128]{1,0:T(8,128)(2,1)}, u32[]{:S(2)}) copy-start(bf16[512,128]{1,0:T(8,128)(2,1)} %get-tuple-element.37.own_ref) | copy-start | bytes 393220
  48.5 14.0 %collective-permute-start.7 = (bf16[8,144,128]{2,1,0:T(8,128)(2,1)S(1)}, bf16[8,144,128]{2,1,0:T(8,128)(2,1)S(1)}, u32[]{:S(2)}, u32[]{:S(2)}) collective-permute-start(bf16[8,144,128]{2,1,0:T(8,128)(2,1)S(1)} %cross_packed.1), channel_id=1, source_target_pairs={{0,16},{4,20},{8,24},{12,28},{16,0},{20,4},{24,8},{28,12},{1,17},{... | collective-permute-start | bytes 884744 | tf_op jit(solution)/shard_map/ppermute | solution.py:613
  50.6 12.8 %all-to-all-start = ((bf16[8,16,1024]{2,1,0:T(8,128)(2,1)}), bf16[8,16,1024]{2,1,0:T(8,128)(2,1)S(1)}, u32[]{:S(2)}, u32[]{:S(2)}) async-start(bf16[8,16,1024]{2,1,0:T(8,128)(2,1)} %self_attention.1), calls=%async_computation | async-start | bytes 524288 | tf_op jit(solution)/shard_map/all_to_all | solution.py:666
  63.4 9.4 %all-to-all-start.1 = ((bf16[8,16,1024]{2,1,0:T(8,128)(2,1)}), bf16[8,16,1024]{2,1,0:T(8,128)(2,1)S(1)}, u32[]{:S(2)}, u32[]{:S(2)}) async-start(bf16[8,16,1024]{2,1,0:T(8,128)(2,1)} %combine_planes.1), calls=%async_computation.1 | async-start | bytes 524288 | tf_op jit(solution)/shard_map/all_to_all | solution.py:666

commit v3 on v2

--- a/solution.py
+++ b/solution.py
@@ -2,6 +2,7 @@
 
 import jax
 import jax.numpy as jnp
+import numpy as np
 from jax import lax
 from jax.experimental import pallas as pl
 from jax.experimental.pallas import tpu as pltpu
@@ -197,8 +198,8 @@
 def prepare_kernel(
     inner,
     range_ref,
-    cosine_ref,
-    sine_ref,
+    position_ref,
+    frequency_ref,
     vision_key_ref,
     vision_value_ref,
     cross_ref,
@@ -211,117 +212,167 @@
     own_ref,
     other_ref,
     own_self_ref,
+    position_row,
+    frequency_row,
+    vision_rows,
     cross_rows,
     query_rows,
     key_rows,
     value_rows,
-    semaphores,
+    packet_rows,
+    self_rows,
+    in_semaphores,
+    out_semaphores,
 ):
     rows = query_rows.shape[0]
     heads = query_rows.shape[1] // inner // HD
     vision = vision_key_ref.shape[0]
+    stacked = heads * rows
     place = lax.rem(lax.axis_index("ctx"), inner)
     sides = (place, 1 - place)
 
     def head_columns(head):
         return pl.ds(pl.multiple_of(head * HD, HD), HD)
 
-    copies = []
+    loads = []
     for source, target in (
+        (position_ref, position_row),
+        (frequency_ref, frequency_row),
         (cross_ref, cross_rows),
         (key_ref, key_rows),
         (value_ref, value_rows),
         (query_ref, query_rows),
     ):
-        copies.append(pltpu.make_async_copy(source, target, semaphores.at[len(copies)]))
-    for target, head in ((near_ref, sides[0]), (across_ref, sides[1]), (beside_ref, sides[1])):
+        loads.append(pltpu.make_async_copy(source, target, in_semaphores.at[len(loads)]))
+    for side in range(2):
         for slot, source in enumerate((vision_key_ref, vision_value_ref)):
-            copies.append(
+            loads.append(
                 pltpu.make_async_copy(
-                    source.at[:, head_columns(head)],
-                    target.at[pl.ds(slot * vision, vision), :],
-                    semaphores.at[len(copies)],
+                    source.at[:, head_columns(sides[side])],
+                    vision_rows.at[side, pl.ds(slot * vision, vision), :],
+                    in_semaphores.at[len(loads)],
                 )
             )
-    for copy in copies:
+    for load in loads:
+        load.start()
+
+    stores = []
+
+    def store(source, target):
+        copy = pltpu.make_async_copy(source, target, out_semaphores.at[len(stores)])
         copy.start()
-    cosine = jnp.concatenate([cosine_ref[...]] * 2, axis=1)
-    sine = jnp.concatenate([-sine_ref[...], sine_ref[...]], axis=1)
+        stores.append(copy)
+
+    def stack(target, head, block):
+        for step in range(rows // TBLOCK):
+            row = (step * heads + head) * TBLOCK
+            target[row : row + TBLOCK, :] = block[step * TBLOCK : (step + 1) * TBLOCK]
+
+    lane = lax.broadcasted_iota(jnp.int32, (TBLOCK, HD), 1)
+    ranges = jnp.zeros((TBLOCK, HD), jnp.int32)
+    for item in range(2 * rows // TBLOCK):
+        ranges = jnp.where(lane == item, range_ref[item % 2, item // 2], ranges)
+    ranges = ranges.astype(jnp.float32).astype(jnp.bfloat16)
+    for load in loads[:2]:
+        load.wait()
+    place_of_row = jnp.broadcast_to(position_row[...].astype(jnp.float32), (HD, rows)).T
+    frequency = jnp.concatenate([frequency_row[...]] * 2, axis=1)
+    angles = place_of_row * frequency
+    cosine = jnp.cos(angles)
+    column = lax.broadcasted_iota(jnp.int32, angles.shape, 1)
+    sine = jnp.sin(angles) * jnp.where(column < HD // 2, -1.0, 1.0)
 
     def turned(block):
         block = block.astype(jnp.float32)
         return (block * cosine + pltpu.roll(block, HD // 2, 1) * sine).astype(jnp.bfloat16)
 
-    lane = lax.broadcasted_iota(jnp.int32, (TBLOCK, HD), 1)
-    ranges = jnp.zeros((TBLOCK, HD), jnp.int32)
-    for item in range(2 * rows // TBLOCK):
-        ranges = jnp.where(lane == item, range_ref[item], ranges)
-    ranges = ranges.astype(jnp.float32).astype(jnp.bfloat16)
-    stacked = heads * rows
-
-    def stack(target, begin, head, block):
-        for step in range(rows // TBLOCK):
-            row = begin + (step * heads + head) * TBLOCK
-            target[row : row + TBLOCK, :] = block[step * TBLOCK : (step + 1) * TBLOCK]
-
-    for copy in copies[:4]:
-        copy.wait()
-    for side, target in enumerate((own_ref, other_ref)):
+    for load in loads[2:5]:
+        load.wait()
+    for side, target in ((1, other_ref), (0, own_ref)):
+        packet = packet_rows.at[side]
         for head in range(heads):
-            stack(target, 0, head, cross_rows[:, head_columns(sides[side] * heads + head)])
-        target[stacked : stacked + rows, :] = turned(key_rows[:, head_columns(sides[side])])
-        target[stacked + rows : stacked + 2 * rows, :] = value_rows[:, head_columns(sides[side])]
-        target[stacked + 2 * rows :, :] = ranges
-    for side, (target, begin) in enumerate(((own_self_ref, 0), (beside_ref, 2 * vision))):
+            stack(packet, head, cross_rows[:, head_columns(sides[side] * heads + head)])
+        packet[stacked : stacked + rows, :] = turned(key_rows[:, head_columns(sides[side])])
+        packet[stacked + rows : stacked + 2 * rows, :] = value_rows[:, head_columns(sides[side])]
+        packet[stacked + 2 * rows :, :] = ranges
+        store(packet, target)
+    key_value = pl.ds(stacked, 2 * rows)
+    store(packet_rows.at[0, key_value, :], near_ref.at[pl.ds(2 * vision, 2 * rows), :])
+    store(packet_rows.at[1, key_value, :], across_ref.at[pl.ds(2 * vision, 2 * rows), :])
+    for load in loads[6:8]:
+        load.wait()
+    store(vision_rows.at[0], near_ref.at[pl.ds(0, 2 * vision), :])
+    for load in loads[8:]:
+        load.wait()
+    store(vision_rows.at[1], across_ref.at[pl.ds(0, 2 * vision), :])
+    store(vision_rows.at[1], beside_ref.at[pl.ds(0, 2 * vision), :])
+    loads[5].wait()
+    for side, target in ((1, beside_ref.at[pl.ds(2 * vision, stacked), :]), (0, own_self_ref)):
         for head in range(heads):
             stack(
-                target,
-                begin,
+                self_rows.at[side],
                 head,
                 turned(query_rows[:, head_columns(sides[side] * heads + head)]),
             )
-    near_ref[2 * vision :, :] = own_ref[stacked : stacked + 2 * rows, :]
-    across_ref[2 * vision :, :] = other_ref[stacked : stacked + 2 * rows, :]
-    for copy in copies[4:]:
+        store(self_rows.at[side], target)
+    for copy in stores:
         copy.wait()
 
 
-def prepare(ranges, cosine, sine, vision_keys, vision_values, cross, query, key, value, inner):
+def prepare(ranges, positions, frequency, vision_keys, vision_values, cross, query, key, value, inner):
     rows, columns = query.shape
     stacked = rows * (columns // inner // HD)
     vision = vision_keys.shape[0]
-    counts = [2 * vision + 2 * rows] * 2 + [2 * vision + stacked]
-    counts += [stacked + 2 * rows + TBLOCK] * 2 + [stacked]
+    packet = stacked + 2 * rows + TBLOCK
+    counts = [2 * vision + 2 * rows] * 2 + [2 * vision + stacked] + [packet] * 2 + [stacked]
     return pl.pallas_call(
         functools.partial(prepare_kernel, inner),
         out_shape=[jax.ShapeDtypeStruct((count, HD), jnp.bfloat16) for count in counts],
         in_specs=[pl.BlockSpec(memory_space=pltpu.SMEM)]
-        + whole(2)
-        + [pl.BlockSpec(memory_space=pltpu.HBM)] * 6,
-        out_specs=whole(6),
+        + [pl.BlockSpec(memory_space=pl.ANY)] * 8,
+        out_specs=[pl.BlockSpec(memory_space=pl.ANY)] * 6,
         scratch_shapes=[
+            pltpu.VMEM((1, rows), jnp.int32),
+            pltpu.VMEM((1, HD // 2), jnp.float32),
+            pltpu.VMEM((2, 2 * vision, HD), jnp.bfloat16),
             pltpu.VMEM(cross.shape, jnp.bfloat16),
             pltpu.VMEM(query.shape, jnp.bfloat16),
             pltpu.VMEM(key.shape, jnp.bfloat16),
             pltpu.VMEM(value.shape, jnp.bfloat16),
+            pltpu.VMEM((2, packet, HD), jnp.bfloat16),
+            pltpu.VMEM((2, stacked, HD), jnp.bfloat16),
             pltpu.SemaphoreType.DMA((10,)),
+            pltpu.SemaphoreType.DMA((9,)),
         ],
         compiler_params=pltpu.CompilerParams(vmem_limit_bytes=60 * 2**20),
         name="prepare_packets",
-    )(ranges.reshape(-1), cosine, sine, vision_keys, vision_values, cross, query, key, value)
-
-
-def fold_keys(keys, values_turned, stacked_ref, peak_ref, total_ref, visible):
+    )(
+        jnp.transpose(ranges),
+        positions.reshape(1, rows),
+        frequency.reshape(1, HD // 2),
+        vision_keys,
+        vision_values,
+        cross,
+        query,
+        key,
+        value,
+    )
+
+
+def fold_keys(keys, values_turned, jobs):
     scale = HD**-0.5 * log2e
-    width = min(256, stacked_ref.shape[0])
-    spans = [slice(begin, begin + width) for begin in range(0, stacked_ref.shape[0], width)]
+    spans = []
+    for job in jobs:
+        width = min(256, job[0].shape[0])
+        for begin in range(0, job[0].shape[0], width):
+            spans.append((job, slice(begin, begin + width)))
     scores = [
         lax.dot_general(
             keys, stacked_ref[span, :], contract_last, preferred_element_type=jnp.float32
         )
-        for span in spans
+        for (stacked_ref, _, _, _), span in spans
     ]
-    for span, score in zip(spans, scores):
+    for ((_, peak_ref, total_ref, visible), span), score in zip(spans, scores):
         peak = peak_ref[0:1, span]
         seen = visible[:, span]
         if seen.shape[0] == 1:
@@ -368,29 +419,36 @@
     )
 
 
-def cross_kernel(inner, heads, columns, groups, chosen, resumed, finish, table_ref, *refs):
+def cross_kernel(inner, heads, columns, units, chosen, resumed, finish, table_ref, *refs):
     refs = list(refs)
-    query_refs = [refs.pop(0) for _ in groups]
+    query_refs = {number: refs.pop(0) for number, frames in units if frames}
     frame_refs = [refs.pop(0) for _ in chosen]
     state_refs = [refs.pop(0) for _ in range(2)] if resumed else None
     out_refs, (turned_ref, peaks_ref, totals_ref) = refs[:-3], refs[-3:]
+    if finish == "state":
+        peaks_ref, totals_ref = out_refs
     lanes = heads * TBLOCK
     blocks = columns // lanes
     frames = frame_numbers(inner)
     vision = turned_ref.shape[2]
-    for slot in range(len(chosen)):
+    for turn, (number, _) in enumerate(units):
+        if resumed:
+            peaks_ref[turn] = state_refs[0][number]
+            totals_ref[turn] = state_refs[1][number]
+        else:
+            clear(peaks_ref.at[turn], totals_ref.at[turn])
+
+    def job(turn, number, flags):
+        visible = jnp.concatenate([jnp.full((1, lanes), flag, jnp.int32) for flag in flags], axis=1)
+        queries = query_refs[number].at[:columns, :]
+        return queries, peaks_ref.at[turn], totals_ref.at[turn], visible > 0
+
+    for slot, index in enumerate(chosen):
         turn_values(frame_refs[slot][vision : 2 * vision, :], turned_ref.at[slot])
-    for turn, number in enumerate(groups):
-        if finish == "state":
-            peak_ref, total_ref = out_refs[0].at[turn], out_refs[1].at[turn]
-        else:
-            peak_ref, total_ref = peaks_ref, totals_ref
-        if resumed:
-            peak_ref[...] = state_refs[0][number]
-            total_ref[...] = state_refs[1][number]
-        else:
-            clear(peak_ref, total_ref)
-        for slot, index in enumerate(chosen):
+        members = []
+        for turn, (number, indices) in enumerate(units):
+            if index not in indices:
+                continue
             flags = []
             for block in range(blocks):
                 at = 2 * (number * blocks + block)
@@ -398,71 +456,81 @@
                     table_ref[at] <= frames[index], frames[index] < table_ref[at + 1]
                 )
                 flags.append(inside.astype(jnp.int32))
-
-            @pl.when(functools.reduce(jnp.maximum, flags) > 0)
-            def _():
-                visible = jnp.concatenate(
-                    [jnp.full((1, lanes), flag, jnp.int32) for flag in flags], axis=1
-                )
-                fold_keys(
-                    frame_refs[slot][:vision, :],
-                    turned_ref[slot],
-                    query_refs[turn].at[:columns, :],
-                    peak_ref,
-                    total_ref,
-                    visible > 0,
-                )
-
-        if finish == "state":
-            continue
-        mixed, log_sum = finish_columns(peak_ref, total_ref)
+            members.append((turn, number, flags, functools.reduce(jnp.maximum, flags)))
+
+        def fold(taken):
+            fold_keys(
+                frame_refs[slot][:vision, :],
+                turned_ref[slot],
+                [job(turn, number, flags) for turn, number, flags, _ in taken],
+            )
+
+        for begin in range(0, len(members), 2):
+            pair = members[begin : begin + 2]
+            if len(pair) == 2:
+                count = pair[0][3] + pair[1][3]
+                pl.when(count == 2)(functools.partial(fold, pair))
+                for member in pair:
+                    alone = jnp.logical_and(count == 1, member[3] == 1)
+                    pl.when(alone)(functools.partial(fold, [member]))
+            else:
+                pl.when(pair[0][3] == 1)(functools.partial(fold, pair))
+
+    if finish == "state":
+        return
+    stats = []
+    for turn in range(len(units)):
+        mixed, log_sum = finish_columns(peaks_ref.at[turn], totals_ref.at[turn])
         for block in range(blocks):
             span = slice(block * lanes, (block + 1) * lanes)
-            part, stat = mixed[:, span], log_sum[:, span]
-            if finish == "packed":
-                high = stat.astype(jnp.bfloat16)
-                rest = stat - high.astype(jnp.float32)
-                middle = rest.astype(jnp.bfloat16)
-                low = (rest - middle.astype(jnp.float32)).astype(jnp.bfloat16)
-                rows = [high, middle, low, jnp.zeros((stat_rows - 3, lanes), jnp.bfloat16)]
-                out_refs[0][turn * blocks + block, :HD, :] = part.astype(jnp.bfloat16)
-                out_refs[0][turn * blocks + block, HD:, :] = jnp.concatenate(rows, axis=0)
-            else:
-                out_refs[0][turn * blocks + block] = part
-                out_refs[1][turn * blocks + block] = jnp.broadcast_to(stat, (8, lanes))
-
-
-def cross_part(table, queries, frames, chosen, groups, state, finish, rows, inner, heads):
+            stats.append(log_sum[:, span])
+            row = (turn * blocks + block) * HD
+            out_refs[0][row : row + HD, :] = mixed[:, span].astype(out_refs[0].dtype)
+    stat = jnp.concatenate(stats, axis=0)
+    if finish == "packed":
+        high = stat.astype(jnp.bfloat16)
+        rest = stat - high.astype(jnp.float32)
+        middle = rest.astype(jnp.bfloat16)
+        low = rest - middle.astype(jnp.float32)
+        rows = [high.astype(jnp.float32), middle.astype(jnp.float32), low, jnp.zeros_like(stat)]
+        out_refs[0][len(stats) * HD :, :] = jnp.concatenate(rows, axis=0).astype(jnp.bfloat16)
+    else:
+        out_refs[1][...] = stat
+
+
+def cross_part(table, queries, frames, units, state, finish, rows, inner, heads):
     lanes = heads * TBLOCK
     columns = rows * heads
     vision = FRAME_LEN
-    count = len(groups) * (rows // TBLOCK)
+    count = len(units) * (rows // TBLOCK)
+    chosen = tuple(sorted({index for _, indices in units for index in indices}))
     if finish == "state":
         out_shape = (
-            jax.ShapeDtypeStruct((len(groups), 8, columns), jnp.float32),
-            jax.ShapeDtypeStruct((len(groups), HD + stat_rows, columns), jnp.float32),
+            jax.ShapeDtypeStruct((len(units), 8, columns), jnp.float32),
+            jax.ShapeDtypeStruct((len(units), HD + stat_rows, columns), jnp.float32),
         )
     elif finish == "packed":
-        out_shape = (jax.ShapeDtypeStruct((count, HD + stat_rows, lanes), jnp.bfloat16),)
+        out_shape = (jax.ShapeDtypeStruct((count * HD + 4 * count, lanes), jnp.bfloat16),)
     else:
         out_shape = (
-            jax.ShapeDtypeStruct((count, HD, lanes), jnp.float32),
-            jax.ShapeDtypeStruct((count, 8, lanes), jnp.float32),
+            jax.ShapeDtypeStruct((count * HD, lanes), jnp.float32),
+            jax.ShapeDtypeStruct((count, lanes), jnp.float32),
         )
-    arguments = [*(queries[number] for number in groups), *(frames[index] for index in chosen), *state]
+    arguments = [queries[number] for number, indices in units if indices]
+    arguments += [*(frames[index] for index in chosen), *state]
     return pl.pallas_call(
         functools.partial(
-            cross_kernel, inner, heads, columns, groups, chosen, len(state) > 0, finish
+            cross_kernel, inner, heads, columns, units, chosen, len(state) > 0, finish
         ),
         out_shape=out_shape,
         in_specs=[pl.BlockSpec(memory_space=pltpu.SMEM)] + whole(len(arguments)),
         out_specs=whole(len(out_shape)),
         scratch_shapes=[
             pltpu.VMEM((len(chosen), HD + stat_rows, vision), jnp.bfloat16),
-            pltpu.VMEM((8, columns), jnp.float32),
-            pltpu.VMEM((HD + stat_rows, columns), jnp.float32),
+            pltpu.VMEM((len(units), 8, columns), jnp.float32),
+            pltpu.VMEM((len(units), HD + stat_rows, columns), jnp.float32),
         ],
-        compiler_params=pltpu.CompilerParams(vmem_limit_bytes=24 * 2**20),
+        compiler_params=pltpu.CompilerParams(vmem_limit_bytes=28 * 2**20),
         name="cross_" + finish,
     )(table, *arguments)
 
@@ -498,7 +566,7 @@
         side = place if slot == 0 else 1 - place
         clear(peak_ref, total_ref)
         visible = key_index <= token + (plane * inner + side) * rows
-        fold_keys(key_ref[...], turned_ref[...], query_ref, peak_ref, total_ref, visible)
+        fold_keys(key_ref[...], turned_ref[...], [(query_ref, peak_ref, total_ref, visible)])
         mixed, _ = finish_columns(peak_ref, total_ref)
         for block in range(rows // TBLOCK):
             part = mixed[:, block * lanes : (block + 1) * lanes].T.astype(jnp.bfloat16)
@@ -527,22 +595,24 @@
 
 
 def combine_kernel(inner, heads, gate_ref, mixed_ref, stat_ref, returned_ref, out_ref):
-    count = mixed_ref.shape[0]
+    count = stat_ref.shape[0]
     side = count // inner
     place = lax.rem(lax.axis_index("ctx"), inner)
     gate = jnp.tanh(jnp.full((1, heads * TBLOCK), gate_ref[0], jnp.float32))
+    stats = returned_ref[count * HD :, :].astype(jnp.float32)
+    far_stat = stats[:count] + stats[count : 2 * count] + stats[2 * count : 3 * count]
+    own_stat = stat_ref[...]
+    peak = jnp.maximum(own_stat, far_stat)
+    own_weight = jnp.exp2(own_stat - peak)
+    far_weight = jnp.exp2(far_stat - peak)
+    ratio = gate / (own_weight + far_weight)
+    own_weight, far_weight = own_weight * ratio, far_weight * ratio
     for block in range(count):
         target = (block % side) * inner + (place if block < side else 1 - place)
-        stats = returned_ref[block, HD:, :].astype(jnp.float32)
-        far_stat = stats[0:1] + stats[1:2] + stats[2:3]
-        own_stat = stat_ref[block, 0:1, :]
-        peak = jnp.maximum(own_stat, far_stat)
-        own_weight = jnp.exp2(own_stat - peak)
-        far_weight = jnp.exp2(far_stat - peak)
-        ratio = gate / (own_weight + far_weight)
-        mixed = mixed_ref[block] * (own_weight * ratio) + returned_ref[block, :HD, :].astype(
+        span = slice(block * HD, (block + 1) * HD)
+        mixed = mixed_ref[span, :] * own_weight[block : block + 1] + returned_ref[span, :].astype(
             jnp.float32
-        ) * (far_weight * ratio)
+        ) * far_weight[block : block + 1]
         part = mixed.T.astype(jnp.bfloat16)
         for head in range(heads):
             out_ref[target, :, head * HD : (head + 1) * HD] = part[
@@ -551,10 +621,9 @@
 
 
 def combine(gate_scale, mixed, stat, returned, inner, heads):
-    count = mixed.shape[0]
     return pl.pallas_call(
         functools.partial(combine_kernel, inner, heads),
-        out_shape=jax.ShapeDtypeStruct((count, TBLOCK, heads * HD), jnp.bfloat16),
+        out_shape=jax.ShapeDtypeStruct((stat.shape[0], TBLOCK, heads * HD), jnp.bfloat16),
         in_specs=[pl.BlockSpec(memory_space=pltpu.SMEM)] + whole(3),
         out_specs=whole(1)[0],
         compiler_params=pltpu.CompilerParams(vmem_limit_bytes=16 * 2**20),
@@ -603,22 +672,21 @@
     def place_of(device):
         return device // inner, device % inner
 
-    def send(values, turn, flip, upward=False):
+    def send(values, turn, flip, upward=0):
         pairs = []
         for device in range(devices):
             plane, place = place_of(device)
             target = plane ^ turn
-            if not upward or target > plane:
+            if upward == 0 or target ^ upward < target:
                 pairs.append((device, target * inner + (place ^ flip)))
         return lax.ppermute(values, "ctx", pairs)
 
-    exponents = jnp.arange(HD // 2, dtype=jnp.float32) * (2.0 / HD)
-    frequency = jnp.power(rope_base, -exponents)
-    angles = positions.astype(jnp.float32)[:, None] * frequency[None, :]
+    exponents = np.arange(HD // 2) * (2.0 / HD)
+    frequency = jnp.asarray(np.power(rope_base, -exponents), jnp.float32)
     near_out, across_out, beside_out, own, other, own_self = prepare(
         media_range,
-        jnp.cos(angles),
-        jnp.sin(angles),
+        positions,
+        frequency,
         key_vision,
         value_vision,
         query_cross,
@@ -630,26 +698,32 @@
     partner = send(other, 0, 1)
     far = send(own, 2, 0)
     near = send(near_out, 1, 0)
-    beside_out, across_out, partner = lax.optimization_barrier((beside_out, across_out, partner))
+    beside = send(beside_out, 0, 1)
+    across_out, partner = lax.optimization_barrier((across_out, partner))
     far_across = send(partner, 2, 0)
     across = send(across_out, 1, 1)
-    beside = send(beside_out, 0, 1)
     tail = slice(rows * heads, rows * heads + 2 * rows)
-    last = send(jnp.concatenate([far[tail], far_across[tail]], axis=0), 1, 0)
+    last = send(jnp.concatenate([own[tail], partner[tail]], axis=0), 3, 0, upward=3)
 
     queries = (own, partner, far, far_across)
     table = [values[-TBLOCK, : 2 * (rows // TBLOCK)] for values in queries]
+    first_table = jnp.concatenate(table[:2]).astype(jnp.int32)
     table = jnp.concatenate(table).astype(jnp.int32)
     frames = (near_out, beside, near, across)
     sizes = (rows, inner, heads)
-    everyone = (0, 1, 2, 3)
-    state = cross_part(table, queries, frames, (0, 2), everyone, (), "state", *sizes)
-    state = cross_part(table, queries, frames, (3,), everyone, state, "state", *sizes)
+    units = ((0, (0, 2)), (1, (0, 2)), (2, ()), (3, ()))
+    state = cross_part(first_table, queries, frames, units, (), "state", *sizes)
+    units = ((0, ()), (1, ()), (2, (0, 2)), (3, (0, 2)))
+    state = cross_part(table, queries, frames, units, state, "state", *sizes)
+    units = ((0, (1,)), (1, (1,)), (2, (1,)), (3, (1,)))
+    state = cross_part(table, queries, frames, units, state, "state", *sizes)
     state, last = lax.optimization_barrier((state, last))
-    (outgoing,) = cross_part(table, queries, frames, (1,), (2, 3), state, "packed", *sizes)
+    units = ((2, (3,)), (3, (3,)))
+    (outgoing,) = cross_part(table, queries, frames, units, state, "packed", *sizes)
     returned = send(outgoing, 2, 0)
     outgoing, table, own_self = lax.optimization_barrier((outgoing, table, own_self))
-    mixed, stat = cross_part(table, queries, frames, (1,), (0, 1), state, "own", *sizes)
+    units = ((0, (3,)), (1, (3,)))
+    mixed, stat = cross_part(table, queries, frames, units, state, "own", *sizes)
     self_rows = self_part(
         own_self, beside, (own, partner, near, across, far, far_across, last), *sizes
     )

time: 74.3 us -> 67.6 us (0.910)
  waiting for transfers between devices: 26 us -> 19.2 us
  starting transfers between devices: 22 us -> 24 us
  other arithmetic: 1.58 us -> 0.16 us
    ppermute x8, waiting for transfers between devices: 20.8 us -> 13.9 us  [send(): return lax.ppermute(values, 'ctx', pairs)]
    ppermute x8, starting transfers between devices: 15.2 us -> 17 us  [send(): return lax.ppermute(values, 'ctx', pairs)]
    sin x1 -> x0, other arithmetic: 0.82 us -> none  [on_device_split(): jnp.sin(angles)]
    unnamed x9 -> x8, local copies, waits for them, and re-layouts: 2.73 us -> 1.96 us
    slice x2, local copies, waits for them, and re-layouts: 0.01 us -> 0.76 us  [the longest x1 0.76 us: on_device_split(): own[tail]]
    pallas_call x4 -> x5, Pallas kernels: 10.5 us -> 11.3 us  [cross_part(): pl.pallas_call(functools.partial(cross_kernel, inner, heads, columns, uni...]
  transfers between devices with their start and end apart: 10 -> 10, of which waited for: 5 -> 5; matrix products, arithmetic and copies ran while one was open for 1% -> 2% of each run, Pallas kernels for 15% -> 19%
where the time goes in v3:
time: 67.6 us; the launch traced here: 67 us
  starting transfers between devices  24 us (36%)
  waiting for transfers between devices  19.2 us (28%)
  Pallas kernels  18.8 us (28%)
  local copies, waits for them, and re-layouts  3.41 us (5%)
  between operations  1.43 us (2%)
    ppermute x8, starting transfers between devices, send(): return lax.ppermute(values, 'ctx', pairs)  17 us
    ppermute x8, waiting for transfers between devices, send(): return lax.ppermute(values, 'ctx', pairs)  13.9 us
    pallas_call x5, Pallas kernels, cross_part(): pl.pallas_call(functools.partial(cross_kernel, inner, heads, columns, uni...  11.3 us
    all_to_all x2, starting transfers between devices, exchange(): lax.all_to_all(outward.reshape(-1, outward.shape[2]), ('ctx', 'head'), 0,...  7.04 us
    all_to_all x2, waiting for transfers between devices, exchange(): lax.all_to_all(outward.reshape(-1, outward.shape[2]), ('ctx', 'head'), 0,...  5.23 us
    pallas_call x1, Pallas kernels, prepare(): pl.pallas_call(functools.partial(prepare_kernel, inner), out_shape=[jax.S...  3.25 us
    pallas_call x1, Pallas kernels, self_part(): pl.pallas_call(functools.partial(self_kernel, inner, heads, rows), out_sh...  2.02 us
    unnamed x8, local copies, waits for them, and re-layouts  1.96 us
  transfers between devices with their start and end apart: 10, of which 5 were waited for; matrix products, arithmetic and copies ran while one was open for 2% of the time, Pallas kernels for 19%

profile of v3, /device:TPU:0, one launch (start us, length us, event | category | flops | bytes accessed | tf_op | source)
XLA Modules:
  0.0 67.0 jit_solution(728071523319603301)
XLA Ops:
  0.6 3.3 %prepare_packets.1 = (bf16[1920,128]{1,0:T(8,128)(2,1)}, bf16[1920,128]{1,0:T(8,128)(2,1)}, bf16[2304,128]{1,0:T(8,128)(2,1)}, bf16[656,128]{1,0:T(8,128)(2,1)},...) custom-call(s32[2,4]{1,0:T(2,128)} %bitcast.10, s32[1,64]{1,0:T(1,128)} %bitcast.11, f32[1,64]{1,0:T(1,128)} %constant.4.frequency_ref, ...), custom_call_target="tpu_custom_call" | custom-call | tf_op jit(solution)/shard_map/prepare_packets/pallas_call | solution.py:328
  3.9 3.0 %collective-permute-start = (bf16[656,128]{1,0:T(8,128)(2,1)}, bf16[656,128]{1,0:T(8,128)(2,1)S(1)}, u32[]{:S(2)}, u32[]{:S(2)}) collective-permute-start(bf16[656,128]{1,0:T(8,128)(2,1)} %get-tuple-element.25), channel_id=1, source_target_pairs={{0,4},{4,0},{8,12},{12,8},{16,20},{20,16},{24,28},{28,24},{1,5},{5... | collective-permute-start | bytes 503816 | tf_op jit(solution)/shard_map/ppermute | solution.py:682
  6.9 2.6 %collective-permute-start.1 = (bf16[656,128]{1,0:T(8,128)(2,1)}, bf16[656,128]{1,0:T(8,128)(2,1)S(1)}, u32[]{:S(2)}, u32[]{:S(2)}) collective-permute-start(bf16[656,128]{1,0:T(8,128)(2,1)} %get-tuple-element.23.refs_0_), channel_id=1, source_target_pairs={{0,16},{4,20},{8,24},{12,28},{16,0},{20,4},{24,8},{28,12},{1,17},{... | collective-permute-start | bytes 503816 | tf_op jit(solution)/shard_map/ppermute | solution.py:682
  9.5 0.5 collective-permute-start.4
  10.0 1.6 %collective-permute-start.5 = (bf16[1920,128]{1,0:T(8,128)(2,1)}, bf16[1920,128]{1,0:T(8,128)(2,1)S(1)}, u32[]{:S(2)}, u32[]{:S(2)}) collective-permute-start(bf16[1920,128]{1,0:T(8,128)(2,1)} %get-tuple-element.29.refs_2_), channel_id=1, source_target_pairs={{0,8},{4,12},{8,0},{12,4},{16,24},{20,28},{24,16},{28,20},{1,9},{5... | collective-permute-start | bytes 1474568 | tf_op jit(solution)/shard_map/ppermute | solution.py:682
  11.6 0.8 %slice.22 = bf16[128,128]{1,0:T(8,128)(2,1)S(1)} slice(bf16[656,128]{1,0:T(8,128)(2,1)} %get-tuple-element.23.refs_0_), slice={[512:640], [0:128]} | slice | bytes 65536 | tf_op jit(solution)/shard_map/slice | solution.py:706
  12.4 0.7 %slice_bitcast_fusion.3 = bf16[8]{0:T(256)(128)(2,1)S(1)} fusion(bf16[656,128]{1,0:T(8,128)(2,1)} %get-tuple-element.23.refs_0_), kind=kLoop, calls=%fused_computation.6 | loop fusion | bytes 32 | tf_op jit(solution)/shard_map/squeeze | solution.py:709
  13.0 0.0 collective-permute-done.refs_1_
  13.0 2.3 %collective-permute-start.2 = (bf16[656,128]{1,0:T(8,128)(2,1)S(1)}, bf16[656,128]{1,0:T(8,128)(2,1)S(1)}, u32[]{:S(2)}, u32[]{:S(2)}) collective-permute-start(bf16[656,128]{1,0:T(8,128)(2,1)S(1)} %collective-permute-done.refs_1_), channel_id=1, source_target_pairs={{0,16},{4,20},{8,24},{12,28},{16,0},{20,4},{24,8},{28,12},{1,17},{... | collective-permute-start | bytes 503816 | tf_op jit(solution)/shard_map/ppermute | solution.py:682
  15.4 2.5 %collective-permute-start.3 = (bf16[1920,128]{1,0:T(8,128)(2,1)}, bf16[1920,128]{1,0:T(8,128)(2,1)S(1)}, u32[]{:S(2)}, u32[]{:S(2)}) collective-permute-start(bf16[1920,128]{1,0:T(8,128)(2,1)} %get-tuple-element.27), channel_id=1, source_target_pairs={{0,12},{4,8},{8,4},{12,0},{16,28},{20,24},{24,20},{28,16},{1,13},{... | collective-permute-start | bytes 1474568 | tf_op jit(solution)/shard_map/ppermute | solution.py:682
  17.9 0.7 %collective-permute-done.1.refs_0_.refs_2_.refs_4_ = bf16[656,128]{1,0:T(8,128)(2,1)S(1)} collective-permute-done((bf16[656,128]{1,0:T(8,128)(2,1)}, bf16[656,128]{1,0:T(8,128)(2,1)S(1)}, u32[]{:S(2)}, u32[]{:S(2)}) %collective-permute-start.1) | collective-permute-done | bytes 167968 | tf_op jit(solution)/shard_map/ppermute | solution.py:682
  18.6 4.3 %collective-permute-start.6 = (bf16[256,128]{1,0:T(8,128)(2,1)S(1)}, bf16[256,128]{1,0:T(8,128)(2,1)S(1)}, u32[]{:S(2)}, u32[]{:S(2)}) collective-permute-start(bf16[256,128]{1,0:T(8,128)(2,1)S(1)} %pad_maximum_fusion), channel_id=1, source_target_pairs={{0,24},{4,28},{8,16},{12,20},{1,25},{5,29},{9,17},{13,21},{2,26},{... | collective-permute-start | bytes 196616 | tf_op jit(solution)/shard_map/ppermute | solution.py:682
  23.0 0.1 maximum_convert_fusion.1.table_ref
  23.1 5.6 %collective-permute-done.2.refs_1_.refs_3_.refs_5_ = bf16[656,128]{1,0:T(8,128)(2,1)S(1)} collective-permute-done((bf16[656,128]{1,0:T(8,128)(2,1)S(1)}, bf16[656,128]{1,0:T(8,128)(2,1)S(1)}, u32[]{:S(2)}, u32[]{:S(2)}) %collective-permute-start.2) | collective-permute-done | bytes 167968 | tf_op jit(solution)/shard_map/ppermute | solution.py:682
  28.6 0.1 maximum_convert_fusion.table_ref
  28.7 1.6 %collective-permute-done.5.refs_3_.refs_2_ = bf16[1920,128]{1,0:T(8,128)(2,1)S(1)} collective-permute-done((bf16[1920,128]{1,0:T(8,128)(2,1)}, bf16[1920,128]{1,0:T(8,128)(2,1)S(1)}, u32[]{:S(2)}, u32[]{:S(2)}) %collective-permute-start.5) | collective-permute-done | bytes 491552 | tf_op jit(solution)/shard_map/ppermute | solution.py:682
  30.3 0.0 copy-start
  30.3 0.9 %copy-done = bf16[656,128]{1,0:T(8,128)(2,1)S(1)} copy-done((bf16[656,128]{1,0:T(8,128)(2,1)S(1)}, bf16[656,128]{1,0:T(8,128)(2,1)}, u32[]{:S(2)}) %copy-start) | copy-done | bytes 167960
  31.3 0.0 copy-start.2
  31.3 1.0 %copy-done.2 = bf16[1920,128]{1,0:T(8,128)(2,1)S(1)} copy-done((bf16[1920,128]{1,0:T(8,128)(2,1)S(1)}, bf16[1920,128]{1,0:T(8,128)(2,1)}, u32[]{:S(2)}) %copy-start.2) | copy-done | bytes 491544
  32.3 1.8 %cross_state.3 = (f32[4,8,512]{2,1,0:T(8,128)S(1)}, f32[4,144,512]{2,1,0:T(8,128)S(1)}) custom-call(s32[16]{0:T(128)S(1)} %maximum_convert_fusion.1.table_ref, bf16[656,128]{1,0:T(8,128)(2,1)S(1)} %copy-done, bf16[656,128]{1,0:T(8,128)(2,1)S(1)} %collective-permute-done.refs_1_, bf16[1920,128]{1,0:T(8,128)(2,1)S(1)} %copy-done.2, ...), custom_call_target="tpu_custom_call" | custom-call | tf_op jit(solution)/shard_map/cross_state/pallas_call | solution.py:521
  34.1 0.0 copy-start.1
  34.1 4.1 %cross_state.4 = (f32[4,8,512]{2,1,0:T(8,128)S(1)}, f32[4,144,512]{2,1,0:T(8,128)S(1)}) custom-call(s32[32]{0:T(128)S(1)} %maximum_convert_fusion.table_ref, bf16[656,128]{1,0:T(8,128)(2,1)S(1)} %collective-permute-done.1.refs_0_.refs_2_.refs_4_, bf16[656,128]{1,0:T(8,128)(2,1)S(1)} %collective-permute-done.2.refs_1_.refs_3_.refs_5_, ...), custom_call_target="tpu_custom_call" | custom-call | tf_op jit(solution)/shard_map/cross_state/pallas_call | solution.py:521
  38.3 0.0 collective-permute-done.4.refs_4_.beside_ref
  38.3 0.0 copy-done.1
  38.3 2.3 %cross_state.5 = (f32[4,8,512]{2,1,0:T(8,128)S(1)}, f32[4,144,512]{2,1,0:T(8,128)S(1)}) custom-call(s32[32]{0:T(128)S(1)} %maximum_convert_fusion.table_ref, bf16[656,128]{1,0:T(8,128)(2,1)S(1)} %copy-done.1, bf16[656,128]{1,0:T(8,128)(2,1)S(1)} %collective-permute-done.refs_1_, bf16[656,128]{1,0:T(8,128)(2,1)S(1)} %collective-permute-done.1.refs_0_.refs_2_.refs_4_, ...), custom_call_target="tpu_custom_call" | custom-call | tf_op jit(solution)/shard_map/cross_state/pallas_call | solution.py:521
  40.6 0.0 copy-start.3
  40.6 0.0 collective-permute-done.6.refs_6_
  40.6 0.0 collective-permute-done.3.refs_2_.refs_3_
  40.6 2.3 %cross_packed.1 = bf16[1056,128]{1,0:T(8,128)(2,1)S(1)} custom-call(s32[32]{0:T(128)S(1)} %maximum_convert_fusion.table_ref, bf16[656,128]{1,0:T(8,128)(2,1)S(1)} %collective-permute-done.1.refs_0_.refs_2_.refs_4_, bf16[656,128]{1,0:T(8,128)(2,1)S(1)} %collective-permute-done.2.refs_1_.refs_3_.refs_5_, ...), custom_call_target="tpu_custom_call" | custom-call | tf_op jit(solution)/shard_map/cross_packed/pallas_call | solution.py:521
  42.9 0.1 collective-permute-start.7
  43.0 0.0 copy-done.3
  43.0 2.0 %self_attention.1 = bf16[8,16,1024]{2,1,0:T(8,128)(2,1)} custom-call(bf16[512,128]{1,0:T(8,128)(2,1)S(1)} %copy-done.3, bf16[2304,128]{1,0:T(8,128)(2,1)S(1)} %collective-permute-done.4.refs_4_.beside_ref, bf16[656,128]{1,0:T(8,128)(2,1)S(1)} %copy-done.1, bf16[656,128]{1,0:T(8,128)(2,1)S(1)} %collective-permute-done.refs_1_, ...), custom_call_target="tpu_custom_call" | custom-call | tf_op jit(solution)/shard_map/self_attention/pallas_call | solution.py:580
  45.0 3.6 %all-to-all-start = ((bf16[8,16,1024]{2,1,0:T(8,128)(2,1)}), bf16[8,16,1024]{2,1,0:T(8,128)(2,1)S(1)}, u32[]{:S(2)}, u32[]{:S(2)}) async-start(bf16[8,16,1024]{2,1,0:T(8,128)(2,1)} %self_attention.1), calls=%async_computation | async-start | bytes 524288 | tf_op jit(solution)/shard_map/all_to_all | solution.py:740
  49.3 0.7 %cross_own.1 = (f32[1024,128]{1,0:T(8,128)S(1)}, f32[8,128]{1,0:T(8,128)S(1)}) custom-call(s32[32]{0:T(128)S(1)} %maximum_convert_fusion.table_ref, bf16[656,128]{1,0:T(8,128)(2,1)S(1)} %copy-done.1, bf16[656,128]{1,0:T(8,128)(2,1)S(1)} %collective-permute-done.refs_1_, bf16[1920,128]{1,0:T(8,128)(2,1)S(1)} %collective-permute-done.3.refs_2_.refs_3_, ...), custom_call_target="tpu_custom_call" | custom-call | tf_op jit(solution)/shard_map/cross_own/pallas_call | solution.py:521
  50.0 6.0 %collective-permute-done.7.returned_ref = bf16[1056,128]{1,0:T(8,128)(2,1)S(1)} collective-permute-done((bf16[1056,128]{1,0:T(8,128)(2,1)S(1)}, bf16[1056,128]{1,0:T(8,128)(2,1)S(1)}, u32[]{:S(2)}, u32[]{:S(2)}) %collective-permute-start.7) | collective-permute-done | bytes 270368 | tf_op jit(solution)/shard_map/ppermute | solution.py:682
  56.0 0.9 %combine_planes.1 = bf16[8,16,1024]{2,1,0:T(8,128)(2,1)} custom-call(f32[1]{0:T(128)S(6)} %copy.12.gate_ref, f32[1024,128]{1,0:T(8,128)S(1)} %get-tuple-element.42.mixed_ref, f32[8,128]{1,0:T(8,128)S(1)} %get-tuple-element.43.stat_ref, bf16[1056,128]{1,0:T(8,128)(2,1)S(1)} %collective-permute-done.7.returned_ref), custom_call_target="tpu_custom_call" | custom-call | tf_op jit(solution)/shard_map/combine_planes/pallas_call | solution.py:624
  56.9 0.0 all-to-all-done.in_ref
  56.9 3.4 %all-to-all-start.1 = ((bf16[8,16,1024]{2,1,0:T(8,128)(2,1)}), bf16[8,16,1024]{2,1,0:T(8,128)(2,1)S(1)}, u32[]{:S(2)}, u32[]{:S(2)}) async-start(bf16[8,16,1024]{2,1,0:T(8,128)(2,1)} %combine_planes.1), calls=%async_computation.1 | async-start | bytes 524288 | tf_op jit(solution)/shard_map/all_to_all | solution.py:740
  60.3 0.7 %spread_heads.2 = bf16[16,8192]{1,0:T(8,128)(2,1)} custom-call(bf16[8,16,1024]{2,1,0:T(8,128)(2,1)S(1)} %all-to-all-done.in_ref), custom_call_target="tpu_custom_call" | custom-call | tf_op jit(solution)/shard_map/spread_heads/pallas_call | solution.py:642
  61.1 5.2 %all-to-all-done.1.in_ref = bf16[8,16,1024]{2,1,0:T(8,128)(2,1)S(1)} async-done(((bf16[8,16,1024]{2,1,0:T(8,128)(2,1)}), bf16[8,16,1024]{2,1,0:T(8,128)(2,1)S(1)}, u32[]{:S(2)}, u32[]{:S(2)}) %all-to-all-start.1) | async-done | bytes 262176 | tf_op jit(solution)/shard_map/all_to_all | solution.py:740
  66.3 0.7 %spread_heads.3 = bf16[16,8192]{1,0:T(8,128)(2,1)} custom-call(bf16[8,16,1024]{2,1,0:T(8,128)(2,1)S(1)} %all-to-all-done.1.in_ref), custom_call_target="tpu_custom_call" | custom-call | tf_op jit(solution)/shard_map/spread_heads/pallas_call | solution.py:642
  (5 shorter events, 0.0 us)
Async XLA Ops:
  3.9 9.2 %collective-permute-start = (bf16[656,128]{1,0:T(8,128)(2,1)}, bf16[656,128]{1,0:T(8,128)(2,1)S(1)}, u32[]{:S(2)}, u32[]{:S(2)}) collective-permute-start(bf16[656,128]{1,0:T(8,128)(2,1)} %get-tuple-element.25), channel_id=1, source_target_pairs={{0,4},{4,0},{8,12},{12,8},{16,20},{20,16},{24,28},{28,24},{1,5},{5... | collective-permute-start | bytes 503816 | tf_op jit(solution)/shard_map/ppermute | solution.py:682
  6.9 11.7 %collective-permute-start.1 = (bf16[656,128]{1,0:T(8,128)(2,1)}, bf16[656,128]{1,0:T(8,128)(2,1)S(1)}, u32[]{:S(2)}, u32[]{:S(2)}) collective-permute-start(bf16[656,128]{1,0:T(8,128)(2,1)} %get-tuple-element.23.refs_0_), channel_id=1, source_target_pairs={{0,16},{4,20},{8,24},{12,28},{16,0},{20,4},{24,8},{28,12},{1,17},{... | collective-permute-start | bytes 503816 | tf_op jit(solution)/shard_map/ppermute | solution.py:682
  9.5 28.8 %collective-permute-start.4 = (bf16[2304,128]{1,0:T(8,128)(2,1)}, bf16[2304,128]{1,0:T(8,128)(2,1)S(1)}, u32[]{:S(2)}, u32[]{:S(2)}) collective-permute-start(bf16[2304,128]{1,0:T(8,128)(2,1)} %get-tuple-element.28), channel_id=1, source_target_pairs={{0,4},{4,0},{8,12},{12,8},{16,20},{20,16},{24,28},{28,24},{1,5},{5... | collective-permute-start | bytes 1769480 | tf_op jit(solution)/shard_map/ppermute | solution.py:682
  10.0 20.3 %collective-permute-start.5 = (bf16[1920,128]{1,0:T(8,128)(2,1)}, bf16[1920,128]{1,0:T(8,128)(2,1)S(1)}, u32[]{:S(2)}, u32[]{:S(2)}) collective-permute-start(bf16[1920,128]{1,0:T(8,128)(2,1)} %get-tuple-element.29.refs_2_), channel_id=1, source_target_pairs={{0,8},{4,12},{8,0},{12,4},{16,24},{20,28},{24,16},{28,20},{1,9},{5... | collective-permute-start | bytes 1474568 | tf_op jit(solution)/shard_map/ppermute | solution.py:682
  13.0 15.6 %collective-permute-start.2 = (bf16[656,128]{1,0:T(8,128)(2,1)S(1)}, bf16[656,128]{1,0:T(8,128)(2,1)S(1)}, u32[]{:S(2)}, u32[]{:S(2)}) collective-permute-start(bf16[656,128]{1,0:T(8,128)(2,1)S(1)} %collective-permute-done.refs_1_), channel_id=1, source_target_pairs={{0,16},{4,20},{8,24},{12,28},{16,0},{20,4},{24,8},{28,12},{1,17},{... | collective-permute-start | bytes 503816 | tf_op jit(solution)/shard_map/ppermute | solution.py:682
  15.4 25.2 %collective-permute-start.3 = (bf16[1920,128]{1,0:T(8,128)(2,1)}, bf16[1920,128]{1,0:T(8,128)(2,1)S(1)}, u32[]{:S(2)}, u32[]{:S(2)}) collective-permute-start(bf16[1920,128]{1,0:T(8,128)(2,1)} %get-tuple-element.27), channel_id=1, source_target_pairs={{0,12},{4,8},{8,4},{12,0},{16,28},{20,24},{24,20},{28,16},{1,13},{... | collective-permute-start | bytes 1474568 | tf_op jit(solution)/shard_map/ppermute | solution.py:682
  18.6 21.9 %collective-permute-start.6 = (bf16[256,128]{1,0:T(8,128)(2,1)S(1)}, bf16[256,128]{1,0:T(8,128)(2,1)S(1)}, u32[]{:S(2)}, u32[]{:S(2)}) collective-permute-start(bf16[256,128]{1,0:T(8,128)(2,1)S(1)} %pad_maximum_fusion), channel_id=1, source_target_pairs={{0,24},{4,28},{8,16},{12,20},{1,25},{5,29},{9,17},{13,21},{2,26},{... | collective-permute-start | bytes 196616 | tf_op jit(solution)/shard_map/ppermute | solution.py:682
  30.3 0.9 %copy-start = (bf16[656,128]{1,0:T(8,128)(2,1)S(1)}, bf16[656,128]{1,0:T(8,128)(2,1)}, u32[]{:S(2)}) copy-start(bf16[656,128]{1,0:T(8,128)(2,1)} %get-tuple-element.23.refs_0_) | copy-start | bytes 503812
  31.3 1.0 %copy-start.2 = (bf16[1920,128]{1,0:T(8,128)(2,1)S(1)}, bf16[1920,128]{1,0:T(8,128)(2,1)}, u32[]{:S(2)}) copy-start(bf16[1920,128]{1,0:T(8,128)(2,1)} %get-tuple-element.29.refs_2_) | copy-start | bytes 1474564
  34.1 4.2 %copy-start.1 = (bf16[656,128]{1,0:T(8,128)(2,1)S(1)}, bf16[656,128]{1,0:T(8,128)(2,1)}, u32[]{:S(2)}) copy-start(bf16[656,128]{1,0:T(8,128)(2,1)} %get-tuple-element.23.refs_0_) | copy-start | bytes 503812
  40.6 2.4 %copy-start.3 = (bf16[512,128]{1,0:T(8,128)(2,1)S(1)}, bf16[512,128]{1,0:T(8,128)(2,1)}, u32[]{:S(2)}) copy-start(bf16[512,128]{1,0:T(8,128)(2,1)} %get-tuple-element.39.own_ref) | copy-start | bytes 393220
  42.9 13.1 %collective-permute-start.7 = (bf16[1056,128]{1,0:T(8,128)(2,1)S(1)}, bf16[1056,128]{1,0:T(8,128)(2,1)S(1)}, u32[]{:S(2)}, u32[]{:S(2)}) collective-permute-start(bf16[1056,128]{1,0:T(8,128)(2,1)S(1)} %cross_packed.1), channel_id=1, source_target_pairs={{0,16},{4,20},{8,24},{12,28},{16,0},{20,4},{24,8},{28,12},{1,17},{... | collective-permute-start | bytes 811016 | tf_op jit(solution)/shard_map/ppermute | solution.py:682
  45.0 11.9 %all-to-all-start = ((bf16[8,16,1024]{2,1,0:T(8,128)(2,1)}), bf16[8,16,1024]{2,1,0:T(8,128)(2,1)S(1)}, u32[]{:S(2)}, u32[]{:S(2)}) async-start(bf16[8,16,1024]{2,1,0:T(8,128)(2,1)} %self_attention.1), calls=%async_computation | async-start | bytes 524288 | tf_op jit(solution)/shard_map/all_to_all | solution.py:740
  56.9 9.4 %all-to-all-start.1 = ((bf16[8,16,1024]{2,1,0:T(8,128)(2,1)}), bf16[8,16,1024]{2,1,0:T(8,128)(2,1)S(1)}, u32[]{:S(2)}, u32[]{:S(2)}) async-start(bf16[8,16,1024]{2,1,0:T(8,128)(2,1)} %combine_planes.1), calls=%async_computation.1 | async-start | bytes 524288 | tf_op jit(solution)/shard_map/all_to_all | solution.py:740

commit v4 on v3

--- a/solution.py
+++ b/solution.py
@@ -419,9 +419,15 @@
     )
 
 
-def cross_kernel(inner, heads, columns, units, chosen, resumed, finish, table_ref, *refs):
+def cross_kernel(inner, heads, columns, places, units, chosen, resumed, finish, table_ref, *refs):
     refs = list(refs)
-    query_refs = {number: refs.pop(0) for number, frames in units if frames}
+    arrays = sorted({places[number][0] for number, frames in units if frames})
+    arrays = {array: refs.pop(0) for array in arrays}
+    query_refs = {}
+    for number, frames in units:
+        if frames:
+            array, row = places[number]
+            query_refs[number] = arrays[array].at[pl.ds(row, columns), :]
     frame_refs = [refs.pop(0) for _ in chosen]
     state_refs = [refs.pop(0) for _ in range(2)] if resumed else None
     out_refs, (turned_ref, peaks_ref, totals_ref) = refs[:-3], refs[-3:]
@@ -440,8 +446,7 @@
 
     def job(turn, number, flags):
         visible = jnp.concatenate([jnp.full((1, lanes), flag, jnp.int32) for flag in flags], axis=1)
-        queries = query_refs[number].at[:columns, :]
-        return queries, peaks_ref.at[turn], totals_ref.at[turn], visible > 0
+        return query_refs[number], peaks_ref.at[turn], totals_ref.at[turn], visible > 0
 
     for slot, index in enumerate(chosen):
         turn_values(frame_refs[slot][vision : 2 * vision, :], turned_ref.at[slot])
@@ -516,11 +521,14 @@
             jax.ShapeDtypeStruct((count * HD, lanes), jnp.float32),
             jax.ShapeDtypeStruct((count, lanes), jnp.float32),
         )
-    arguments = [queries[number] for number, indices in units if indices]
+    packet = columns + 2 * rows + TBLOCK
+    places = ((0, 0), (1, 0), (2, 0), (2, packet))
+    arrays = sorted({places[number][0] for number, indices in units if indices})
+    arguments = [queries[array] for array in arrays]
     arguments += [*(frames[index] for index in chosen), *state]
     return pl.pallas_call(
         functools.partial(
-            cross_kernel, inner, heads, columns, units, chosen, len(state) > 0, finish
+            cross_kernel, inner, heads, columns, places, units, chosen, len(state) > 0, finish
         ),
         out_shape=out_shape,
         in_specs=[pl.BlockSpec(memory_space=pltpu.SMEM)] + whole(len(arguments)),
@@ -536,17 +544,19 @@
 
 
 def self_kernel(inner, heads, rows, own_ref, beside_ref, *refs):
-    key_value_refs, out_ref = refs[:7], refs[7]
-    key_ref, value_ref, turned_ref, peak_ref, total_ref = refs[8:]
+    key_value_refs, out_ref = refs[:6], refs[6]
+    key_ref, value_ref, turned_ref, peak_ref, total_ref = refs[7:]
     device = lax.axis_index("ctx")
     plane, place = device // inner, lax.rem(device, inner)
     lanes = heads * TBLOCK
     columns = rows * heads
     vision = beside_ref.shape[0] - columns
-    tails = [(ref, ref.shape[0] - TBLOCK - 2 * rows) for ref in key_value_refs[:2]]
-    tails += [(ref, ref.shape[0] - 2 * rows) for ref in key_value_refs[2:4]]
-    tails += [(ref, ref.shape[0] - TBLOCK - 2 * rows) for ref in key_value_refs[4:6]]
-    tails += [(key_value_refs[6], 0), (key_value_refs[6], 2 * rows)]
+    own_kv, partner_kv, near_kv, across_kv, far_kv, last_kv = key_value_refs
+    packet = own_kv.shape[0]
+    vision_rows = near_kv.shape[0] - 2 * rows
+    tails = [(own_kv, columns), (partner_kv, columns), (near_kv, vision_rows)]
+    tails += [(across_kv, vision_rows), (far_kv, columns), (far_kv, packet + columns)]
+    tails += [(last_kv, 0), (last_kv, 2 * rows)]
     for slot, (ref, begin) in enumerate(tails):
         span = slice(slot * rows, (slot + 1) * rows)
         key_ref[span, :] = ref[begin : begin + rows, :]
@@ -696,17 +706,19 @@
         inner,
     )
     partner = send(other, 0, 1)
-    far = send(own, 2, 0)
     near = send(near_out, 1, 0)
     beside = send(beside_out, 0, 1)
     across_out, partner = lax.optimization_barrier((across_out, partner))
-    far_across = send(partner, 2, 0)
+    packets = jnp.concatenate([own, partner], axis=0)
+    far = send(packets, 2, 0)
     across = send(across_out, 1, 1)
     tail = slice(rows * heads, rows * heads + 2 * rows)
     last = send(jnp.concatenate([own[tail], partner[tail]], axis=0), 3, 0, upward=3)
 
-    queries = (own, partner, far, far_across)
-    table = [values[-TBLOCK, : 2 * (rows // TBLOCK)] for values in queries]
+    queries = (own, partner, far)
+    count = own.shape[0]
+    table = [values[count - TBLOCK, : 2 * (rows // TBLOCK)] for values in queries]
+    table.append(far[2 * count - TBLOCK, : 2 * (rows // TBLOCK)])
     first_table = jnp.concatenate(table[:2]).astype(jnp.int32)
     table = jnp.concatenate(table).astype(jnp.int32)
     frames = (near_out, beside, near, across)
@@ -725,7 +737,7 @@
     units = ((0, (3,)), (1, (3,)))
     mixed, stat = cross_part(table, queries, frames, units, state, "own", *sizes)
     self_rows = self_part(
-        own_self, beside, (own, partner, near, across, far, far_across, last), *sizes
+        own_self, beside, (own, partner, near, across, far, last), *sizes
     )
     planes = [
         [

time: 67.6 us -> 66 us (0.976)
  starting transfers between devices: 24 us -> 21.1 us
  waiting for transfers between devices: 19.2 us -> 20.7 us
  local copies, waits for them, and re-layouts: 3.41 us -> 2.38 us
  other arithmetic: 0.16 us -> 1.1 us
    ppermute x8 -> x7, starting transfers between devices: 17 us -> 14.1 us  [send(): return lax.ppermute(values, 'ctx', pairs)]
    ppermute x8 -> x7, waiting for transfers between devices: 13.9 us -> 15.4 us  [send(): return lax.ppermute(values, 'ctx', pairs)]
    unnamed x8, local copies, waits for them, and re-layouts: 1.96 us -> 0.93 us
    concatenate x0 -> x1, other arithmetic: none -> 0.94 us  [on_device_split(): packets = jnp.concatenate([own, partner], axis=0)]
  transfers between devices with their start and end apart: 10 -> 9, of which waited for: 5 -> 6; matrix products, arithmetic and copies ran while one was open for 2% -> 4% of each run, Pallas kernels for 19% -> 19%
where the time goes in v4:
time: 66 us; the launch traced here: 65.5 us
  starting transfers between devices  21.1 us (32%)
  waiting for transfers between devices  20.7 us (31%)
  Pallas kernels  18.8 us (28%)
  local copies, waits for them, and re-layouts  2.38 us (4%)
  between operations  1.41 us (2%)
  other arithmetic  1.1 us (2%)
    ppermute x7, waiting for transfers between devices, send(): return lax.ppermute(values, 'ctx', pairs)  15.4 us
    ppermute x7, starting transfers between devices, send(): return lax.ppermute(values, 'ctx', pairs)  14.1 us
    pallas_call x5, Pallas kernels, cross_part(): pl.pallas_call(functools.partial(cross_kernel, inner, heads, columns, pla...  11.2 us
    all_to_all x2, starting transfers between devices, exchange(): lax.all_to_all(outward.reshape(-1, outward.shape[2]), ('ctx', 'head'), 0,...  7.04 us
    all_to_all x2, waiting for transfers between devices, exchange(): lax.all_to_all(outward.reshape(-1, outward.shape[2]), ('ctx', 'head'), 0,...  5.23 us
    pallas_call x1, Pallas kernels, prepare(): pl.pallas_call(functools.partial(prepare_kernel, inner), out_shape=[jax.S...  3.25 us
    pallas_call x1, Pallas kernels, self_part(): pl.pallas_call(functools.partial(self_kernel, inner, heads, rows), out_sh...  2.02 us
    pallas_call x2, Pallas kernels, spread(): pl.pallas_call(spread_kernel, out_shape=jax.ShapeDtypeStruct((rows, count...  1.44 us
  transfers between devices with their start and end apart: 9, of which 6 were waited for; matrix products, arithmetic and copies ran while one was open for 4% of the time, Pallas kernels for 19%

profile of v4, /device:TPU:0, one launch (start us, length us, event | category | flops | bytes accessed | tf_op | source)
XLA Modules:
  0.0 65.5 jit_solution(13796584803042002543)
XLA Ops:
  0.6 3.3 %prepare_packets.1 = (bf16[1920,128]{1,0:T(8,128)(2,1)}, bf16[1920,128]{1,0:T(8,128)(2,1)}, bf16[2304,128]{1,0:T(8,128)(2,1)}, bf16[656,128]{1,0:T(8,128)(2,1)},...) custom-call(s32[2,4]{1,0:T(2,128)} %bitcast.10, s32[1,64]{1,0:T(1,128)} %bitcast.11, f32[1,64]{1,0:T(1,128)} %constant.4.frequency_ref, ...), custom_call_target="tpu_custom_call" | custom-call | tf_op jit(solution)/shard_map/prepare_packets/pallas_call | solution.py:328
  3.9 0.0 copy-start.2
  3.9 3.0 %collective-permute-start = (bf16[656,128]{1,0:T(8,128)(2,1)}, bf16[656,128]{1,0:T(8,128)(2,1)S(1)}, u32[]{:S(2)}, u32[]{:S(2)}) collective-permute-start(bf16[656,128]{1,0:T(8,128)(2,1)} %get-tuple-element.25), channel_id=1, source_target_pairs={{0,4},{4,0},{8,12},{12,8},{16,20},{20,16},{24,28},{28,24},{1,5},{5... | collective-permute-start | bytes 503816 | tf_op jit(solution)/shard_map/ppermute | solution.py:692
  6.9 0.1 collective-permute-start.3
  7.0 2.0 %collective-permute-start.4 = (bf16[1920,128]{1,0:T(8,128)(2,1)}, bf16[1920,128]{1,0:T(8,128)(2,1)S(1)}, u32[]{:S(2)}, u32[]{:S(2)}) collective-permute-start(bf16[1920,128]{1,0:T(8,128)(2,1)} %get-tuple-element.29.refs_2_.refs_1_), channel_id=1, source_target_pairs={{0,8},{4,12},{8,0},{12,4},{16,24},{20,28},{24,16},{28,20},{1,9},{5... | collective-permute-start | bytes 1474568 | tf_op jit(solution)/shard_map/ppermute | solution.py:692
  9.0 0.8 %slice.22 = bf16[128,128]{1,0:T(8,128)(2,1)S(1)} slice(bf16[656,128]{1,0:T(8,128)(2,1)} %get-tuple-element.23.refs_0_), slice={[512:640], [0:128]} | slice | bytes 65536 | tf_op jit(solution)/shard_map/slice | solution.py:716
  9.8 0.7 %slice_bitcast_fusion.3 = bf16[8]{0:T(256)(128)(2,1)S(1)} fusion(bf16[656,128]{1,0:T(8,128)(2,1)} %get-tuple-element.23.refs_0_), kind=kLoop, calls=%fused_computation.7 | loop fusion | bytes 32 | tf_op jit(solution)/shard_map/squeeze | solution.py:720
  10.5 1.8 %collective-permute-done.refs_1_ = bf16[656,128]{1,0:T(8,128)(2,1)S(1)} collective-permute-done((bf16[656,128]{1,0:T(8,128)(2,1)}, bf16[656,128]{1,0:T(8,128)(2,1)S(1)}, u32[]{:S(2)}, u32[]{:S(2)}) %collective-permute-start) | collective-permute-done | bytes 167968 | tf_op jit(solution)/shard_map/ppermute | solution.py:692
  12.3 0.9 %pad_maximum_fusion = bf16[1312,128]{1,0:T(8,128)(2,1)S(1)} fusion(bf16[656,128]{1,0:T(8,128)(2,1)S(1)} %collective-permute-done.refs_1_, bf16[656,128]{1,0:T(8,128)(2,1)} %get-tuple-element.23.refs_0_), kind=kLoop, calls=%fused_computation | loop fusion | flops 671744 | bytes 671744 | tf_op jit(solution)/shard_map/concatenate | solution.py:712
  13.2 3.2 %collective-permute-start.1 = (bf16[1312,128]{1,0:T(8,128)(2,1)S(1)}, bf16[1312,128]{1,0:T(8,128)(2,1)S(1)}, u32[]{:S(2)}, u32[]{:S(2)}) collective-permute-start(bf16[1312,128]{1,0:T(8,128)(2,1)S(1)} %pad_maximum_fusion), channel_id=1, source_target_pairs={{0,16},{4,20},{8,24},{12,28},{16,0},{20,4},{24,8},{28,12},{1,17},{... | collective-permute-start | bytes 1007624 | tf_op jit(solution)/shard_map/ppermute | solution.py:692
  16.4 2.5 %collective-permute-start.2 = (bf16[1920,128]{1,0:T(8,128)(2,1)}, bf16[1920,128]{1,0:T(8,128)(2,1)S(1)}, u32[]{:S(2)}, u32[]{:S(2)}) collective-permute-start(bf16[1920,128]{1,0:T(8,128)(2,1)} %get-tuple-element.27), channel_id=1, source_target_pairs={{0,12},{4,8},{8,4},{12,0},{16,28},{20,24},{24,20},{28,16},{1,13},{... | collective-permute-start | bytes 1474568 | tf_op jit(solution)/shard_map/ppermute | solution.py:692
  18.9 2.1 %collective-permute-start.5 = (bf16[256,128]{1,0:T(8,128)(2,1)S(1)}, bf16[256,128]{1,0:T(8,128)(2,1)S(1)}, u32[]{:S(2)}, u32[]{:S(2)}) collective-permute-start(bf16[256,128]{1,0:T(8,128)(2,1)S(1)} %pad_maximum_fusion.1), channel_id=1, source_target_pairs={{0,24},{4,28},{8,16},{12,20},{1,25},{5,29},{9,17},{13,21},{2,26},{... | collective-permute-start | bytes 196616 | tf_op jit(solution)/shard_map/ppermute | solution.py:692
  21.1 0.1 maximum_convert_fusion.1.table_ref
  21.1 7.4 %collective-permute-done.4.refs_3_.refs_2_ = bf16[1920,128]{1,0:T(8,128)(2,1)S(1)} collective-permute-done((bf16[1920,128]{1,0:T(8,128)(2,1)}, bf16[1920,128]{1,0:T(8,128)(2,1)S(1)}, u32[]{:S(2)}, u32[]{:S(2)}) %collective-permute-start.4) | collective-permute-done | bytes 491552 | tf_op jit(solution)/shard_map/ppermute | solution.py:692
  28.6 0.0 copy-done.2
  28.6 0.0 copy-start
  28.6 0.9 %copy-done = bf16[656,128]{1,0:T(8,128)(2,1)S(1)} copy-done((bf16[656,128]{1,0:T(8,128)(2,1)S(1)}, bf16[656,128]{1,0:T(8,128)(2,1)}, u32[]{:S(2)}) %copy-start) | copy-done | bytes 167960
  29.5 1.8 %cross_state.3 = (f32[4,8,512]{2,1,0:T(8,128)S(1)}, f32[4,144,512]{2,1,0:T(8,128)S(1)}) custom-call(s32[16]{0:T(128)S(1)} %maximum_convert_fusion.1.table_ref, bf16[656,128]{1,0:T(8,128)(2,1)S(1)} %copy-done, bf16[656,128]{1,0:T(8,128)(2,1)S(1)} %collective-permute-done.refs_1_, bf16[1920,128]{1,0:T(8,128)(2,1)S(1)} %copy-done.2, ...), custom_call_target="tpu_custom_call" | custom-call | tf_op jit(solution)/shard_map/cross_state/pallas_call | solution.py:529
  31.3 0.0 collective-permute-done.1.refs_0_.refs_2_.refs_4_
  31.4 0.1 maximum_convert_fusion.table_ref
  31.4 0.0 copy-start.1
  31.4 4.1 %cross_state.4 = (f32[4,8,512]{2,1,0:T(8,128)S(1)}, f32[4,144,512]{2,1,0:T(8,128)S(1)}) custom-call(s32[32]{0:T(128)S(1)} %maximum_convert_fusion.table_ref, bf16[1312,128]{1,0:T(8,128)(2,1)S(1)} %collective-permute-done.1.refs_0_.refs_2_.refs_4_, bf16[1920,128]{1,0:T(8,128)(2,1)S(1)} %copy-done.2, ...), custom_call_target="tpu_custom_call" | custom-call | tf_op jit(solution)/shard_map/cross_state/pallas_call | solution.py:529
  35.6 0.0 collective-permute-done.3.refs_3_.beside_ref
  35.6 0.0 copy-done.1
  35.6 2.3 %cross_state.5 = (f32[4,8,512]{2,1,0:T(8,128)S(1)}, f32[4,144,512]{2,1,0:T(8,128)S(1)}) custom-call(s32[32]{0:T(128)S(1)} %maximum_convert_fusion.table_ref, bf16[656,128]{1,0:T(8,128)(2,1)S(1)} %copy-done.1, bf16[656,128]{1,0:T(8,128)(2,1)S(1)} %collective-permute-done.refs_1_, bf16[1312,128]{1,0:T(8,128)(2,1)S(1)} %collective-permute-done.1.refs_0_.refs_2_.refs_4_, ...), custom_call_target="tpu_custom_call" | custom-call | tf_op jit(solution)/shard_map/cross_state/pallas_call | solution.py:529
  37.9 0.0 copy-start.3
  37.9 0.4 collective-permute-done.5.refs_5_
  38.3 0.4 collective-permute-done.2.refs_1_.refs_3_.refs_2_
  38.7 2.3 %cross_packed.1 = bf16[1056,128]{1,0:T(8,128)(2,1)S(1)} custom-call(s32[32]{0:T(128)S(1)} %maximum_convert_fusion.table_ref, bf16[1312,128]{1,0:T(8,128)(2,1)S(1)} %collective-permute-done.1.refs_0_.refs_2_.refs_4_, bf16[1920,128]{1,0:T(8,128)(2,1)S(1)} %collective-permute-done.2.refs_1_.refs_3_.refs_2_, f32[4,8,512]{2,1,0:T(8,128)S(1)} %get-tuple-element.36.refs_2_.refs_3_, ...), custom_call_target="tpu_custom_call" | custom-call | tf_op jit(solution)/shard_map/cross_packed/pallas_call | solution.py:529
  41.0 1.1 %collective-permute-start.6 = (bf16[1056,128]{1,0:T(8,128)(2,1)S(1)}, bf16[1056,128]{1,0:T(8,128)(2,1)S(1)}, u32[]{:S(2)}, u32[]{:S(2)}) collective-permute-start(bf16[1056,128]{1,0:T(8,128)(2,1)S(1)} %cross_packed.1), channel_id=1, source_target_pairs={{0,16},{4,20},{8,24},{12,28},{16,0},{20,4},{24,8},{28,12},{1,17},{... | collective-permute-start | bytes 811016 | tf_op jit(solution)/shard_map/ppermute | solution.py:692
  42.2 0.0 copy-done.3
  42.2 2.0 %self_attention.1 = bf16[8,16,1024]{2,1,0:T(8,128)(2,1)} custom-call(bf16[512,128]{1,0:T(8,128)(2,1)S(1)} %copy-done.3, bf16[2304,128]{1,0:T(8,128)(2,1)S(1)} %collective-permute-done.3.refs_3_.beside_ref, bf16[656,128]{1,0:T(8,128)(2,1)S(1)} %copy-done.1, bf16[656,128]{1,0:T(8,128)(2,1)S(1)} %collective-permute-done.refs_1_, ...), custom_call_target="tpu_custom_call" | custom-call | tf_op jit(solution)/shard_map/self_attention/pallas_call | solution.py:590
  44.2 3.6 %all-to-all-start = ((bf16[8,16,1024]{2,1,0:T(8,128)(2,1)}), bf16[8,16,1024]{2,1,0:T(8,128)(2,1)S(1)}, u32[]{:S(2)}, u32[]{:S(2)}) async-start(bf16[8,16,1024]{2,1,0:T(8,128)(2,1)} %self_attention.1), calls=%async_computation | async-start | bytes 524288 | tf_op jit(solution)/shard_map/all_to_all | solution.py:752
  48.5 0.7 %cross_own.1 = (f32[1024,128]{1,0:T(8,128)S(1)}, f32[8,128]{1,0:T(8,128)S(1)}) custom-call(s32[32]{0:T(128)S(1)} %maximum_convert_fusion.table_ref, bf16[656,128]{1,0:T(8,128)(2,1)S(1)} %copy-done.1, bf16[656,128]{1,0:T(8,128)(2,1)S(1)} %collective-permute-done.refs_1_, bf16[1920,128]{1,0:T(8,128)(2,1)S(1)} %collective-permute-done.2.refs_1_.refs_3_.refs_2_, ...), custom_call_target="tpu_custom_call" | custom-call | tf_op jit(solution)/shard_map/cross_own/pallas_call | solution.py:529
  49.2 5.3 %collective-permute-done.6.returned_ref = bf16[1056,128]{1,0:T(8,128)(2,1)S(1)} collective-permute-done((bf16[1056,128]{1,0:T(8,128)(2,1)S(1)}, bf16[1056,128]{1,0:T(8,128)(2,1)S(1)}, u32[]{:S(2)}, u32[]{:S(2)}) %collective-permute-start.6) | collective-permute-done | bytes 270368 | tf_op jit(solution)/shard_map/ppermute | solution.py:692
  54.5 0.9 %combine_planes.1 = bf16[8,16,1024]{2,1,0:T(8,128)(2,1)} custom-call(f32[1]{0:T(128)S(6)} %copy.12.gate_ref, f32[1024,128]{1,0:T(8,128)S(1)} %get-tuple-element.42.mixed_ref, f32[8,128]{1,0:T(8,128)S(1)} %get-tuple-element.43.stat_ref, bf16[1056,128]{1,0:T(8,128)(2,1)S(1)} %collective-permute-done.6.returned_ref), custom_call_target="tpu_custom_call" | custom-call | tf_op jit(solution)/shard_map/combine_planes/pallas_call | solution.py:634
  55.4 0.0 all-to-all-done.in_ref
  55.4 3.4 %all-to-all-start.1 = ((bf16[8,16,1024]{2,1,0:T(8,128)(2,1)}), bf16[8,16,1024]{2,1,0:T(8,128)(2,1)S(1)}, u32[]{:S(2)}, u32[]{:S(2)}) async-start(bf16[8,16,1024]{2,1,0:T(8,128)(2,1)} %combine_planes.1), calls=%async_computation.1 | async-start | bytes 524288 | tf_op jit(solution)/shard_map/all_to_all | solution.py:752
  58.8 0.7 %spread_heads.2 = bf16[16,8192]{1,0:T(8,128)(2,1)} custom-call(bf16[8,16,1024]{2,1,0:T(8,128)(2,1)S(1)} %all-to-all-done.in_ref), custom_call_target="tpu_custom_call" | custom-call | tf_op jit(solution)/shard_map/spread_heads/pallas_call | solution.py:652
  59.6 5.2 %all-to-all-done.1.in_ref = bf16[8,16,1024]{2,1,0:T(8,128)(2,1)S(1)} async-done(((bf16[8,16,1024]{2,1,0:T(8,128)(2,1)}), bf16[8,16,1024]{2,1,0:T(8,128)(2,1)S(1)}, u32[]{:S(2)}, u32[]{:S(2)}) %all-to-all-start.1) | async-done | bytes 262176 | tf_op jit(solution)/shard_map/all_to_all | solution.py:752
  64.8 0.7 %spread_heads.3 = bf16[16,8192]{1,0:T(8,128)(2,1)} custom-call(bf16[8,16,1024]{2,1,0:T(8,128)(2,1)S(1)} %all-to-all-done.1.in_ref), custom_call_target="tpu_custom_call" | custom-call | tf_op jit(solution)/shard_map/spread_heads/pallas_call | solution.py:652
  (4 shorter events, 0.0 us)
Async XLA Ops:
  3.9 24.7 %copy-start.2 = (bf16[1920,128]{1,0:T(8,128)(2,1)S(1)}, bf16[1920,128]{1,0:T(8,128)(2,1)}, u32[]{:S(2)}) copy-start(bf16[1920,128]{1,0:T(8,128)(2,1)} %get-tuple-element.29.refs_2_.refs_1_) | copy-start | bytes 1474564
  3.9 8.4 %collective-permute-start = (bf16[656,128]{1,0:T(8,128)(2,1)}, bf16[656,128]{1,0:T(8,128)(2,1)S(1)}, u32[]{:S(2)}, u32[]{:S(2)}) collective-permute-start(bf16[656,128]{1,0:T(8,128)(2,1)} %get-tuple-element.25), channel_id=1, source_target_pairs={{0,4},{4,0},{8,12},{12,8},{16,20},{20,16},{24,28},{28,24},{1,5},{5... | collective-permute-start | bytes 503816 | tf_op jit(solution)/shard_map/ppermute | solution.py:692
  6.9 28.6 %collective-permute-start.3 = (bf16[2304,128]{1,0:T(8,128)(2,1)}, bf16[2304,128]{1,0:T(8,128)(2,1)S(1)}, u32[]{:S(2)}, u32[]{:S(2)}) collective-permute-start(bf16[2304,128]{1,0:T(8,128)(2,1)} %get-tuple-element.28), channel_id=1, source_target_pairs={{0,4},{4,0},{8,12},{12,8},{16,20},{20,16},{24,28},{28,24},{1,5},{5... | collective-permute-start | bytes 1769480 | tf_op jit(solution)/shard_map/ppermute | solution.py:692
  7.0 21.6 %collective-permute-start.4 = (bf16[1920,128]{1,0:T(8,128)(2,1)}, bf16[1920,128]{1,0:T(8,128)(2,1)S(1)}, u32[]{:S(2)}, u32[]{:S(2)}) collective-permute-start(bf16[1920,128]{1,0:T(8,128)(2,1)} %get-tuple-element.29.refs_2_.refs_1_), channel_id=1, source_target_pairs={{0,8},{4,12},{8,0},{12,4},{16,24},{20,28},{24,16},{28,20},{1,9},{5... | collective-permute-start | bytes 1474568 | tf_op jit(solution)/shard_map/ppermute | solution.py:692
  13.2 18.1 %collective-permute-start.1 = (bf16[1312,128]{1,0:T(8,128)(2,1)S(1)}, bf16[1312,128]{1,0:T(8,128)(2,1)S(1)}, u32[]{:S(2)}, u32[]{:S(2)}) collective-permute-start(bf16[1312,128]{1,0:T(8,128)(2,1)S(1)} %pad_maximum_fusion), channel_id=1, source_target_pairs={{0,16},{4,20},{8,24},{12,28},{16,0},{20,4},{24,8},{28,12},{1,17},{... | collective-permute-start | bytes 1007624 | tf_op jit(solution)/shard_map/ppermute | solution.py:692
  16.4 22.3 %collective-permute-start.2 = (bf16[1920,128]{1,0:T(8,128)(2,1)}, bf16[1920,128]{1,0:T(8,128)(2,1)S(1)}, u32[]{:S(2)}, u32[]{:S(2)}) collective-permute-start(bf16[1920,128]{1,0:T(8,128)(2,1)} %get-tuple-element.27), channel_id=1, source_target_pairs={{0,12},{4,8},{8,4},{12,0},{16,28},{20,24},{24,20},{28,16},{1,13},{... | collective-permute-start | bytes 1474568 | tf_op jit(solution)/shard_map/ppermute | solution.py:692
  18.9 19.4 %collective-permute-start.5 = (bf16[256,128]{1,0:T(8,128)(2,1)S(1)}, bf16[256,128]{1,0:T(8,128)(2,1)S(1)}, u32[]{:S(2)}, u32[]{:S(2)}) collective-permute-start(bf16[256,128]{1,0:T(8,128)(2,1)S(1)} %pad_maximum_fusion.1), channel_id=1, source_target_pairs={{0,24},{4,28},{8,16},{12,20},{1,25},{5,29},{9,17},{13,21},{2,26},{... | collective-permute-start | bytes 196616 | tf_op jit(solution)/shard_map/ppermute | solution.py:692
  28.6 0.9 %copy-start = (bf16[656,128]{1,0:T(8,128)(2,1)S(1)}, bf16[656,128]{1,0:T(8,128)(2,1)}, u32[]{:S(2)}) copy-start(bf16[656,128]{1,0:T(8,128)(2,1)} %get-tuple-element.23.refs_0_) | copy-start | bytes 503812
  31.4 4.2 %copy-start.1 = (bf16[656,128]{1,0:T(8,128)(2,1)S(1)}, bf16[656,128]{1,0:T(8,128)(2,1)}, u32[]{:S(2)}) copy-start(bf16[656,128]{1,0:T(8,128)(2,1)} %get-tuple-element.23.refs_0_) | copy-start | bytes 503812
  37.9 4.3 %copy-start.3 = (bf16[512,128]{1,0:T(8,128)(2,1)S(1)}, bf16[512,128]{1,0:T(8,128)(2,1)}, u32[]{:S(2)}) copy-start(bf16[512,128]{1,0:T(8,128)(2,1)} %get-tuple-element.39.own_ref) | copy-start | bytes 393220
  41.0 13.5 %collective-permute-start.6 = (bf16[1056,128]{1,0:T(8,128)(2,1)S(1)}, bf16[1056,128]{1,0:T(8,128)(2,1)S(1)}, u32[]{:S(2)}, u32[]{:S(2)}) collective-permute-start(bf16[1056,128]{1,0:T(8,128)(2,1)S(1)} %cross_packed.1), channel_id=1, source_target_pairs={{0,16},{4,20},{8,24},{12,28},{16,0},{20,4},{24,8},{28,12},{1,17},{... | collective-permute-start | bytes 811016 | tf_op jit(solution)/shard_map/ppermute | solution.py:692
  44.2 11.2 %all-to-all-start = ((bf16[8,16,1024]{2,1,0:T(8,128)(2,1)}), bf16[8,16,1024]{2,1,0:T(8,128)(2,1)S(1)}, u32[]{:S(2)}, u32[]{:S(2)}) async-start(bf16[8,16,1024]{2,1,0:T(8,128)(2,1)} %self_attention.1), calls=%async_computation | async-start | bytes 524288 | tf_op jit(solution)/shard_map/all_to_all | solution.py:752
  55.4 9.4 %all-to-all-start.1 = ((bf16[8,16,1024]{2,1,0:T(8,128)(2,1)}), bf16[8,16,1024]{2,1,0:T(8,128)(2,1)S(1)}, u32[]{:S(2)}, u32[]{:S(2)}) async-start(bf16[8,16,1024]{2,1,0:T(8,128)(2,1)} %combine_planes.1), calls=%async_computation.1 | async-start | bytes 524288 | tf_op jit(solution)/shard_map/all_to_all | solution.py:752
